TPU v7x, 32 devices: a whole 2x2x4 slice. The times are simulated.
32 devices in a mesh: ep: 8 (over z, x), blk: 4 (over y, core).
Axes of the slice: x: 2, y: 2, z: 4, core: 2. Of those that a mesh axis runs over, the one named last changes fastest.
Arguments:
- tokens: bfloat16 [4096, 1536], P(('ep', 'blk')), may hold values from -6 to 6
- norm_gain: bfloat16 [1536], replicated, may hold values from 0.099609375 to 1.8984375
- router_weight: bfloat16 [1536, 8], replicated, may hold values from -0.15625 to 0.15625
- routes: int32 [4096, 4], P(('ep', 'blk')), may hold values from 0 to 7, all different within a row; in each aligned block of 128 rows (0 to 127, 128 to 255, ...) at most 96 rows name the same one
- placement: int32 [8], replicated, may hold values from 0 to 7, each once
- gate_weight: bfloat16 [8, 1536, 768], P('ep', 'blk'), may hold values from -0.15625 to 0.15625
- up_weight: bfloat16 [8, 1536, 768], P('ep', 'blk'), may hold values from -0.15625 to 0.15625
- down_weight: bfloat16 [8, 768, 1536], P('ep', 'blk'), may hold values from -0.21875 to 0.21875
Outputs:
- mixed: bfloat16 [4096, 1536], P(('ep', 'blk'))
Inputs may be any that keep to these rules, and one draw needn't show every extreme that they name: `routes`: among the rows of one device, each expert is named by at most 96 rows, a bound that some block reaches; a row names 4 different experts. `placement`: each index of ep holds exactly one expert.
All inputs are finite; a program needn't handle non-finite values.
Results may differ from a plain program's by a relative error of at most 0.0071.
Values may be sent and summed in bfloat16 or wider, within the bound.
No kernel may reach another device: no remote copies, remote signals or barrier semaphores. Data moves between devices by JAX's collectives and lax.ppermute only.
A program may use at most 64 MiB of HBM per device.

v0:
```python
import jax
import jax.numpy as jnp
from jax import lax
from jax.sharding import PartitionSpec as P


def add_product(left, piece):
    return jnp.dot(left, piece, preferred_element_type=jnp.float32)


def on_device(
    tokens, norm_gain, router_weight, routes, placement, gate_weight, up_weight, down_weight
):
    tok_rows = tokens.shape[0]
    width = tokens.shape[1]
    top_count = routes.shape[1]
    experts = router_weight.shape[1]
    holders = lax.axis_size("ep")
    capacity = 3 * tok_rows * top_count // (2 * experts)
    values = tokens.astype(jnp.float32)
    square = jnp.mean(values * values, axis=-1, keepdims=True)
    normed = (values * lax.rsqrt(square + 1e-06) * norm_gain.astype(jnp.float32)).astype(
        jnp.bfloat16
    )
    logits = jnp.dot(normed, router_weight, preferred_element_type=jnp.float32)
    picked = jax.nn.sigmoid(jnp.take_along_axis(logits, routes, axis=1))
    gates = picked / jnp.sum(picked, axis=1, keepdims=True)
    flat_ids = routes.reshape(-1)
    onehot = flat_ids[:, None] == jnp.arange(experts, dtype=jnp.int32)[None, :]
    counts = jnp.cumsum(onehot.astype(jnp.int32), axis=0)
    slots = jnp.sum(jnp.where(onehot, counts - 1, 0), axis=1)
    target = jnp.sum(jnp.where(onehot, placement[None, :], 0), axis=1)
    repeated = jnp.repeat(normed, top_count, axis=0)
    outgoing = jnp.zeros((holders, capacity, width), jnp.bfloat16).at[target, slots].set(repeated)
    incoming = lax.all_to_all(outgoing, "ep", split_axis=0, concat_axis=0, tiled=True)
    expert_in = incoming.reshape(holders * capacity, width)

    def add_gate(piece):
        return add_product(expert_in, piece)

    gate = add_gate(lax.all_gather(gate_weight[0], "blk", axis=0, tiled=True))
    upper = add_gate(lax.all_gather(up_weight[0], "blk", axis=0, tiled=True))
    hidden = (jax.nn.relu(gate) * upper).astype(jnp.bfloat16)
    summed_out = add_product(hidden, lax.all_gather(down_weight[0], "blk", axis=0, tiled=True))
    expert_out = summed_out.astype(jnp.bfloat16)
    returned = lax.all_to_all(
        expert_out.reshape(holders, capacity, width), "ep", split_axis=0, concat_axis=0, tiled=True
    )
    collected = returned[target, slots].astype(jnp.float32)
    summed = jnp.sum(collected.reshape(tok_rows, top_count, width) * gates[:, :, None], axis=1)
    return summed.astype(jnp.bfloat16)


def solution(mesh):
    in_specs = (
        P(("ep", "blk"), None),
        P(),
        P(),
        P(("ep", "blk"), None),
        P(),
        P("ep", "blk", None),
        P("ep", "blk", None),
        P("ep", "blk", None),
    )
    out_specs = P(("ep", "blk"), None)
    return jax.shard_map(
        on_device, mesh=mesh, in_specs=in_specs, out_specs=out_specs, check_vma=False
    )
```

profile of v0, /device:TPU:0, one launch (start us, length us, event | category | flops | bytes accessed | tf_op | source)
XLA Modules:
  0.0 253.6 jit_solution(10710029093419195814)
XLA Ops:
  6.5 0.7 all-gather.9.cloned.1.call-update
  7.3 0.7 all-gather.11.cloned.1.call-update
  8.0 0.8 copy.17
  8.8 0.1 eq.29
  8.9 0.1 eq.25
  9.0 1.1 reduce-window.6
  10.2 0.2 slice_reduce_fusion
  10.4 0.7 convert_element_type.32
  11.1 1.2 fusion.7
  12.3 1.2 fusion.9
  13.5 0.7 copy-done.1
  14.2 0.4 broadcast_in_dim.37
  14.6 0.4 reshape.112
  15.0 0.1 fusion.12
  15.1 1.7 broadcast_in_dim.22
  16.8 82.3 %scatter_fusion = bf16[8,96,1536]{2,1,0:T(8,128)(2,1)} fusion(bf16[8,96,1536]{2,1,0:T(8,128)(2,1)} %broadcast_in_dim.22, s32[512]{0:T(512)S(1)} %bitcast.34, bf16[512,1536]{1,0:T(8,128)(2,1)S(1)} %reshape.112), kind=kCustom, calls=%fused_computation.2 | custom fusion | bytes 4722688 | tf_op jit(solution)/shard_map/scatter | solution.py:34
  99.1 6.5 %all-to-all-start = ((bf16[8,96,1536]{2,1,0:T(8,128)(2,1)}), bf16[8,96,1536]{2,1,0:T(8,128)(2,1)S(1)}, u32[]{:S(2)}, u32[]{:S(2)}) async-start(bf16[8,96,1536]{2,1,0:T(8,128)(2,1)} %scatter_fusion), calls=%async_computation | async-start | bytes 4718592 | tf_op jit(solution)/shard_map/all_to_all | solution.py:35
  105.7 0.7 all-gather.7.cloned.1.call-update
  106.4 53.0 %all-to-all-done = bf16[8,96,1536]{2,1,0:T(8,128)(2,1)S(1)} async-done(((bf16[8,96,1536]{2,1,0:T(8,128)(2,1)}), bf16[8,96,1536]{2,1,0:T(8,128)(2,1)S(1)}, u32[]{:S(2)}, u32[]{:S(2)}) %all-to-all-start) | async-done | bytes 2359328 | tf_op jit(solution)/shard_map/all_to_all | solution.py:35
  159.4 5.1 %fusion.1 = f32[768,768]{1,0:T(8,128)} fusion(bf16[768,1536]{1,0:T(8,128)(2,1)S(1)} %bitcast.35, bf16[1,1536,768]{2,1,0:T(8,128)(2,1)} %all-gather.9.cloned.1.call-done), kind=kOutput, calls=%fused_computation.6 | convolution fusion | flops 1811939328 | bytes 7077888 | tf_op jit(solution)/shard_map/dot_general | solution.py:8
  164.6 9.0 %convolution_convert_fusion = bf16[768,1536]{1,0:T(8,128)(2,1)} fusion(bf16[1,768,1536]{2,1,0:T(8,128)(2,1)} %all-gather.11.cloned.1.call-done, f32[768,768]{1,0:T(8,128)} %fusion.1, bf16[768,1536]{1,0:T(8,128)(2,1)S(1)} %bitcast.36, bf16[1,1536,768]{2,1,0:T(8,128)(2,1)} %all-gather.7.cloned.1.call-done), kind=kOutput, calls=%fused_computation.3 | convolution fusion | flops 3626827776 | bytes 11796480 | tf_op jit(solution)/shard_map/dot_general | solution.py:8
  173.6 3.9 %all-to-all-start.1 = ((bf16[8,96,1536]{2,1,0:T(8,128)(2,1)}), bf16[8,96,1536]{2,1,0:T(8,128)(2,1)S(1)}, u32[]{:S(2)}, u32[]{:S(2)}) async-start(bf16[8,96,1536]{2,1,0:T(8,128)(2,1)} %bitcast.37), calls=%async_computation.1 | async-start | bytes 4718592 | tf_op jit(solution)/shard_map/all_to_all | solution.py:46
  177.6 0.1 copy.19
  177.7 0.1 reshape.104
  177.8 0.2 fusion.17
  178.0 2.6 %gather_fusion.1 = f32[512]{0:T(512)S(1)} fusion(f32[128,8]{0,1:T(8,128)S(1)} %fusion.17, s32[512]{0:T(512)S(1)} %reshape.104), kind=kCustom, calls=%fused_computation.1 | custom fusion | bytes 8192 | tf_op jit(solution)/shard_map/jit(take_along_axis)/gather | solution.py:26
  180.6 0.1 reshape.107
  180.8 0.1 copy.21
  180.9 50.5 %all-to-all-done.1 = bf16[8,96,1536]{2,1,0:T(8,128)(2,1)S(1)} async-done(((bf16[8,96,1536]{2,1,0:T(8,128)(2,1)}), bf16[8,96,1536]{2,1,0:T(8,128)(2,1)S(1)}, u32[]{:S(2)}, u32[]{:S(2)}) %all-to-all-start.1) | async-done | bytes 2359328 | tf_op jit(solution)/shard_map/all_to_all | solution.py:46
  231.5 9.7 %gather_fusion = bf16[512,1536]{1,0:T(8,128)(2,1)} fusion(bf16[8,96,1536]{2,1,0:T(8,128)(2,1)S(1)} %all-to-all-done.1, s32[512]{0:T(512)S(1)} %bitcast.33), kind=kCustom, calls=%fused_computation | custom fusion | bytes 3149824 | tf_op jit(solution)/shard_map/gather | solution.py:49
  241.2 2.9 %reshape.97 = f32[128,4,1536]{2,1,0:T(4,128)S(1)} reshape(bf16[512,1536]{1,0:T(8,128)(2,1)} %gather_fusion) | data formatting | bytes 4718592 | tf_op jit(solution)/shard_map/convert_element_type | solution.py:49
  244.0 3.0 %multiply_reduce_fusion = bf16[128,1536]{1,0:T(8,128)(2,1)} fusion(f32[128,4,1536]{2,1,0:T(4,128)S(1)} %reshape.97, f32[128,4]{1,0:T(8,128)S(1)} %copy.21), kind=kLoop, calls=%fused_computation.4 | loop fusion | flops 1376256 | bytes 3540992 | tf_op jit(solution)/shard_map/reduce_sum | solution.py:50
  (24 shorter events, 0.3 us)
Async XLA Ops:
  6.5 171.3 %copy-start = (bf16[1536,8]{0,1:T(8,128)(2,1)S(1)}, bf16[1536,8]{0,1:T(8,128)(2,1)}, u32[]{:S(2)}) copy-start(bf16[1536,8]{0,1:T(8,128)(2,1)} %param.10) | copy-start | bytes 73732
  6.5 99.8 %all-gather.9.cloned.1.call-start = ((), (), s32[]{:S(2)}) async-start(), calls=%async_computation.3 | async-start | bytes 2949120 | tf_op jit(solution)/shard_map/all_gather | solution.py:42
  7.3 157.3 %all-gather.11.cloned.1.call-start = ((), (), s32[]{:S(2)}) async-start(), calls=%async_computation.4 | async-start | bytes 2949120 | tf_op jit(solution)/shard_map/all_gather | solution.py:44
  13.5 0.7 copy-start.1
  14.2 0.8 copy-start.4
  99.1 60.3 %all-to-all-start = ((bf16[8,96,1536]{2,1,0:T(8,128)(2,1)}), bf16[8,96,1536]{2,1,0:T(8,128)(2,1)S(1)}, u32[]{:S(2)}, u32[]{:S(2)}) async-start(bf16[8,96,1536]{2,1,0:T(8,128)(2,1)} %scatter_fusion), calls=%async_computation | async-start | bytes 4718592 | tf_op jit(solution)/shard_map/all_to_all | solution.py:35
  105.6 58.9 %all-gather.7.cloned.1.call-start = ((), (), s32[]{:S(2)}) async-start(), calls=%async_computation.2 | async-start | bytes 2949120 | tf_op jit(solution)/shard_map/all_gather | solution.py:41
  173.6 3.9 %copy-start.3 = (s32[128,4]{0,1:T(4,128)S(1)}, s32[128,4]{0,1:T(4,128)}, u32[]{:S(2)}) copy-start(s32[128,4]{0,1:T(4,128)} %param.11) | copy-start | bytes 6148
  173.6 4.2 %copy-start.2 = (bf16[128,1536]{1,0:T(8,128)(2,1)S(1)}, bf16[128,1536]{1,0:T(8,128)(2,1)}, u32[]{:S(2)}) copy-start(bf16[128,1536]{1,0:T(8,128)(2,1)} %copy-done.1) | copy-start | bytes 1179652
  173.6 57.8 %all-to-all-start.1 = ((bf16[8,96,1536]{2,1,0:T(8,128)(2,1)}), bf16[8,96,1536]{2,1,0:T(8,128)(2,1)S(1)}, u32[]{:S(2)}, u32[]{:S(2)}) async-start(bf16[8,96,1536]{2,1,0:T(8,128)(2,1)} %bitcast.37), calls=%async_computation.1 | async-start | bytes 4718592 | tf_op jit(solution)/shard_map/all_to_all | solution.py:46
Sparse Core Ops, SparseCore 0:
  8.9 26.8 all-gather.8
  37.3 24.0 all-gather.10
  108.0 25.7 all-gather.6
where the time goes:
time: 257 us; the launch traced here: 254 us
  waiting for transfers between devices  106 us (41%)
  local copies, waits for them, and re-layouts  102 us (40%)
  matrix products  14.4 us (6%)
  between operations  13.3 us (5%)
  starting transfers between devices  10.5 us (4%)
  other arithmetic  7.42 us (3%)
    scatter x1, local copies, waits for them, and re-layouts, on_device(): jnp.zeros((holders, capacity, width), jnp.bfloat16).at[target, slots]  82.3 us
    all_to_all x1, waiting for transfers between devices, on_device(): lax.all_to_all(outgoing, 'ep', split_axis=0, concat_axis=0, tiled=True)  53 us
    all_to_all x1, waiting for transfers between devices, on_device(): lax.all_to_all(expert_out.reshape(holders, capacity, width), 'ep', split_...  50.5 us
    dot_general x2, matrix products, add_product(): return jnp.dot(left, piece, preferred_element_type=jnp.float32)  14.2 us
    gather x1, local copies, waits for them, and re-layouts, on_device(): collected = returned[target, slots].astype(jnp.float32)  9.69 us
    all_to_all x1, starting transfers between devices, on_device(): lax.all_to_all(outgoing, 'ep', split_axis=0, concat_axis=0, tiled=True)  6.49 us
  transfers between devices with their start and end apart: 5, of which 2 were waited for; matrix products, arithmetic and copies ran while one was open for 39% of the time, Pallas kernels for 0%

commit v1 on v0

v1 whole, which is shorter than its diff:
```python
import functools

import jax
import jax.numpy as jnp
from jax import lax
from jax.experimental import pallas as pl
from jax.experimental.pallas import tpu as pltpu
from jax.sharding import PartitionSpec as P

VMEM_LIMIT = 28 * 1024 * 1024
WHOLE = pl.BlockSpec(memory_space=pltpu.VMEM)
SCALAR = pl.BlockSpec(memory_space=pltpu.SMEM)
ANYWHERE = pl.BlockSpec(memory_space=pl.ANY)


def params():
    return pltpu.CompilerParams(vmem_limit_bytes=VMEM_LIMIT)


def cost(flops, moved):
    return pl.CostEstimate(flops=int(flops), bytes_accessed=int(moved), transcendentals=0)


def ring_order(holders):
    columns = 1
    while 2 * (columns * 2) ** 2 <= holders:
        columns *= 2
    columns = max(columns, 2) if holders >= 4 else 1
    rows = holders // columns
    order = [row * columns for row in range(rows)]
    for back, row in enumerate(reversed(range(rows))):
        line = range(1, columns) if back % 2 == 0 else reversed(range(1, columns))
        order += [row * columns + column for column in line]
    return order


def norm_kernel(parts, experts, own_ref, gain_ref, router_ref, *refs):
    count = len(parts)
    token_refs, route_refs = refs[: len(sum(parts, []))], refs[len(sum(parts, [])) : -2]
    normed_ref, weight_ref = refs[-2:]
    gain = gain_ref[...].astype(jnp.float32)
    base = 0
    flat = 0
    for block in range(count):
        start = base
        for _ in parts[block]:
            rows = token_refs[flat].shape[0]
            for at in range(0, rows, 32):
                values = token_refs[flat][at : at + 32, :].astype(jnp.float32)
                square = jnp.mean(values * values, axis=-1, keepdims=True)
                normed = values * lax.rsqrt(square + 1e-06) * gain
                normed_ref[base + at : base + at + 32, :] = normed.astype(jnp.bfloat16)
            base += rows
            flat += 1
        rows = base - start
        logits = jnp.dot(
            normed_ref[start:base, :], router_ref[...], preferred_element_type=jnp.float32
        )
        routes = route_refs[block][...]
        lanes = lax.broadcasted_iota(jnp.int32, (rows, rows), 0)
        named = lanes == routes[0:1, :]
        for choice in range(1, routes.shape[0]):
            named = named | (lanes == routes[choice : choice + 1, :])
        named = jnp.where(named, 1.0, 0.0).T[:, :experts]
        picked = jax.nn.sigmoid(logits) * named
        total = jnp.sum(picked, axis=1, keepdims=True)
        mine = jnp.sum(picked * own_ref[...], axis=1, keepdims=True) / total
        chosen = jnp.sum(named * own_ref[...], axis=1, keepdims=True)
        weight = jnp.where(chosen > 0, mine, 0.0)
        weight_ref[start:base, :] = jnp.broadcast_to(weight, (rows, 128))


def norm_blocks(own, gain, router, tokens, routes):
    parts = [[0] * len(block) for block in tokens]
    rows = sum(part.shape[0] for block in tokens for part in block)
    width = gain.shape[1]
    flat = [part for block in tokens for part in block]
    return pl.pallas_call(
        functools.partial(norm_kernel, parts, router.shape[1]),
        out_shape=(
            jax.ShapeDtypeStruct((rows, width), jnp.bfloat16),
            jax.ShapeDtypeStruct((rows, 128), jnp.float32),
        ),
        in_specs=[WHOLE] * (3 + len(flat) + len(routes)),
        out_specs=(WHOLE, WHOLE),
        compiler_params=params(),
        cost_estimate=cost(rows * width * 16, rows * width * 4),
        name="norm_gate",
    )(own, gain, router, *flat, *routes)


def fetch(me, refs, target, sems, first):
    copies = []
    depth = refs[0].shape[0]
    for apart, ref in enumerate(refs):
        at = pl.multiple_of((me ^ apart) * depth, depth)
        copies.append(
            pltpu.make_async_copy(ref, target.at[pl.ds(at, depth), :], sems.at[first + apart])
        )
        copies[-1].start()
    return copies


def hidden_kernel(inputs, pieces, me_ref, *refs):
    normed, weight = refs[:inputs], refs[inputs : 2 * inputs]
    gates = refs[2 * inputs : 2 * inputs + pieces]
    uppers = refs[2 * inputs + pieces : 2 * inputs + 2 * pieces]
    outs = refs[2 * inputs + 2 * pieces : 3 * inputs + 2 * pieces]
    gate_mat, upper_mat, sems = refs[3 * inputs + 2 * pieces :]
    me = me_ref[0]
    gate_copies = fetch(me, gates, gate_mat, sems, 0)
    upper_copies = fetch(me, uppers, upper_mat, sems, pieces)
    for copy in gate_copies:
        copy.wait()
    for copy in upper_copies:
        copy.wait()
    for at in range(inputs):
        rows = normed[at][...]
        gate = jnp.dot(rows, gate_mat[...], preferred_element_type=jnp.float32)
        upper = jnp.dot(rows, upper_mat[...], preferred_element_type=jnp.float32)
        scale = weight[at][:, :1]
        outs[at][...] = jnp.where(
            scale > 0, jnp.maximum(gate, 0.0) * upper * scale, 0.0
        ).astype(jnp.bfloat16)


def hidden_blocks(me, normed, weight, gates, uppers):
    pieces = len(gates)
    width, units = gates[0].shape[0] * pieces, gates[0].shape[1]
    rows = sum(block.shape[0] for block in normed)
    return pl.pallas_call(
        functools.partial(hidden_kernel, len(normed), pieces),
        out_shape=tuple(
            jax.ShapeDtypeStruct((block.shape[0], units), jnp.bfloat16) for block in normed
        ),
        in_specs=[SCALAR] + [WHOLE] * (2 * len(normed)) + [ANYWHERE] * (2 * pieces),
        out_specs=tuple(WHOLE for _ in normed),
        scratch_shapes=[
            pltpu.VMEM((width, units), jnp.bfloat16),
            pltpu.VMEM((width, units), jnp.bfloat16),
            pltpu.SemaphoreType.DMA((2 * pieces,)),
        ],
        compiler_params=params(),
        cost_estimate=cost(4 * rows * width * units, 4 * width * units),
        name="hidden",
    )(me, *normed, *weight, *gates, *uppers)


def down_kernel(counts, pieces, me_ref, *refs):
    inputs = len(counts)
    hidden = refs[:inputs]
    downs = refs[inputs : inputs + pieces]
    outs = refs[inputs + pieces : inputs + pieces + sum(counts)]
    down_mat, sems = refs[inputs + pieces + sum(counts) :]
    for copy in fetch(me_ref[0], downs, down_mat, sems, 0):
        copy.wait()
    at = 0
    for block, count in enumerate(counts):
        out = jnp.dot(hidden[block][...], down_mat[...], preferred_element_type=jnp.float32)
        rows = out.shape[0] // count
        for part in range(count):
            outs[at][...] = out[part * rows : (part + 1) * rows, :].astype(outs[at].dtype)
            at += 1


def down_blocks(me, hidden, counts, kinds, downs):
    pieces = len(downs)
    units, width = downs[0].shape[0] * pieces, downs[0].shape[1]
    shapes = []
    for block, count in zip(hidden, counts):
        shapes += [(block.shape[0] // count, width)] * count
    rows = sum(shape[0] for shape in shapes)
    return pl.pallas_call(
        functools.partial(down_kernel, counts, pieces),
        out_shape=tuple(jax.ShapeDtypeStruct(s, kind) for s, kind in zip(shapes, kinds)),
        in_specs=[SCALAR] + [WHOLE] * len(hidden) + [ANYWHERE] * pieces,
        out_specs=tuple(WHOLE for _ in shapes),
        scratch_shapes=[
            pltpu.VMEM((units, width), jnp.bfloat16),
            pltpu.SemaphoreType.DMA((pieces,)),
        ],
        compiler_params=params(),
        cost_estimate=cost(2 * rows * width * units, 2 * width * units + 4 * rows * width),
        name="down",
    )(me, *hidden, *downs)


def gather_blk(piece):
    size = lax.axis_size("blk")
    have = {0: piece}
    bit = size // 2
    while bit:
        pairs = [(i, i ^ bit) for i in range(size)]
        have.update({k ^ bit: lax.ppermute(v, "blk", pairs) for k, v in list(have.items())})
        bit //= 2
    return [have[k] for k in range(size)]


def add_round(*terms):
    total = terms[0].astype(jnp.float32)
    for term in terms[1:]:
        total = total + term.astype(jnp.float32)
    return total.astype(jnp.bfloat16)


def on_device(
    tokens, norm_gain, router_weight, routes, placement, gate_weight, up_weight, down_weight
):
    holders = lax.axis_size("ep")
    tok_rows, width = tokens.shape
    far = holders // 2
    order = ring_order(holders)
    ahead = [(order[i], order[(i + 1) % holders]) for i in range(holders)]
    behind = [(target, source) for source, target in ahead]

    def clock(x):
        return lax.ppermute(x, "ep", ahead)

    def counter(x):
        return lax.ppermute(x, "ep", behind)

    me = lax.axis_index("blk").astype(jnp.int32).reshape(1)
    own = (placement == lax.axis_index("ep")).astype(jnp.float32)[None, :]
    gain = norm_gain[None, :]
    gates = gather_blk(gate_weight[0])
    uppers = gather_blk(up_weight[0])
    half = width // 2
    downs = [gather_blk(down_weight[0][:, :half]), gather_blk(down_weight[0][:, half:])]

    names = routes.T
    cut = tok_rows // 2
    from_behind, from_ahead = [tokens], [tokens]
    names_behind, names_ahead = [names], [names]
    for step in range(1, far):
        from_behind.append(clock(from_behind[-1]))
        names_behind.append(clock(names_behind[-1]))
        from_ahead.append(counter(from_ahead[-1]))
        names_ahead.append(counter(names_ahead[-1]))
    far_parts = [clock(from_behind[-1][:cut]), counter(from_ahead[-1][cut:])]
    far_names = clock(names_behind[-1])

    def norm(blocks, block_names):
        return norm_blocks(own, gain, router_weight, blocks, block_names)

    stages = [norm([[tokens]], [names])]
    for step in range(1, far):
        stages.append(
            norm(
                [[from_behind[step]], [from_ahead[step]]],
                [names_behind[step], names_ahead[step]],
            )
        )
    stages.append(norm([far_parts], [far_names]))

    hidden = []
    groups = [stages[:3]] + [stages[at : at + 2] for at in range(3, len(stages), 2)]
    for group in groups:
        hidden += hidden_blocks(
            me, [normed for normed, _ in group], [w for _, w in group], gates, uppers
        )

    results = []
    for side, down in enumerate(downs):
        long_way, short_way = (clock, counter) if side == 0 else (counter, clock)
        to_behind, to_ahead = {}, {}
        for at in range(0, len(hidden), 5):
            chosen = list(range(at, min(at + 5, len(hidden))))
            counts = [1 if step in (0, far) else 2 for step in chosen]
            kinds, slots = [], []
            for step in chosen:
                if step in (0, far):
                    kinds.append(jnp.bfloat16 if step == far else jnp.float32)
                    slots.append((to_behind, step))
                else:
                    first_behind = side == 0 and step == far - 1
                    first_ahead = side == 1 and step == far - 1
                    kinds += [
                        jnp.bfloat16 if first_behind else jnp.float32,
                        jnp.bfloat16 if first_ahead else jnp.float32,
                    ]
                    slots += [(to_behind, step), (to_ahead, step)]
            outs = down_blocks(me, [hidden[step] for step in chosen], counts, kinds, down)
            for (table, step), out in zip(slots, outs):
                table[step] = out
        long_sums, short_sums = (to_ahead, to_behind) if side == 0 else (to_behind, to_ahead)
        long_run = long_way(to_behind[far])
        short_run = short_way(short_sums[far - 1])
        for step in range(far - 1, 0, -1):
            long_run = long_way(add_round(long_run, long_sums[step]))
            if step > 1:
                short_run = short_way(add_round(short_run, short_sums[step - 1]))
        results.append(add_round(to_behind[0], long_run, short_run))
    return jnp.concatenate(results, axis=1)


def solution(mesh):
    in_specs = (
        P(("ep", "blk"), None),
        P(),
        P(),
        P(("ep", "blk"), None),
        P(),
        P("ep", "blk", None),
        P("ep", "blk", None),
        P("ep", "blk", None),
    )
    out_specs = P(("ep", "blk"), None)
    return jax.shard_map(
        on_device, mesh=mesh, in_specs=in_specs, out_specs=out_specs, check_vma=False
    )
```

time: 257 us -> 119 us (0.46); the launches traced: 254 us -> 119 us
  local copies, waits for them, and re-layouts: 102 us -> 2.82 us
  waiting for transfers between devices: 106 us -> 54.8 us
  starting transfers between devices: 10.5 us -> 42.4 us
  Pallas kernels: 0 us -> 17.2 us
  matrix products: 14.4 us -> 0 us
  between operations: 13.3 us -> 0.31 us
  other arithmetic: 7.42 us -> 1.26 us
    all_to_all x2 -> x0, waiting for transfers between devices: 104 us -> none  [the longest x1 53 us: on_device(): lax.all_to_all(outgoing, 'ep', split_axis=0, concat_axis=0, tiled=True)]
    scatter x1 -> x0, local copies, waits for them, and re-layouts: 82.3 us -> none  [on_device(): jnp.zeros((holders, capacity, width), jnp.bfloat16).at[target, slots]]
    ppermute x0 -> x41, waiting for transfers between devices: none -> 54.8 us  [the longest x14 32.7 us: counter(): return lax.ppermute(x, 'ep', behind)]
    ppermute x0 -> x41, starting transfers between devices: none -> 42.4 us  [the longest x15 25.4 us: clock(): return lax.ppermute(x, 'ep', ahead)]
    pallas_call x0 -> x9, Pallas kernels: none -> 17.2 us  [the longest x2 10 us: hidden_blocks(): pl.pallas_call(functools.partial(hidden_kernel, len(normed), pieces), out...]
    dot_general x3 -> x0, matrix products: 14.4 us -> none  [the longest x2 14.2 us: add_product(): return jnp.dot(left, piece, preferred_element_type=jnp.float32)]
    gather x6 -> x0, local copies, waits for them, and re-layouts: 12.6 us -> none  [the longest x1 9.69 us: on_device(): collected = returned[target, slots].astype(jnp.float32)]
    all_to_all x2 -> x0, starting transfers between devices: 10.4 us -> none  [the longest x1 6.49 us: on_device(): lax.all_to_all(outgoing, 'ep', split_axis=0, concat_axis=0, tiled=True)]
  transfers between devices with their start and end apart: 5 -> 41, of which waited for: 2 -> 18; matrix products, arithmetic and copies ran while one was open for 39% -> 2% of each run, Pallas kernels for 0% -> 14%
where the time goes in v1:
time: 119 us
  waiting for transfers between devices  54.8 us (46%)
  starting transfers between devices  42.4 us (36%)
  Pallas kernels  17.2 us (14%)
  local copies, waits for them, and re-layouts  2.82 us (2%)
  other arithmetic  1.26 us (1%)
    ppermute x14, waiting for transfers between devices, counter(): return lax.ppermute(x, 'ep', behind)  32.7 us
    ppermute x15, starting transfers between devices, clock(): return lax.ppermute(x, 'ep', ahead)  25.4 us
    ppermute x15, waiting for transfers between devices, clock(): return lax.ppermute(x, 'ep', ahead)  22.1 us
    pallas_call x2, Pallas kernels, hidden_blocks(): pl.pallas_call(functools.partial(hidden_kernel, len(normed), pieces), out...  10 us
    ppermute x14, starting transfers between devices, counter(): return lax.ppermute(x, 'ep', behind)  9.74 us
    ppermute x12, starting transfers between devices, gather_blk(): lax.ppermute(v, 'blk', pairs)  7.21 us
    pallas_call x2, Pallas kernels, down_blocks(): pl.pallas_call(functools.partial(down_kernel, counts, pieces), out_shape=...  4.28 us
    pallas_call x5, Pallas kernels, norm_blocks(): pl.pallas_call(functools.partial(norm_kernel, parts, router.shape[1]), ou...  2.86 us
  transfers between devices with their start and end apart: 41, of which 18 were waited for; matrix products, arithmetic and copies ran while one was open for 2% of the time, Pallas kernels for 14%

profile of v1, /device:TPU:0, one launch (start us, length us, event | category | flops | bytes accessed | tf_op | source)
XLA Modules:
  0.0 118.7 jit_solution(6987816493416233200)
XLA Ops:
  0.0 3.0 %collective-permute-start = (bf16[128,1536]{1,0:T(8,128)(2,1)}, bf16[128,1536]{1,0:T(8,128)(2,1)S(1)}, u32[]{:S(2)}, u32[]{:S(2)}) collective-permute-start(bf16[128,1536]{1,0:T(8,128)(2,1)} %refs_0_.1), channel_id=1, source_target_pairs={{0,8},{8,16},{16,24},{24,28},{28,20},{20,12},{12,4},{4,0},{1,9},{9... | collective-permute-start | bytes 1179656 | tf_op jit(solution)/shard_map/ppermute | solution.py:217
  3.0 9.2 %collective-permute-done.refs_0_ = bf16[128,1536]{1,0:T(8,128)(2,1)S(1)} collective-permute-done((bf16[128,1536]{1,0:T(8,128)(2,1)}, bf16[128,1536]{1,0:T(8,128)(2,1)S(1)}, u32[]{:S(2)}, u32[]{:S(2)}) %collective-permute-start) | collective-permute-done | bytes 393248 | tf_op jit(solution)/shard_map/ppermute | solution.py:217
  12.3 1.8 %collective-permute-start.4 = (bf16[128,1536]{1,0:T(8,128)(2,1)S(1)}, bf16[128,1536]{1,0:T(8,128)(2,1)S(1)}, u32[]{:S(2)}, u32[]{:S(2)}) collective-permute-start(bf16[128,1536]{1,0:T(8,128)(2,1)S(1)} %collective-permute-done.refs_0_), channel_id=1, source_target_pairs={{0,8},{8,16},{16,24},{24,28},{28,20},{20,12},{12,4},{4,0},{1,9},{9... | collective-permute-start | bytes 1179656 | tf_op jit(solution)/shard_map/ppermute | solution.py:217
  14.1 1.5 %collective-permute-start.9 = (bf16[384,768]{1,0:T(8,128)(2,1)}, bf16[384,768]{1,0:T(8,128)(2,1)}, u32[]{:S(2)}, u32[]{:S(2)}) collective-permute-start(bf16[384,768]{1,0:T(8,128)(2,1)} %bitcast.3.refs_6_.refs_4_), channel_id=1, source_target_pairs={{0,2},{1,3},{2,0},{3,1},{4,6},{5,7},{6,4},{7,5},{8,10},{9,11},{10,... | collective-permute-start | bytes 1769480 | tf_op jit(solution)/shard_map/ppermute | solution.py:194
  16.1 1.6 %collective-permute-start.2 = (s32[4,128]{1,0:T(4,128)S(1)}, s32[4,128]{1,0:T(4,128)S(1)}, u32[]{:S(2)}, u32[]{:S(2)}) collective-permute-start(s32[4,128]{1,0:T(4,128)S(1)} %bitcast.7), channel_id=1, source_target_pairs={{0,8},{8,16},{16,24},{24,28},{28,20},{20,12},{12,4},{4,0},{1,9},{9... | collective-permute-start | bytes 6152 | tf_op jit(solution)/shard_map/ppermute | solution.py:217
  17.7 4.9 %collective-permute-done.2.refs_2_ = s32[4,128]{1,0:T(4,128)S(1)} collective-permute-done((s32[4,128]{1,0:T(4,128)S(1)}, s32[4,128]{1,0:T(4,128)S(1)}, u32[]{:S(2)}, u32[]{:S(2)}) %collective-permute-start.2) | collective-permute-done | bytes 2080 | tf_op jit(solution)/shard_map/ppermute | solution.py:217
  24.0 2.2 %collective-permute-done.3.refs_3_ = s32[4,128]{1,0:T(4,128)S(1)} collective-permute-done((s32[4,128]{1,0:T(4,128)S(1)}, s32[4,128]{1,0:T(4,128)S(1)}, u32[]{:S(2)}, u32[]{:S(2)}) %collective-permute-start.3) | collective-permute-done | bytes 2080 | tf_op jit(solution)/shard_map/ppermute | solution.py:220
  27.7 2.1 %collective-permute-done.6.refs_2_ = s32[4,128]{1,0:T(4,128)S(1)} collective-permute-done((s32[4,128]{1,0:T(4,128)S(1)}, s32[4,128]{1,0:T(4,128)S(1)}, u32[]{:S(2)}, u32[]{:S(2)}) %collective-permute-start.6) | collective-permute-done | bytes 2080 | tf_op jit(solution)/shard_map/ppermute | solution.py:217
  31.2 2.2 %collective-permute-done.7.refs_3_ = s32[4,128]{1,0:T(4,128)S(1)} collective-permute-done((s32[4,128]{1,0:T(4,128)S(1)}, s32[4,128]{1,0:T(4,128)S(1)}, u32[]{:S(2)}, u32[]{:S(2)}) %collective-permute-start.7) | collective-permute-done | bytes 2080 | tf_op jit(solution)/shard_map/ppermute | solution.py:220
  34.9 2.1 %collective-permute-done.16.refs_2_ = s32[4,128]{1,0:T(4,128)S(1)} collective-permute-done((s32[4,128]{1,0:T(4,128)S(1)}, s32[4,128]{1,0:T(4,128)S(1)}, u32[]{:S(2)}, u32[]{:S(2)}) %collective-permute-start.16) | collective-permute-done | bytes 2080 | tf_op jit(solution)/shard_map/ppermute | solution.py:217
  38.4 2.2 %collective-permute-done.17.refs_3_ = s32[4,128]{1,0:T(4,128)S(1)} collective-permute-done((s32[4,128]{1,0:T(4,128)S(1)}, s32[4,128]{1,0:T(4,128)S(1)}, u32[]{:S(2)}, u32[]{:S(2)}) %collective-permute-start.17) | collective-permute-done | bytes 2080 | tf_op jit(solution)/shard_map/ppermute | solution.py:220
  45.3 1.6 %collective-permute-start.22 = (bf16[192,768]{1,0:T(8,128)(2,1)S(1)}, bf16[192,768]{1,0:T(8,128)(2,1)S(1)}, u32[]{:S(2)}, u32[]{:S(2)}) collective-permute-start(bf16[192,768]{1,0:T(8,128)(2,1)S(1)} %get-tuple-element.67.refs_5_), channel_id=1, source_target_pairs={{0,2},{1,3},{2,0},{3,1},{4,6},{5,7},{6,4},{7,5},{8,10},{9,11},{10,... | collective-permute-start | bytes 884744 | tf_op jit(solution)/shard_map/ppermute | solution.py:194
  46.9 6.9 %collective-permute-done.5.refs_1_ = bf16[128,1536]{1,0:T(8,128)(2,1)S(1)} collective-permute-done((bf16[128,1536]{1,0:T(8,128)(2,1)S(1)}, bf16[128,1536]{1,0:T(8,128)(2,1)S(1)}, u32[]{:S(2)}, u32[]{:S(2)}) %collective-permute-start.5) | collective-permute-done | bytes 393248 | tf_op jit(solution)/shard_map/ppermute | solution.py:220
  55.7 6.0 %collective-permute-done.15.refs_1_ = bf16[128,1536]{1,0:T(8,128)(2,1)S(1)} collective-permute-done((bf16[128,1536]{1,0:T(8,128)(2,1)S(1)}, bf16[128,1536]{1,0:T(8,128)(2,1)S(1)}, u32[]{:S(2)}, u32[]{:S(2)}) %collective-permute-start.15) | collective-permute-done | bytes 393248 | tf_op jit(solution)/shard_map/ppermute | solution.py:220
  61.6 1.5 %collective-permute-start.32 = (bf16[192,768]{1,0:T(8,128)(2,1)S(1)}, bf16[192,768]{1,0:T(8,128)(2,1)}, u32[]{:S(2)}, u32[]{:S(2)}) collective-permute-start(bf16[192,768]{1,0:T(8,128)(2,1)S(1)} %get-tuple-element.68.refs_5_), channel_id=1, source_target_pairs={{0,2},{1,3},{2,0},{3,1},{4,6},{5,7},{6,4},{7,5},{8,10},{9,11},{10,... | collective-permute-start | bytes 884744 | tf_op jit(solution)/shard_map/ppermute | solution.py:194
  67.2 1.6 %collective-permute-start.18 = (bf16[64,1536]{1,0:T(8,128)(2,1)S(1)}, bf16[64,1536]{1,0:T(8,128)(2,1)S(1)}, u32[]{:S(2)}, u32[]{:S(2)}) collective-permute-start(bf16[64,1536]{1,0:T(8,128)(2,1)S(1)} %slice.16), channel_id=1, source_target_pairs={{0,8},{8,16},{16,24},{24,28},{28,20},{20,12},{12,4},{4,0},{1,9},{9... | collective-permute-start | bytes 589832 | tf_op jit(solution)/shard_map/ppermute | solution.py:217
  69.2 5.6 %hidden.2 = (bf16[128,768]{1,0:T(8,128)(2,1)S(1)}, bf16[256,768]{1,0:T(8,128)(2,1)S(1)}, bf16[256,768]{1,0:T(8,128)(2,1)S(1)}) custom-call(s32[1]{0:T(128)} %bitcast.me_ref, bf16[128,1536]{1,0:T(8,128)(2,1)S(1)} %get-tuple-element.36.refs_0_, bf16[256,1536]{1,0:T(8,128)(2,1)S(1)} %get-tuple-element.37.refs_1_, ...), custom_call_target="tpu_custom_call" | custom-call | flops 3019898880 | bytes 4718592 | tf_op jit(solution)/shard_map/hidden/pallas_call | solution.py:131
  76.6 4.4 %hidden.3 = (bf16[256,768]{1,0:T(8,128)(2,1)S(1)}, bf16[128,768]{1,0:T(8,128)(2,1)S(1)}) custom-call(s32[1]{0:T(128)} %bitcast.me_ref, bf16[256,1536]{1,0:T(8,128)(2,1)S(1)} %get-tuple-element.45.refs_0_, bf16[128,1536]{1,0:T(8,128)(2,1)S(1)} %get-tuple-element.46.refs_1_, f32[256,128]{1,0:T(8,128)S(1)} %get-tuple-element.47.refs_2_, ...), custom_call_target="tpu_custom_call" | custom-call | flops 1811939328 | bytes 4718592 | tf_op jit(solution)/shard_map/hidden/pallas_call | solution.py:131
  81.0 1.7 %down.2 = (f32[128,768]{1,0:T(8,128)S(1)}, f32[128,768]{1,0:T(8,128)S(1)}, f32[128,768]{1,0:T(8,128)S(1)}, f32[128,768]{1,0:T(8,128)S(1)}, f32[128,768]{1,0:T(8,...) custom-call(s32[1]{0:T(128)} %bitcast.me_ref, ...), custom_call_target="tpu_custom_call" | custom-call | flops 1207959552 | bytes 4325376 | tf_op jit(solution)/shard_map/down/pallas_call | solution.py:173
  82.8 1.6 %collective-permute-start.24 = (bf16[128,768]{1,0:T(8,128)(2,1)S(1)}, bf16[128,768]{1,0:T(8,128)(2,1)S(1)}, u32[]{:S(2)}, u32[]{:S(2)}) collective-permute-start(bf16[128,768]{1,0:T(8,128)(2,1)S(1)} %get-tuple-element.52), channel_id=1, source_target_pairs={{0,8},{8,16},{16,24},{24,28},{28,20},{20,12},{12,4},{4,0},{1,9},{9... | collective-permute-start | bytes 589832 | tf_op jit(solution)/shard_map/ppermute | solution.py:217
  84.8 2.5 %down.3 = (f32[128,768]{1,0:T(8,128)S(1)}, f32[128,768]{1,0:T(8,128)S(1)}, f32[128,768]{1,0:T(8,128)S(1)}, f32[128,768]{1,0:T(8,128)S(1)}, f32[128,768]{1,0:T(8,...) custom-call(s32[1]{0:T(128)} %bitcast.me_ref, ...), custom_call_target="tpu_custom_call" | custom-call | flops 1207959552 | bytes 4325376 | tf_op jit(solution)/shard_map/down/pallas_call | solution.py:173
  87.9 1.6 %collective-permute-start.38 = (bf16[128,768]{1,0:T(8,128)(2,1)S(1)}, bf16[128,768]{1,0:T(8,128)(2,1)S(1)}, u32[]{:S(2)}, u32[]{:S(2)}) collective-permute-start(bf16[128,768]{1,0:T(8,128)(2,1)S(1)} %get-tuple-element.64), channel_id=1, source_target_pairs={{0,8},{8,16},{16,24},{24,28},{28,20},{20,12},{12,4},{4,0},{1,9},{9... | collective-permute-start | bytes 589832 | tf_op jit(solution)/shard_map/ppermute | solution.py:217
  89.8 1.6 %collective-permute-start.25 = (bf16[128,768]{1,0:T(8,128)(2,1)S(1)}, bf16[128,768]{1,0:T(8,128)(2,1)S(1)}, u32[]{:S(2)}, u32[]{:S(2)}) collective-permute-start(bf16[128,768]{1,0:T(8,128)(2,1)S(1)} %add_convert_fusion.11), channel_id=1, source_target_pairs={{0,8},{8,16},{16,24},{24,28},{28,20},{20,12},{12,4},{4,0},{1,9},{9... | collective-permute-start | bytes 589832 | tf_op jit(solution)/shard_map/ppermute | solution.py:217
  92.7 3.7 %collective-permute-done.34 = bf16[128,768]{1,0:T(8,128)(2,1)S(1)} collective-permute-done((bf16[128,768]{1,0:T(8,128)(2,1)S(1)}, bf16[128,768]{1,0:T(8,128)(2,1)S(1)}, u32[]{:S(2)}, u32[]{:S(2)}) %collective-permute-start.34) | collective-permute-done | bytes 196640 | tf_op jit(solution)/shard_map/ppermute | solution.py:220
  97.0 1.6 %collective-permute-start.39 = (bf16[128,768]{1,0:T(8,128)(2,1)S(1)}, bf16[128,768]{1,0:T(8,128)(2,1)S(1)}, u32[]{:S(2)}, u32[]{:S(2)}) collective-permute-start(bf16[128,768]{1,0:T(8,128)(2,1)S(1)} %add_convert_fusion.2), channel_id=1, source_target_pairs={{0,8},{8,16},{16,24},{24,28},{28,20},{20,12},{12,4},{4,0},{1,9},{9... | collective-permute-start | bytes 589832 | tf_op jit(solution)/shard_map/ppermute | solution.py:217
  99.2 1.6 %collective-permute-start.26 = (bf16[128,768]{1,0:T(8,128)(2,1)S(1)}, bf16[128,768]{1,0:T(8,128)(2,1)S(1)}, u32[]{:S(2)}, u32[]{:S(2)}) collective-permute-start(bf16[128,768]{1,0:T(8,128)(2,1)S(1)} %add_convert_fusion.10), channel_id=1, source_target_pairs={{0,8},{8,16},{16,24},{24,28},{28,20},{20,12},{12,4},{4,0},{1,9},{9... | collective-permute-start | bytes 589832 | tf_op jit(solution)/shard_map/ppermute | solution.py:217
  101.7 3.2 %collective-permute-done.35 = bf16[128,768]{1,0:T(8,128)(2,1)S(1)} collective-permute-done((bf16[128,768]{1,0:T(8,128)(2,1)S(1)}, bf16[128,768]{1,0:T(8,128)(2,1)S(1)}, u32[]{:S(2)}, u32[]{:S(2)}) %collective-permute-start.35) | collective-permute-done | bytes 196640 | tf_op jit(solution)/shard_map/ppermute | solution.py:220
  105.4 1.6 %collective-permute-start.40 = (bf16[128,768]{1,0:T(8,128)(2,1)S(1)}, bf16[128,768]{1,0:T(8,128)(2,1)S(1)}, u32[]{:S(2)}, u32[]{:S(2)}) collective-permute-start(bf16[128,768]{1,0:T(8,128)(2,1)S(1)} %add_convert_fusion.1), channel_id=1, source_target_pairs={{0,8},{8,16},{16,24},{24,28},{28,20},{20,12},{12,4},{4,0},{1,9},{9... | collective-permute-start | bytes 589832 | tf_op jit(solution)/shard_map/ppermute | solution.py:217
  107.6 1.6 %collective-permute-start.27 = (bf16[128,768]{1,0:T(8,128)(2,1)S(1)}, bf16[128,768]{1,0:T(8,128)(2,1)S(1)}, u32[]{:S(2)}, u32[]{:S(2)}) collective-permute-start(bf16[128,768]{1,0:T(8,128)(2,1)S(1)} %add_convert_fusion.9), channel_id=1, source_target_pairs={{0,8},{8,16},{16,24},{24,28},{28,20},{20,12},{12,4},{4,0},{1,9},{9... | collective-permute-start | bytes 589832 | tf_op jit(solution)/shard_map/ppermute | solution.py:217
  109.3 2.8 %collective-permute-done.36 = bf16[128,768]{1,0:T(8,128)(2,1)S(1)} collective-permute-done((bf16[128,768]{1,0:T(8,128)(2,1)S(1)}, bf16[128,768]{1,0:T(8,128)(2,1)S(1)}, u32[]{:S(2)}, u32[]{:S(2)}) %collective-permute-start.36) | collective-permute-done | bytes 196640 | tf_op jit(solution)/shard_map/ppermute | solution.py:220
  112.6 2.4 %collective-permute-done.27 = bf16[128,768]{1,0:T(8,128)(2,1)S(1)} collective-permute-done((bf16[128,768]{1,0:T(8,128)(2,1)S(1)}, bf16[128,768]{1,0:T(8,128)(2,1)S(1)}, u32[]{:S(2)}, u32[]{:S(2)}) %collective-permute-start.27) | collective-permute-done | bytes 196640 | tf_op jit(solution)/shard_map/ppermute | solution.py:217
  115.1 2.8 %collective-permute-done.37 = bf16[128,768]{1,0:T(8,128)(2,1)S(1)} collective-permute-done((bf16[128,768]{1,0:T(8,128)(2,1)S(1)}, bf16[128,768]{1,0:T(8,128)(2,1)S(1)}, u32[]{:S(2)}, u32[]{:S(2)}) %collective-permute-start.37) | collective-permute-done | bytes 196640 | tf_op jit(solution)/shard_map/ppermute | solution.py:220
  (96 shorter events, 27.5 us)
Async XLA Ops:
  0.0 12.3 %collective-permute-start = (bf16[128,1536]{1,0:T(8,128)(2,1)}, bf16[128,1536]{1,0:T(8,128)(2,1)S(1)}, u32[]{:S(2)}, u32[]{:S(2)}) collective-permute-start(bf16[128,1536]{1,0:T(8,128)(2,1)} %refs_0_.1), channel_id=1, source_target_pairs={{0,8},{8,16},{16,24},{24,28},{28,20},{20,12},{12,4},{4,0},{1,9},{9... | collective-permute-start | bytes 1179656 | tf_op jit(solution)/shard_map/ppermute | solution.py:217
  3.0 39.1 %collective-permute-start.1 = (bf16[128,1536]{1,0:T(8,128)(2,1)}, bf16[128,1536]{1,0:T(8,128)(2,1)S(1)}, u32[]{:S(2)}, u32[]{:S(2)}) collective-permute-start(bf16[128,1536]{1,0:T(8,128)(2,1)} %refs_0_.1), channel_id=1, source_target_pairs={{8,0},{16,8},{24,16},{28,24},{20,28},{12,20},{4,12},{0,4},{9,1},{1... | collective-permute-start | bytes 1179656 | tf_op jit(solution)/shard_map/ppermute | solution.py:220
  12.3 30.4 %collective-permute-start.4 = (bf16[128,1536]{1,0:T(8,128)(2,1)S(1)}, bf16[128,1536]{1,0:T(8,128)(2,1)S(1)}, u32[]{:S(2)}, u32[]{:S(2)}) collective-permute-start(bf16[128,1536]{1,0:T(8,128)(2,1)S(1)} %collective-permute-done.refs_0_), channel_id=1, source_target_pairs={{0,8},{8,16},{16,24},{24,28},{28,20},{20,12},{12,4},{4,0},{1,9},{9... | collective-permute-start | bytes 1179656 | tf_op jit(solution)/shard_map/ppermute | solution.py:217
  14.1 40.5 %collective-permute-start.9 = (bf16[384,768]{1,0:T(8,128)(2,1)}, bf16[384,768]{1,0:T(8,128)(2,1)}, u32[]{:S(2)}, u32[]{:S(2)}) collective-permute-start(bf16[384,768]{1,0:T(8,128)(2,1)} %bitcast.3.refs_6_.refs_4_), channel_id=1, source_target_pairs={{0,2},{1,3},{2,0},{3,1},{4,6},{5,7},{6,4},{7,5},{8,10},{9,11},{10,... | collective-permute-start | bytes 1769480 | tf_op jit(solution)/shard_map/ppermute | solution.py:194
  15.6 39.5 %collective-permute-start.12 = (bf16[384,768]{1,0:T(8,128)(2,1)}, bf16[384,768]{1,0:T(8,128)(2,1)}, u32[]{:S(2)}, u32[]{:S(2)}) collective-permute-start(bf16[384,768]{1,0:T(8,128)(2,1)} %bitcast.4.refs_10_.refs_8_), channel_id=1, source_target_pairs={{0,2},{1,3},{2,0},{3,1},{4,6},{5,7},{6,4},{7,5},{8,10},{9,11},{10,... | collective-permute-start | bytes 1769480 | tf_op jit(solution)/shard_map/ppermute | solution.py:194
  42.1 11.7 %collective-permute-start.5 = (bf16[128,1536]{1,0:T(8,128)(2,1)S(1)}, bf16[128,1536]{1,0:T(8,128)(2,1)S(1)}, u32[]{:S(2)}, u32[]{:S(2)}) collective-permute-start(bf16[128,1536]{1,0:T(8,128)(2,1)S(1)} %collective-permute-done.1.refs_1_), channel_id=1, source_target_pairs={{8,0},{16,8},{24,16},{28,24},{20,28},{12,20},{4,12},{0,4},{9,1},{1... | collective-permute-start | bytes 1179656 | tf_op jit(solution)/shard_map/ppermute | solution.py:220
  42.7 12.6 %collective-permute-start.14 = (bf16[128,1536]{1,0:T(8,128)(2,1)S(1)}, bf16[128,1536]{1,0:T(8,128)(2,1)S(1)}, u32[]{:S(2)}, u32[]{:S(2)}) collective-permute-start(bf16[128,1536]{1,0:T(8,128)(2,1)S(1)} %collective-permute-done.4.refs_0_), channel_id=1, source_target_pairs={{0,8},{8,16},{16,24},{24,28},{28,20},{20,12},{12,4},{4,0},{1,9},{9... | collective-permute-start | bytes 1179656 | tf_op jit(solution)/shard_map/ppermute | solution.py:217
  45.3 9.3 %collective-permute-start.22 = (bf16[192,768]{1,0:T(8,128)(2,1)S(1)}, bf16[192,768]{1,0:T(8,128)(2,1)S(1)}, u32[]{:S(2)}, u32[]{:S(2)}) collective-permute-start(bf16[192,768]{1,0:T(8,128)(2,1)S(1)} %get-tuple-element.67.refs_5_), channel_id=1, source_target_pairs={{0,2},{1,3},{2,0},{3,1},{4,6},{5,7},{6,4},{7,5},{8,10},{9,11},{10,... | collective-permute-start | bytes 884744 | tf_op jit(solution)/shard_map/ppermute | solution.py:194
  53.8 7.8 %collective-permute-start.15 = (bf16[128,1536]{1,0:T(8,128)(2,1)S(1)}, bf16[128,1536]{1,0:T(8,128)(2,1)S(1)}, u32[]{:S(2)}, u32[]{:S(2)}) collective-permute-start(bf16[128,1536]{1,0:T(8,128)(2,1)S(1)} %collective-permute-done.5.refs_1_), channel_id=1, source_target_pairs={{8,0},{16,8},{24,16},{28,24},{20,28},{12,20},{4,12},{0,4},{9,1},{1... | collective-permute-start | bytes 1179656 | tf_op jit(solution)/shard_map/ppermute | solution.py:220
  54.6 11.1 %collective-permute-start.11 = (bf16[384,768]{1,0:T(8,128)(2,1)}, bf16[384,768]{1,0:T(8,128)(2,1)}, u32[]{:S(2)}, u32[]{:S(2)}) collective-permute-start(bf16[384,768]{1,0:T(8,128)(2,1)} %bitcast.4.refs_10_.refs_8_), channel_id=1, source_target_pairs={{0,1},{1,0},{2,3},{3,2},{4,5},{5,4},{6,7},{7,6},{8,9},{9,8},{10,11... | collective-permute-start | bytes 1769480 | tf_op jit(solution)/shard_map/ppermute | solution.py:194
  54.6 12.0 %collective-permute-start.8 = (bf16[384,768]{1,0:T(8,128)(2,1)}, bf16[384,768]{1,0:T(8,128)(2,1)}, u32[]{:S(2)}, u32[]{:S(2)}) collective-permute-start(bf16[384,768]{1,0:T(8,128)(2,1)} %bitcast.3.refs_6_.refs_4_), channel_id=1, source_target_pairs={{0,1},{1,0},{2,3},{3,2},{4,5},{5,4},{6,7},{7,6},{8,9},{9,8},{10,11... | collective-permute-start | bytes 1769480 | tf_op jit(solution)/shard_map/ppermute | solution.py:194
  55.1 12.0 %collective-permute-start.10 = (bf16[384,768]{1,0:T(8,128)(2,1)}, bf16[384,768]{1,0:T(8,128)(2,1)}, u32[]{:S(2)}, u32[]{:S(2)}) collective-permute-start(bf16[384,768]{1,0:T(8,128)(2,1)} %collective-permute-done.9.refs_8_.refs_6_), channel_id=1, source_target_pairs={{0,1},{1,0},{2,3},{3,2},{4,5},{5,4},{6,7},{7,6},{8,9},{9,8},{10,11... | collective-permute-start | bytes 1769480 | tf_op jit(solution)/shard_map/ppermute | solution.py:194
  55.2 13.5 %collective-permute-start.13 = (bf16[384,768]{1,0:T(8,128)(2,1)}, bf16[384,768]{1,0:T(8,128)(2,1)}, u32[]{:S(2)}, u32[]{:S(2)}) collective-permute-start(bf16[384,768]{1,0:T(8,128)(2,1)} %collective-permute-done.12.refs_12_.refs_10_), channel_id=1, source_target_pairs={{0,1},{1,0},{2,3},{3,2},{4,5},{5,4},{6,7},{7,6},{8,9},{9,8},{10,11... | collective-permute-start | bytes 1769480 | tf_op jit(solution)/shard_map/ppermute | solution.py:194
  61.6 13.9 %collective-permute-start.32 = (bf16[192,768]{1,0:T(8,128)(2,1)S(1)}, bf16[192,768]{1,0:T(8,128)(2,1)}, u32[]{:S(2)}, u32[]{:S(2)}) collective-permute-start(bf16[192,768]{1,0:T(8,128)(2,1)S(1)} %get-tuple-element.68.refs_5_), channel_id=1, source_target_pairs={{0,2},{1,3},{2,0},{3,1},{4,6},{5,7},{6,4},{7,5},{8,10},{9,11},{10,... | collective-permute-start | bytes 884744 | tf_op jit(solution)/shard_map/ppermute | solution.py:194
  66.7 14.3 %collective-permute-start.21 = (bf16[192,768]{1,0:T(8,128)(2,1)S(1)}, bf16[192,768]{1,0:T(8,128)(2,1)S(1)}, u32[]{:S(2)}, u32[]{:S(2)}) collective-permute-start(bf16[192,768]{1,0:T(8,128)(2,1)S(1)} %copy-done.2), channel_id=1, source_target_pairs={{0,1},{1,0},{2,3},{3,2},{4,5},{5,4},{6,7},{7,6},{8,9},{9,8},{10,11... | collective-permute-start | bytes 884744 | tf_op jit(solution)/shard_map/ppermute | solution.py:194
  66.7 14.3 %collective-permute-start.23 = (bf16[192,768]{1,0:T(8,128)(2,1)S(1)}, bf16[192,768]{1,0:T(8,128)(2,1)S(1)}, u32[]{:S(2)}, u32[]{:S(2)}) collective-permute-start(bf16[192,768]{1,0:T(8,128)(2,1)S(1)} %copy-done.5), channel_id=1, source_target_pairs={{0,1},{1,0},{2,3},{3,2},{4,5},{5,4},{6,7},{7,6},{8,9},{9,8},{10,11... | collective-permute-start | bytes 884744 | tf_op jit(solution)/shard_map/ppermute | solution.py:194
  67.2 8.4 %collective-permute-start.18 = (bf16[64,1536]{1,0:T(8,128)(2,1)S(1)}, bf16[64,1536]{1,0:T(8,128)(2,1)S(1)}, u32[]{:S(2)}, u32[]{:S(2)}) collective-permute-start(bf16[64,1536]{1,0:T(8,128)(2,1)S(1)} %slice.16), channel_id=1, source_target_pairs={{0,8},{8,16},{16,24},{24,28},{28,20},{20,12},{12,4},{4,0},{1,9},{9... | collective-permute-start | bytes 589832 | tf_op jit(solution)/shard_map/ppermute | solution.py:217
  68.8 7.3 %collective-permute-start.19 = (bf16[64,1536]{1,0:T(8,128)(2,1)S(1)}, bf16[64,1536]{1,0:T(8,128)(2,1)S(1)}, u32[]{:S(2)}, u32[]{:S(2)}) collective-permute-start(bf16[64,1536]{1,0:T(8,128)(2,1)S(1)} %slice.17), channel_id=1, source_target_pairs={{8,0},{16,8},{24,16},{28,24},{20,28},{12,20},{4,12},{0,4},{9,1},{1... | collective-permute-start | bytes 589832 | tf_op jit(solution)/shard_map/ppermute | solution.py:220
  75.5 9.3 %collective-permute-start.31 = (bf16[192,768]{1,0:T(8,128)(2,1)S(1)}, bf16[192,768]{1,0:T(8,128)(2,1)S(1)}, u32[]{:S(2)}, u32[]{:S(2)}) collective-permute-start(bf16[192,768]{1,0:T(8,128)(2,1)S(1)} %get-tuple-element.68.refs_5_), channel_id=1, source_target_pairs={{0,1},{1,0},{2,3},{3,2},{4,5},{5,4},{6,7},{7,6},{8,9},{9,8},{10,11... | collective-permute-start | bytes 884744 | tf_op jit(solution)/shard_map/ppermute | solution.py:194
  75.6 9.3 %collective-permute-start.33 = (bf16[192,768]{1,0:T(8,128)(2,1)}, bf16[192,768]{1,0:T(8,128)(2,1)S(1)}, u32[]{:S(2)}, u32[]{:S(2)}) collective-permute-start(bf16[192,768]{1,0:T(8,128)(2,1)} %collective-permute-done.32.refs_7_), channel_id=1, source_target_pairs={{0,1},{1,0},{2,3},{3,2},{4,5},{5,4},{6,7},{7,6},{8,9},{9,8},{10,11... | collective-permute-start | bytes 884744 | tf_op jit(solution)/shard_map/ppermute | solution.py:194
  84.4 7.8 %collective-permute-start.28 = (bf16[128,768]{1,0:T(8,128)(2,1)S(1)}, bf16[128,768]{1,0:T(8,128)(2,1)S(1)}, u32[]{:S(2)}, u32[]{:S(2)}) collective-permute-start(bf16[128,768]{1,0:T(8,128)(2,1)S(1)} %get-tuple-element.56), channel_id=1, source_target_pairs={{8,0},{16,8},{24,16},{28,24},{20,28},{12,20},{4,12},{0,4},{9,1},{1... | collective-permute-start | bytes 589832 | tf_op jit(solution)/shard_map/ppermute | solution.py:220
  87.4 9.0 %collective-permute-start.34 = (bf16[128,768]{1,0:T(8,128)(2,1)S(1)}, bf16[128,768]{1,0:T(8,128)(2,1)S(1)}, u32[]{:S(2)}, u32[]{:S(2)}) collective-permute-start(bf16[128,768]{1,0:T(8,128)(2,1)S(1)} %get-tuple-element.60), channel_id=1, source_target_pairs={{8,0},{16,8},{24,16},{28,24},{20,28},{12,20},{4,12},{0,4},{9,1},{1... | collective-permute-start | bytes 589832 | tf_op jit(solution)/shard_map/ppermute | solution.py:220
  87.9 9.0 %collective-permute-start.38 = (bf16[128,768]{1,0:T(8,128)(2,1)S(1)}, bf16[128,768]{1,0:T(8,128)(2,1)S(1)}, u32[]{:S(2)}, u32[]{:S(2)}) collective-permute-start(bf16[128,768]{1,0:T(8,128)(2,1)S(1)} %get-tuple-element.64), channel_id=1, source_target_pairs={{0,8},{8,16},{16,24},{24,28},{28,20},{20,12},{12,4},{4,0},{1,9},{9... | collective-permute-start | bytes 589832 | tf_op jit(solution)/shard_map/ppermute | solution.py:217
  89.8 9.4 %collective-permute-start.25 = (bf16[128,768]{1,0:T(8,128)(2,1)S(1)}, bf16[128,768]{1,0:T(8,128)(2,1)S(1)}, u32[]{:S(2)}, u32[]{:S(2)}) collective-permute-start(bf16[128,768]{1,0:T(8,128)(2,1)S(1)} %add_convert_fusion.11), channel_id=1, source_target_pairs={{0,8},{8,16},{16,24},{24,28},{28,20},{20,12},{12,4},{4,0},{1,9},{9... | collective-permute-start | bytes 589832 | tf_op jit(solution)/shard_map/ppermute | solution.py:217
  92.2 8.6 %collective-permute-start.29 = (bf16[128,768]{1,0:T(8,128)(2,1)S(1)}, bf16[128,768]{1,0:T(8,128)(2,1)S(1)}, u32[]{:S(2)}, u32[]{:S(2)}) collective-permute-start(bf16[128,768]{1,0:T(8,128)(2,1)S(1)} %add_convert_fusion.8), channel_id=1, source_target_pairs={{8,0},{16,8},{24,16},{28,24},{20,28},{12,20},{4,12},{0,4},{9,1},{1... | collective-permute-start | bytes 589832 | tf_op jit(solution)/shard_map/ppermute | solution.py:220
  96.4 8.4 %collective-permute-start.35 = (bf16[128,768]{1,0:T(8,128)(2,1)S(1)}, bf16[128,768]{1,0:T(8,128)(2,1)S(1)}, u32[]{:S(2)}, u32[]{:S(2)}) collective-permute-start(bf16[128,768]{1,0:T(8,128)(2,1)S(1)} %add_convert_fusion.5), channel_id=1, source_target_pairs={{8,0},{16,8},{24,16},{28,24},{20,28},{12,20},{4,12},{0,4},{9,1},{1... | collective-permute-start | bytes 589832 | tf_op jit(solution)/shard_map/ppermute | solution.py:220
  97.0 8.4 %collective-permute-start.39 = (bf16[128,768]{1,0:T(8,128)(2,1)S(1)}, bf16[128,768]{1,0:T(8,128)(2,1)S(1)}, u32[]{:S(2)}, u32[]{:S(2)}) collective-permute-start(bf16[128,768]{1,0:T(8,128)(2,1)S(1)} %add_convert_fusion.2), channel_id=1, source_target_pairs={{0,8},{8,16},{16,24},{24,28},{28,20},{20,12},{12,4},{4,0},{1,9},{9... | collective-permute-start | bytes 589832 | tf_op jit(solution)/shard_map/ppermute | solution.py:217
  99.2 8.4 %collective-permute-start.26 = (bf16[128,768]{1,0:T(8,128)(2,1)S(1)}, bf16[128,768]{1,0:T(8,128)(2,1)S(1)}, u32[]{:S(2)}, u32[]{:S(2)}) collective-permute-start(bf16[128,768]{1,0:T(8,128)(2,1)S(1)} %add_convert_fusion.10), channel_id=1, source_target_pairs={{0,8},{8,16},{16,24},{24,28},{28,20},{20,12},{12,4},{4,0},{1,9},{9... | collective-permute-start | bytes 589832 | tf_op jit(solution)/shard_map/ppermute | solution.py:217
  100.9 11.7 %collective-permute-start.30 = (bf16[128,768]{1,0:T(8,128)(2,1)S(1)}, bf16[128,768]{1,0:T(8,128)(2,1)S(1)}, u32[]{:S(2)}, u32[]{:S(2)}) collective-permute-start(bf16[128,768]{1,0:T(8,128)(2,1)S(1)} %add_convert_fusion.7), channel_id=1, source_target_pairs={{8,0},{16,8},{24,16},{28,24},{20,28},{12,20},{4,12},{0,4},{9,1},{1... | collective-permute-start | bytes 589832 | tf_op jit(solution)/shard_map/ppermute | solution.py:220
  104.9 7.2 %collective-permute-start.36 = (bf16[128,768]{1,0:T(8,128)(2,1)S(1)}, bf16[128,768]{1,0:T(8,128)(2,1)S(1)}, u32[]{:S(2)}, u32[]{:S(2)}) collective-permute-start(bf16[128,768]{1,0:T(8,128)(2,1)S(1)} %add_convert_fusion.4), channel_id=1, source_target_pairs={{8,0},{16,8},{24,16},{28,24},{20,28},{12,20},{4,12},{0,4},{9,1},{1... | collective-permute-start | bytes 589832 | tf_op jit(solution)/shard_map/ppermute | solution.py:220
  105.4 9.7 %collective-permute-start.40 = (bf16[128,768]{1,0:T(8,128)(2,1)S(1)}, bf16[128,768]{1,0:T(8,128)(2,1)S(1)}, u32[]{:S(2)}, u32[]{:S(2)}) collective-permute-start(bf16[128,768]{1,0:T(8,128)(2,1)S(1)} %add_convert_fusion.1), channel_id=1, source_target_pairs={{0,8},{8,16},{16,24},{24,28},{28,20},{20,12},{12,4},{4,0},{1,9},{9... | collective-permute-start | bytes 589832 | tf_op jit(solution)/shard_map/ppermute | solution.py:217
  107.6 7.4 %collective-permute-start.27 = (bf16[128,768]{1,0:T(8,128)(2,1)S(1)}, bf16[128,768]{1,0:T(8,128)(2,1)S(1)}, u32[]{:S(2)}, u32[]{:S(2)}) collective-permute-start(bf16[128,768]{1,0:T(8,128)(2,1)S(1)} %add_convert_fusion.9), channel_id=1, source_target_pairs={{0,8},{8,16},{16,24},{24,28},{28,20},{20,12},{12,4},{4,0},{1,9},{9... | collective-permute-start | bytes 589832 | tf_op jit(solution)/shard_map/ppermute | solution.py:217
  (18 other events, 114.2 us)

commit v2 on v0

v2 whole, which is shorter than its diff:
```python
import functools

import jax
import jax.numpy as jnp
from jax import lax
from jax.experimental import pallas as pl
from jax.experimental.pallas import tpu as pltpu
from jax.sharding import PartitionSpec as P

VMEM_LIMIT = 28 * 1024 * 1024
MOST_VMEM = 60 * 1024 * 1024
MUCH_VMEM = 54 * 1024 * 1024
EXTRA = 128
WHOLE = pl.BlockSpec(memory_space=pltpu.VMEM)
SCALAR = pl.BlockSpec(memory_space=pltpu.SMEM)
ANYWHERE = pl.BlockSpec(memory_space=pl.ANY)


def params(limit=VMEM_LIMIT):
    return pltpu.CompilerParams(vmem_limit_bytes=limit)


def cost(flops, moved):
    return pl.CostEstimate(flops=int(flops), bytes_accessed=int(moved), transcendentals=0)


def ring_order(holders):
    columns = 1
    while 2 * (columns * 2) ** 2 <= holders:
        columns *= 2
    columns = max(columns, 2) if holders >= 4 else 1
    rows = holders // columns
    order = [row * columns for row in range(rows)]
    for back, row in enumerate(reversed(range(rows))):
        line = range(1, columns) if back % 2 == 0 else reversed(range(1, columns))
        order += [row * columns + column for column in line]
    return order


def after_kernel(*refs):
    pass


def after(place, value, *others):
    marks = [other[:8, :128] for other in others]
    return pl.pallas_call(
        after_kernel,
        out_shape=jax.ShapeDtypeStruct(value.shape, value.dtype),
        in_specs=[place] + [WHOLE] * len(marks),
        out_specs=place,
        input_output_aliases={0: 0},
        compiler_params=params(),
        cost_estimate=cost(0, 4096),
        name="after",
    )(value, *marks)


def pack_kernel(experts, *refs):
    sources, (out_ref, pair_ref, gain_ref, router_ref, routes_ref, token_ref, sems) = refs[:6], refs[6:]
    depth = sources[4].shape[0]
    targets = [gain_ref, router_ref, routes_ref, token_ref]
    targets += [pair_ref.at[:depth, :], pair_ref.at[depth:, :]]
    copies = [
        pltpu.make_async_copy(source, target, sems.at[at])
        for at, (source, target) in enumerate(zip(sources, targets))
    ]
    for copy in copies:
        copy.start()
    for copy in copies[:4]:
        copy.wait()
    rows, width = token_ref.shape
    gain = gain_ref[...].astype(jnp.float32)[None, :]
    for at in range(0, rows, 32):
        values = token_ref[at : at + 32, :].astype(jnp.float32)
        square = jnp.mean(values * values, axis=-1, keepdims=True)
        normed = values * lax.rsqrt(square + 1e-06) * gain
        out_ref[at : at + 32, :width] = normed.astype(jnp.bfloat16)
    logits = lax.dot_general(
        out_ref[:, :width],
        router_ref[...],
        (((1,), (1,)), ((), ())),
        preferred_element_type=jnp.float32,
    )
    routes = routes_ref[...]
    lanes = lax.broadcasted_iota(jnp.int32, (128, rows), 0)
    named = lanes == routes[0:1, :]
    for choice in range(1, routes.shape[0]):
        named = named | (lanes == routes[choice : choice + 1, :])
    named = jnp.where(named, 1.0, 0.0).T[:, :experts] > 0
    picked = jnp.where(named, jax.nn.sigmoid(logits), 0.0)
    weight = picked / jnp.sum(picked, axis=1, keepdims=True)
    weight = jnp.where(named, weight, 0.0)
    high = weight.astype(jnp.bfloat16)
    low = (weight - high.astype(jnp.float32)).astype(jnp.bfloat16)
    spare = jnp.zeros((rows, EXTRA - 2 * experts), jnp.bfloat16)
    out_ref[:, width:] = jnp.concatenate([high, low, spare], axis=1)
    for copy in copies[4:]:
        copy.wait()


def pack(gain, router, names, tokens, gate, upper):
    rows, width = tokens.shape
    depth, units = gate.shape
    small = [gain, router, names, tokens]
    return pl.pallas_call(
        functools.partial(pack_kernel, router.shape[0]),
        out_shape=(
            jax.ShapeDtypeStruct((rows, width + EXTRA), jnp.bfloat16),
            jax.ShapeDtypeStruct((2 * depth, units), jnp.bfloat16),
        ),
        in_specs=[ANYWHERE] * 6,
        out_specs=(WHOLE, WHOLE),
        scratch_shapes=[pltpu.VMEM(x.shape, x.dtype) for x in small]
        + [pltpu.SemaphoreType.DMA((6,))],
        compiler_params=params(MOST_VMEM),
        cost_estimate=cost(rows * width * 16, rows * width * 4 + 8 * depth * units),
        name="pack",
    )(*small, gate, upper)


def fetch(me, refs, first, columns, target, sems):
    depth = target.shape[0] // len(refs)
    copies = []
    for apart, ref in enumerate(refs):
        at = pl.multiple_of((me ^ apart) * depth, depth)
        source = ref.at[pl.ds(first, depth), columns]
        copy = pltpu.make_async_copy(source, target.at[pl.ds(at, depth), :], sems.at[apart])
        copy.start()
        copies.append(copy)
    return copies


def hidden_rows(rows, own_ref, gate_mat, upper_mat, ready=()):
    width = gate_mat.shape[0]
    scale = jnp.sum(rows[:, width:].astype(jnp.float32) * own_ref[...], axis=1, keepdims=True)
    gate = jnp.dot(rows[:, :width], gate_mat[...], preferred_element_type=jnp.float32)
    for copy in ready:
        copy.wait()
    upper = jnp.dot(rows[:, :width], upper_mat[...], preferred_element_type=jnp.float32)
    hidden = jnp.where(scale > 0, jnp.maximum(gate, 0.0) * upper * scale, 0.0)
    return hidden.astype(jnp.bfloat16)


def first_hidden_kernel(inputs, pieces, me_ref, own_ref, *refs):
    blocks, weights = refs[:inputs], refs[inputs : inputs + pieces]
    outs, scratch = refs[inputs + pieces : -4], refs[-4:]
    outs, (gate_mat, upper_mat) = outs[:-2], outs[-2:]
    rows_ref, gate_sems, upper_sems, row_sems = scratch
    width, units = gate_mat.shape
    columns = pl.ds(0, units)
    row_copies, at = [], 0
    for place, block in enumerate(blocks):
        target = rows_ref.at[at : at + block.shape[0], :]
        row_copies.append(pltpu.make_async_copy(block, target, row_sems.at[place]))
        at += block.shape[0]
    for copy in row_copies:
        copy.start()
    gate_copies = fetch(me_ref[0], weights, 0, columns, gate_mat, gate_sems)
    upper_copies = fetch(me_ref[0], weights, width // pieces, columns, upper_mat, upper_sems)
    for copy in row_copies + gate_copies:
        copy.wait()
    at = 0
    for out in outs:
        rows = rows_ref[at : at + out.shape[0], :]
        ready = () if at else upper_copies
        out[...] = hidden_rows(rows, own_ref, gate_mat, upper_mat, ready)
        at += out.shape[0]


def first_hidden_blocks(me, own, groups, pairs):
    pieces = len(pairs)
    width, units = pairs[0].shape[0] // 2 * pieces, pairs[0].shape[1]
    heights = [sum(block.shape[0] for block in group) for group in groups]
    blocks = [block for group in groups for block in group]
    shapes = [(height, units) for height in heights] + [(width, units)] * 2
    return pl.pallas_call(
        functools.partial(first_hidden_kernel, len(blocks), pieces),
        out_shape=tuple(jax.ShapeDtypeStruct(shape, jnp.bfloat16) for shape in shapes),
        in_specs=[SCALAR, WHOLE] + [ANYWHERE] * (len(blocks) + pieces),
        out_specs=tuple(WHOLE for _ in shapes),
        scratch_shapes=[
            pltpu.VMEM((sum(heights), width + EXTRA), jnp.bfloat16),
            pltpu.SemaphoreType.DMA((pieces,)),
            pltpu.SemaphoreType.DMA((pieces,)),
            pltpu.SemaphoreType.DMA((len(blocks),)),
        ],
        compiler_params=params(MUCH_VMEM),
        name="first_hidden",
    )(me, own, *blocks, *pairs)


def hidden_kernel(counts, own_ref, gate_mat, upper_mat, *refs):
    outs, at = refs[sum(counts) :], 0
    for count, out in zip(counts, outs):
        group = [block[...] for block in refs[at : at + count]]
        at += count
        rows = jnp.concatenate(group, axis=0) if count > 1 else group[0]
        out[...] = hidden_rows(rows, own_ref, gate_mat, upper_mat)


def hidden_blocks(own, groups, gate_mat, upper_mat):
    width, units = gate_mat.shape
    heights = [sum(block.shape[0] for block in group) for group in groups]
    blocks = [block for group in groups for block in group]
    return pl.pallas_call(
        functools.partial(hidden_kernel, [len(group) for group in groups]),
        out_shape=tuple(jax.ShapeDtypeStruct((h, units), jnp.bfloat16) for h in heights),
        in_specs=[WHOLE] * (3 + len(blocks)),
        out_specs=tuple(WHOLE for _ in groups),
        compiler_params=params(),
        name="hidden",
    )(own, gate_mat, upper_mat, *blocks)


def down_kernel(slots, pieces, column, me_ref, *refs):
    inputs = len(slots)
    hidden = refs[:inputs]
    outs = refs[inputs + pieces : -2]
    down_mat, sems = refs[-2:]
    columns = pl.ds(column, down_mat.shape[1])
    for copy in fetch(me_ref[0], refs[inputs : inputs + pieces], 0, columns, down_mat, sems):
        copy.wait()
    for group, parts in zip(hidden, slots):
        out = jnp.dot(group[...], down_mat[...], preferred_element_type=jnp.float32)
        at = 0
        for slot, first, count in parts:
            part = out[at : at + count, :]
            outs[slot][first : first + count, :] = part.astype(outs[slot].dtype)
            at += count


def down_blocks(me, column, width, hidden, slots, kinds, downs):
    pieces = len(downs)
    units = downs[0].shape[0] * pieces
    flat = [part for parts in slots for part in parts]
    heights = [sum(c for slot, _, c in flat if slot == at) for at in range(len(kinds))]
    rows = sum(heights)
    return pl.pallas_call(
        functools.partial(down_kernel, slots, pieces, column),
        out_shape=tuple(
            jax.ShapeDtypeStruct((height, width), kind) for height, kind in zip(heights, kinds)
        ),
        in_specs=[SCALAR] + [WHOLE] * len(hidden) + [ANYWHERE] * pieces,
        out_specs=tuple(WHOLE for _ in kinds),
        scratch_shapes=[
            pltpu.VMEM((units, width), jnp.bfloat16),
            pltpu.SemaphoreType.DMA((pieces,)),
        ],
        compiler_params=params(),
        cost_estimate=cost(2 * rows * width * units, 2 * width * units + 4 * rows * width),
        name="down",
    )(me, *hidden, *downs)


def swap_blk(value, bit):
    pairs = [(i, i ^ bit) for i in range(lax.axis_size("blk"))]
    return lax.ppermute(value, "blk", pairs)


def outer_rounds(piece):
    have = {0: piece}
    bit = lax.axis_size("blk") // 2
    while bit > 1:
        have.update({k ^ bit: swap_blk(value, bit) for k, value in list(have.items())})
        bit //= 2
    return have


def last_round(have, *others):
    have = {k: after(ANYWHERE, value, *others) if k else value for k, value in have.items()}
    have.update({k ^ 1: swap_blk(value, 1) for k, value in list(have.items())})
    return [have[k] for k in sorted(have)]


def add_round(*terms):
    total = terms[0].astype(jnp.float32)
    for term in terms[1:]:
        total = total + term.astype(jnp.float32)
    return total.astype(jnp.bfloat16)


def on_device(
    tokens, norm_gain, router_weight, routes, placement, gate_weight, up_weight, down_weight
):
    holders = lax.axis_size("ep")
    tok_rows, width = tokens.shape
    far = holders // 2
    order = ring_order(holders)
    ahead = [(order[i], order[(i + 1) % holders]) for i in range(holders)]
    behind = [(target, source) for source, target in ahead]

    def clock(x):
        return lax.ppermute(x, "ep", ahead)

    def counter(x):
        return lax.ppermute(x, "ep", behind)

    me = lax.axis_index("blk").astype(jnp.int32).reshape(1)
    experts = router_weight.shape[1]
    held = (placement == lax.axis_index("ep")).astype(jnp.float32)
    own = jnp.pad(jnp.concatenate([held, held]), (0, EXTRA - 2 * experts))[None, :]

    packed, pair = pack(
        norm_gain, router_weight.T, routes.T, tokens, gate_weight[0], up_weight[0]
    )
    pairs = outer_rounds(pair)
    half = width // 2
    downs = outer_rounds(down_weight[0])

    cut = tok_rows // 2
    from_behind, from_ahead = [packed], [packed]
    for step in range(1, far):
        from_behind.append(clock(from_behind[-1]))
        from_ahead.append(counter(from_ahead[-1]))
    far_parts = [clock(from_behind[-1][:cut]), counter(from_ahead[-1][cut:])]

    pairs = last_round(pairs, from_behind[far - 1], from_ahead[far - 1])

    groups = [[((0, 0), 0, packed)]]
    for step in range(1, far):
        groups.append([((-1, step), 0, from_behind[step]), ((1, step), 0, from_ahead[step])])
    groups.append([((0, far), 0, far_parts[0]), ((0, far), cut, far_parts[1])])
    def only_blocks(chosen):
        return [[block for _, _, block in group] for group in chosen]

    *hidden, gate_mat, upper_mat = first_hidden_blocks(me, own, only_blocks(groups[:3]), pairs)
    first_done = hidden[-1]
    for low in range(3, len(groups), 2):
        blocks = only_blocks(groups[low : low + 2])
        blocks[-1] = [after(WHOLE, block, first_done) for block in blocks[-1]]
        hidden += hidden_blocks(own, blocks, gate_mat, upper_mat)

    downs = last_round(downs, hidden[-1])
    results = []
    for side in range(2):
        long_way, short_way = (clock, counter) if side == 0 else (counter, clock)
        long_sign = 1 if side == 0 else -1
        sent_first = [(0, far), (-long_sign, far - 1)]
        table = {}
        for low in range(0, len(hidden), 5):
            chosen = groups[low : low + 5]
            keys = list(dict.fromkeys(key for group in chosen for key, _, _ in group))
            kinds = [jnp.bfloat16 if key in sent_first else jnp.float32 for key in keys]
            slots = [
                [(keys.index(key), first, block.shape[0]) for key, first, block in group]
                for group in chosen
            ]
            outs = down_blocks(me, side * half, half, hidden[low : low + 5], slots, kinds, downs)
            table.update(zip(keys, outs))
        long_run = long_way(table[0, far])
        short_run = short_way(table[-long_sign, far - 1])
        for step in range(far - 1, 0, -1):
            long_run = long_way(add_round(long_run, table[long_sign, step]))
            if step > 1:
                short_run = short_way(add_round(short_run, table[-long_sign, step - 1]))
        results.append(add_round(table[0, 0], long_run, short_run))
    return jnp.concatenate(results, axis=1)


def solution(mesh):
    in_specs = (
        P(("ep", "blk"), None),
        P(),
        P(),
        P(("ep", "blk"), None),
        P(),
        P("ep", "blk", None),
        P("ep", "blk", None),
        P("ep", "blk", None),
    )
    out_specs = P(("ep", "blk"), None)
    return jax.shard_map(
        on_device, mesh=mesh, in_specs=in_specs, out_specs=out_specs, check_vma=False
    )
```

time: 257 us -> 98.4 us (0.38); the launches traced: 254 us -> 98.1 us
  local copies, waits for them, and re-layouts: 102 us -> 5.37 us
  waiting for transfers between devices: 106 us -> 46.3 us
  starting transfers between devices: 10.5 us -> 28.3 us
  Pallas kernels: 0 us -> 16 us
  matrix products: 14.4 us -> 0 us
  between operations: 13.3 us -> 0.27 us
  other arithmetic: 7.42 us -> 1.85 us
    all_to_all x2 -> x0, waiting for transfers between devices: 104 us -> none  [the longest x1 53 us: on_device(): lax.all_to_all(outgoing, 'ep', split_axis=0, concat_axis=0, tiled=True)]
    scatter x1 -> x0, local copies, waits for them, and re-layouts: 82.3 us -> none  [on_device(): jnp.zeros((holders, capacity, width), jnp.bfloat16).at[target, slots]]
    ppermute x0 -> x28, waiting for transfers between devices: none -> 46.3 us  [the longest x11 30.2 us: clock(): return lax.ppermute(x, 'ep', ahead)]
    ppermute x0 -> x28, starting transfers between devices: none -> 28.3 us  [the longest x11 19.7 us: clock(): return lax.ppermute(x, 'ep', ahead)]
    pallas_call x0 -> x9, Pallas kernels: none -> 16 us  [the longest x1 7.93 us: first_hidden_blocks(): pl.pallas_call(functools.partial(first_hidden_kernel, len(blocks), pieces...]
    dot_general x3 -> x0, matrix products: 14.4 us -> none  [the longest x2 14.2 us: add_product(): return jnp.dot(left, piece, preferred_element_type=jnp.float32)]
    gather x6 -> x0, local copies, waits for them, and re-layouts: 12.6 us -> none  [the longest x1 9.69 us: on_device(): collected = returned[target, slots].astype(jnp.float32)]
    all_to_all x2 -> x0, starting transfers between devices: 10.4 us -> none  [the longest x1 6.49 us: on_device(): lax.all_to_all(outgoing, 'ep', split_axis=0, concat_axis=0, tiled=True)]
  transfers between devices with their start and end apart: 5 -> 28, of which waited for: 2 -> 13; matrix products, arithmetic and copies ran while one was open for 39% -> 2% of each run, Pallas kernels for 0% -> 12%
where the time goes in v2:
time: 98.4 us; the launch traced here: 98.1 us
  waiting for transfers between devices  46.3 us (47%)
  starting transfers between devices  28.3 us (29%)
  Pallas kernels  16 us (16%)
  local copies, waits for them, and re-layouts  5.37 us (5%)
  other arithmetic  1.85 us (2%)
    ppermute x11, waiting for transfers between devices, clock(): return lax.ppermute(x, 'ep', ahead)  30.2 us
    ppermute x11, starting transfers between devices, clock(): return lax.ppermute(x, 'ep', ahead)  19.7 us
    ppermute x11, waiting for transfers between devices, counter(): return lax.ppermute(x, 'ep', behind)  14.5 us
    pallas_call x1, Pallas kernels, first_hidden_blocks(): pl.pallas_call(functools.partial(first_hidden_kernel, len(blocks), pieces...  7.93 us
    unnamed x26, local copies, waits for them, and re-layouts  4.64 us
    ppermute x11, starting transfers between devices, counter(): return lax.ppermute(x, 'ep', behind)  4.49 us
    ppermute x6, starting transfers between devices, swap_blk(): return lax.ppermute(value, 'blk', pairs)  4.12 us
    pallas_call x2, Pallas kernels, down_blocks(): pl.pallas_call(functools.partial(down_kernel, slots, pieces, column), out...  3.12 us
  transfers between devices with their start and end apart: 28, of which 13 were waited for; matrix products, arithmetic and copies ran while one was open for 2% of the time, Pallas kernels for 12%

profile of v2, /device:TPU:0, one launch (start us, length us, event | category | flops | bytes accessed | tf_op | source)
XLA Modules:
  0.0 98.1 jit_solution(5382891571348196922)
XLA Ops:
  0.0 2.9 %pack.1 = (bf16[128,1664]{1,0:T(8,128)(2,1)}, bf16[768,768]{1,0:T(8,128)(2,1)}) custom-call(bf16[1536]{0:T(1024)(128)(2,1)} %refs_0_.1, bf16[8,1536]{1,0:T(8,128)(2,1)} %bitcast.14, s32[4,128]{1,0:T(4,128)} %bitcast.15, bf16[128,1536]{1,0:T(8,128)(2,1)} %refs_3_.1, bf16[384,768]{1,0:T(8,128)(2,1)} %bitcast.12, bf16[384,768]{1,0:T(8,128)(2,1)} %bitcast.13), custom_call_target="tpu_custom_call" | custom-call | flops 3145728 | bytes 3145728 | tf_op jit(solution)/shard_map/pack/pallas_call | solution.py:105
  2.9 3.1 %collective-permute-start = (bf16[128,1664]{1,0:T(8,128)(2,1)}, bf16[128,1664]{1,0:T(8,128)(2,1)S(1)}, u32[]{:S(2)}, u32[]{:S(2)}) collective-permute-start(bf16[128,1664]{1,0:T(8,128)(2,1)} %get-tuple-element.30.refs_0_), channel_id=1, source_target_pairs={{0,8},{8,16},{16,24},{24,28},{28,20},{20,12},{12,4},{4,0},{1,9},{9... | collective-permute-start | bytes 1277960 | tf_op jit(solution)/shard_map/ppermute | solution.py:293
  5.9 2.0 %collective-permute-start.5 = (bf16[768,768]{1,0:T(8,128)(2,1)}, bf16[768,768]{1,0:T(8,128)(2,1)S(1)}, u32[]{:S(2)}, u32[]{:S(2)}) collective-permute-start(bf16[768,768]{1,0:T(8,128)(2,1)} %get-tuple-element.31.refs_5_), channel_id=1, source_target_pairs={{0,2},{1,3},{2,0},{3,1},{4,6},{5,7},{6,4},{7,5},{8,10},{9,11},{10,... | collective-permute-start | bytes 3538952 | tf_op jit(solution)/shard_map/ppermute | solution.py:257
  7.9 8.0 %collective-permute-done.refs_1_ = bf16[128,1664]{1,0:T(8,128)(2,1)S(1)} collective-permute-done((bf16[128,1664]{1,0:T(8,128)(2,1)}, bf16[128,1664]{1,0:T(8,128)(2,1)S(1)}, u32[]{:S(2)}, u32[]{:S(2)}) %collective-permute-start) | collective-permute-done | bytes 426016 | tf_op jit(solution)/shard_map/ppermute | solution.py:293
  15.9 1.8 %collective-permute-start.2 = (bf16[128,1664]{1,0:T(8,128)(2,1)S(1)}, bf16[128,1664]{1,0:T(8,128)(2,1)S(1)}, u32[]{:S(2)}, u32[]{:S(2)}) collective-permute-start(bf16[128,1664]{1,0:T(8,128)(2,1)S(1)} %collective-permute-done.refs_1_), channel_id=1, source_target_pairs={{0,8},{8,16},{16,24},{24,28},{28,20},{20,12},{12,4},{4,0},{1,9},{9... | collective-permute-start | bytes 1277960 | tf_op jit(solution)/shard_map/ppermute | solution.py:293
  17.9 9.0 %collective-permute-done.2.refs_3_ = bf16[128,1664]{1,0:T(8,128)(2,1)S(1)} collective-permute-done((bf16[128,1664]{1,0:T(8,128)(2,1)S(1)}, bf16[128,1664]{1,0:T(8,128)(2,1)S(1)}, u32[]{:S(2)}, u32[]{:S(2)}) %collective-permute-start.2) | collective-permute-done | bytes 426016 | tf_op jit(solution)/shard_map/ppermute | solution.py:293
  26.9 1.5 %collective-permute-start.6 = (bf16[128,1664]{1,0:T(8,128)(2,1)S(1)}, bf16[128,1664]{1,0:T(8,128)(2,1)S(1)}, u32[]{:S(2)}, u32[]{:S(2)}) collective-permute-start(bf16[128,1664]{1,0:T(8,128)(2,1)S(1)} %collective-permute-done.2.refs_3_), channel_id=1, source_target_pairs={{0,8},{8,16},{16,24},{24,28},{28,20},{20,12},{12,4},{4,0},{1,9},{9... | collective-permute-start | bytes 1277960 | tf_op jit(solution)/shard_map/ppermute | solution.py:293
  28.9 8.0 %collective-permute-done.6.refs_0_ = bf16[128,1664]{1,0:T(8,128)(2,1)S(1)} collective-permute-done((bf16[128,1664]{1,0:T(8,128)(2,1)S(1)}, bf16[128,1664]{1,0:T(8,128)(2,1)S(1)}, u32[]{:S(2)}, u32[]{:S(2)}) %collective-permute-start.6) | collective-permute-done | bytes 426016 | tf_op jit(solution)/shard_map/ppermute | solution.py:293
  37.0 0.9 collective-permute-done.7.refs_1_
  38.0 1.3 %copy-done.5 = bf16[1,192,1536]{2,1,0:T(8,128)(2,1)S(1)} copy-done((bf16[1,192,1536]{2,1,0:T(8,128)(2,1)S(1)}, bf16[1,192,1536]{2,1,0:T(8,128)(2,1)}, u32[]{:S(2)}) %copy-start.5) | copy-done | bytes 589848
  39.3 1.5 %collective-permute-start.12 = (bf16[192,1536]{1,0:T(8,128)(2,1)S(1)}, bf16[192,1536]{1,0:T(8,128)(2,1)S(1)}, u32[]{:S(2)}, u32[]{:S(2)}) collective-permute-start(bf16[192,1536]{1,0:T(8,128)(2,1)S(1)} %bitcast.8), channel_id=1, source_target_pairs={{0,2},{1,3},{2,0},{3,1},{4,6},{5,7},{6,4},{7,5},{8,10},{9,11},{10,... | collective-permute-start | bytes 1769480 | tf_op jit(solution)/shard_map/ppermute | solution.py:257
  41.4 1.6 %collective-permute-start.9 = (bf16[64,1664]{1,0:T(8,128)(2,1)S(1)}, bf16[64,1664]{1,0:T(8,128)(2,1)S(1)}, u32[]{:S(2)}, u32[]{:S(2)}) collective-permute-start(bf16[64,1664]{1,0:T(8,128)(2,1)S(1)} %slice.27), channel_id=1, source_target_pairs={{0,8},{8,16},{16,24},{24,28},{28,20},{20,12},{12,4},{4,0},{1,9},{9... | collective-permute-start | bytes 638984 | tf_op jit(solution)/shard_map/ppermute | solution.py:293
  43.6 7.9 %first_hidden.1 = (bf16[128,768]{1,0:T(8,128)(2,1)}, bf16[256,768]{1,0:T(8,128)(2,1)}, bf16[256,768]{1,0:T(8,128)(2,1)}, bf16[1536,768]{1,0:T(8,128)(2,1)}, bf16[1536,768]{1,0:T(8,128)(2,1)}) custom-call(s32[1]{0:T(128)} %bitcast.me_ref, f32[1,128]{1,0:T(1,128)} %fusion.own_ref, bf16[128,1664]{1,0:T(8,128)(2,1)} %get-tuple-element.30.refs_0_, ...), custom_call_target="tpu_custom_call" | custom-call | tf_op jit(solution)/shard_map/first_hidden/pallas_call | solution.py:176
  52.3 1.7 %copy-done.1 = bf16[1536,768]{1,0:T(8,128)(2,1)S(1)} copy-done((bf16[1536,768]{1,0:T(8,128)(2,1)S(1)}, bf16[1536,768]{1,0:T(8,128)(2,1)}, u32[]{:S(2)}) %copy-start.1) | copy-done | bytes 2359320
  53.9 1.7 %copy-done.2 = bf16[1536,768]{1,0:T(8,128)(2,1)S(1)} copy-done((bf16[1536,768]{1,0:T(8,128)(2,1)S(1)}, bf16[1536,768]{1,0:T(8,128)(2,1)}, u32[]{:S(2)}) %copy-start.2) | copy-done | bytes 2359320
  55.6 2.1 %hidden.1 = (bf16[256,768]{1,0:T(8,128)(2,1)S(1)}, bf16[128,768]{1,0:T(8,128)(2,1)S(1)}) custom-call(f32[1,128]{1,0:T(1,128)S(1)} %copy-done.3, bf16[1536,768]{1,0:T(8,128)(2,1)S(1)} %copy-done.1, bf16[1536,768]{1,0:T(8,128)(2,1)S(1)} %copy-done.2, bf16[128,1664]{1,0:T(8,128)(2,1)S(1)} %collective-permute-done.6.refs_0_, ...), custom_call_target="tpu_custom_call" | custom-call | tf_op jit(solution)/shard_map/hidden/pallas_call | solution.py:205
  58.3 1.6 %collective-permute-done.13.refs_8_ = bf16[192,1536]{1,0:T(8,128)(2,1)S(1)} collective-permute-done((bf16[192,1536]{1,0:T(8,128)(2,1)S(1)}, bf16[192,1536]{1,0:T(8,128)(2,1)S(1)}, u32[]{:S(2)}, u32[]{:S(2)}) %collective-permute-start.13) | collective-permute-done | bytes 589856 | tf_op jit(solution)/shard_map/ppermute | solution.py:257
  59.9 1.6 %down.2 = (f32[128,768]{1,0:T(8,128)S(1)}, f32[128,768]{1,0:T(8,128)S(1)}, f32[128,768]{1,0:T(8,128)S(1)}, f32[128,768]{1,0:T(8,128)S(1)}, f32[128,768]{1,0:T(8,...) custom-call(s32[1]{0:T(128)} %bitcast.me_ref, ...), custom_call_target="tpu_custom_call" | custom-call | flops 1207959552 | bytes 4325376 | tf_op jit(solution)/shard_map/down/pallas_call | solution.py:238
  61.5 1.7 %collective-permute-start.14 = (bf16[128,768]{1,0:T(8,128)(2,1)S(1)}, bf16[128,768]{1,0:T(8,128)(2,1)S(1)}, u32[]{:S(2)}, u32[]{:S(2)}) collective-permute-start(bf16[128,768]{1,0:T(8,128)(2,1)S(1)} %get-tuple-element.40), channel_id=1, source_target_pairs={{0,8},{8,16},{16,24},{24,28},{28,20},{20,12},{12,4},{4,0},{1,9},{9... | collective-permute-start | bytes 589832 | tf_op jit(solution)/shard_map/ppermute | solution.py:293
  63.6 1.6 %down.3 = (f32[128,768]{1,0:T(8,128)S(1)}, f32[128,768]{1,0:T(8,128)S(1)}, f32[128,768]{1,0:T(8,128)S(1)}, f32[128,768]{1,0:T(8,128)S(1)}, f32[128,768]{1,0:T(8,...) custom-call(s32[1]{0:T(128)} %bitcast.me_ref, ...), custom_call_target="tpu_custom_call" | custom-call | flops 1207959552 | bytes 4325376 | tf_op jit(solution)/shard_map/down/pallas_call | solution.py:238
  65.7 1.6 %collective-permute-start.25 = (bf16[128,768]{1,0:T(8,128)(2,1)S(1)}, bf16[128,768]{1,0:T(8,128)(2,1)S(1)}, u32[]{:S(2)}, u32[]{:S(2)}) collective-permute-start(bf16[128,768]{1,0:T(8,128)(2,1)S(1)} %get-tuple-element.52), channel_id=1, source_target_pairs={{0,8},{8,16},{16,24},{24,28},{28,20},{20,12},{12,4},{4,0},{1,9},{9... | collective-permute-start | bytes 589832 | tf_op jit(solution)/shard_map/ppermute | solution.py:293
  67.2 2.0 %collective-permute-done.14 = bf16[128,768]{1,0:T(8,128)(2,1)S(1)} collective-permute-done((bf16[128,768]{1,0:T(8,128)(2,1)S(1)}, bf16[128,768]{1,0:T(8,128)(2,1)S(1)}, u32[]{:S(2)}, u32[]{:S(2)}) %collective-permute-start.14) | collective-permute-done | bytes 196640 | tf_op jit(solution)/shard_map/ppermute | solution.py:293
  69.3 1.7 %collective-permute-start.15 = (bf16[128,768]{1,0:T(8,128)(2,1)S(1)}, bf16[128,768]{1,0:T(8,128)(2,1)S(1)}, u32[]{:S(2)}, u32[]{:S(2)}) collective-permute-start(bf16[128,768]{1,0:T(8,128)(2,1)S(1)} %add_convert_fusion.11), channel_id=1, source_target_pairs={{0,8},{8,16},{16,24},{24,28},{28,20},{20,12},{12,4},{4,0},{1,9},{9... | collective-permute-start | bytes 589832 | tf_op jit(solution)/shard_map/ppermute | solution.py:293
  71.5 3.7 %collective-permute-done.21 = bf16[128,768]{1,0:T(8,128)(2,1)S(1)} collective-permute-done((bf16[128,768]{1,0:T(8,128)(2,1)S(1)}, bf16[128,768]{1,0:T(8,128)(2,1)S(1)}, u32[]{:S(2)}, u32[]{:S(2)}) %collective-permute-start.21) | collective-permute-done | bytes 196640 | tf_op jit(solution)/shard_map/ppermute | solution.py:296
  75.7 1.7 %collective-permute-start.26 = (bf16[128,768]{1,0:T(8,128)(2,1)S(1)}, bf16[128,768]{1,0:T(8,128)(2,1)S(1)}, u32[]{:S(2)}, u32[]{:S(2)}) collective-permute-start(bf16[128,768]{1,0:T(8,128)(2,1)S(1)} %add_convert_fusion.2), channel_id=1, source_target_pairs={{0,8},{8,16},{16,24},{24,28},{28,20},{20,12},{12,4},{4,0},{1,9},{9... | collective-permute-start | bytes 589832 | tf_op jit(solution)/shard_map/ppermute | solution.py:293
  77.7 1.7 %collective-permute-start.16 = (bf16[128,768]{1,0:T(8,128)(2,1)S(1)}, bf16[128,768]{1,0:T(8,128)(2,1)S(1)}, u32[]{:S(2)}, u32[]{:S(2)}) collective-permute-start(bf16[128,768]{1,0:T(8,128)(2,1)S(1)} %add_convert_fusion.10), channel_id=1, source_target_pairs={{0,8},{8,16},{16,24},{24,28},{28,20},{20,12},{12,4},{4,0},{1,9},{9... | collective-permute-start | bytes 589832 | tf_op jit(solution)/shard_map/ppermute | solution.py:293
  79.9 3.7 %collective-permute-done.22 = bf16[128,768]{1,0:T(8,128)(2,1)S(1)} collective-permute-done((bf16[128,768]{1,0:T(8,128)(2,1)S(1)}, bf16[128,768]{1,0:T(8,128)(2,1)S(1)}, u32[]{:S(2)}, u32[]{:S(2)}) %collective-permute-start.22) | collective-permute-done | bytes 196640 | tf_op jit(solution)/shard_map/ppermute | solution.py:296
  84.1 1.7 %collective-permute-start.27 = (bf16[128,768]{1,0:T(8,128)(2,1)S(1)}, bf16[128,768]{1,0:T(8,128)(2,1)S(1)}, u32[]{:S(2)}, u32[]{:S(2)}) collective-permute-start(bf16[128,768]{1,0:T(8,128)(2,1)S(1)} %add_convert_fusion.1), channel_id=1, source_target_pairs={{0,8},{8,16},{16,24},{24,28},{28,20},{20,12},{12,4},{4,0},{1,9},{9... | collective-permute-start | bytes 589832 | tf_op jit(solution)/shard_map/ppermute | solution.py:293
  86.3 1.8 %collective-permute-start.17 = (bf16[128,768]{1,0:T(8,128)(2,1)S(1)}, bf16[128,768]{1,0:T(8,128)(2,1)S(1)}, u32[]{:S(2)}, u32[]{:S(2)}) collective-permute-start(bf16[128,768]{1,0:T(8,128)(2,1)S(1)} %add_convert_fusion.9), channel_id=1, source_target_pairs={{0,8},{8,16},{16,24},{24,28},{28,20},{20,12},{12,4},{4,0},{1,9},{9... | collective-permute-start | bytes 589832 | tf_op jit(solution)/shard_map/ppermute | solution.py:293
  88.0 3.1 %collective-permute-done.23 = bf16[128,768]{1,0:T(8,128)(2,1)S(1)} collective-permute-done((bf16[128,768]{1,0:T(8,128)(2,1)S(1)}, bf16[128,768]{1,0:T(8,128)(2,1)S(1)}, u32[]{:S(2)}, u32[]{:S(2)}) %collective-permute-start.23) | collective-permute-done | bytes 196640 | tf_op jit(solution)/shard_map/ppermute | solution.py:296
  91.7 2.4 %collective-permute-done.17 = bf16[128,768]{1,0:T(8,128)(2,1)S(1)} collective-permute-done((bf16[128,768]{1,0:T(8,128)(2,1)S(1)}, bf16[128,768]{1,0:T(8,128)(2,1)S(1)}, u32[]{:S(2)}, u32[]{:S(2)}) %collective-permute-start.17) | collective-permute-done | bytes 196640 | tf_op jit(solution)/shard_map/ppermute | solution.py:293
  94.2 3.1 %collective-permute-done.24 = bf16[128,768]{1,0:T(8,128)(2,1)S(1)} collective-permute-done((bf16[128,768]{1,0:T(8,128)(2,1)S(1)}, bf16[128,768]{1,0:T(8,128)(2,1)S(1)}, u32[]{:S(2)}, u32[]{:S(2)}) %collective-permute-start.24) | collective-permute-done | bytes 196640 | tf_op jit(solution)/shard_map/ppermute | solution.py:296
  (81 shorter events, 8.6 us)
Async XLA Ops:
  2.9 13.0 %collective-permute-start = (bf16[128,1664]{1,0:T(8,128)(2,1)}, bf16[128,1664]{1,0:T(8,128)(2,1)S(1)}, u32[]{:S(2)}, u32[]{:S(2)}) collective-permute-start(bf16[128,1664]{1,0:T(8,128)(2,1)} %get-tuple-element.30.refs_0_), channel_id=1, source_target_pairs={{0,8},{8,16},{16,24},{24,28},{28,20},{20,12},{12,4},{4,0},{1,9},{9... | collective-permute-start | bytes 1277960 | tf_op jit(solution)/shard_map/ppermute | solution.py:293
  5.9 11.8 %collective-permute-start.1 = (bf16[128,1664]{1,0:T(8,128)(2,1)}, bf16[128,1664]{1,0:T(8,128)(2,1)S(1)}, u32[]{:S(2)}, u32[]{:S(2)}) collective-permute-start(bf16[128,1664]{1,0:T(8,128)(2,1)} %get-tuple-element.30.refs_0_), channel_id=1, source_target_pairs={{8,0},{16,8},{24,16},{28,24},{20,28},{12,20},{4,12},{0,4},{9,1},{1... | collective-permute-start | bytes 1277960 | tf_op jit(solution)/shard_map/ppermute | solution.py:296
  5.9 32.0 %collective-permute-start.5 = (bf16[768,768]{1,0:T(8,128)(2,1)}, bf16[768,768]{1,0:T(8,128)(2,1)S(1)}, u32[]{:S(2)}, u32[]{:S(2)}) collective-permute-start(bf16[768,768]{1,0:T(8,128)(2,1)} %get-tuple-element.31.refs_5_), channel_id=1, source_target_pairs={{0,2},{1,3},{2,0},{3,1},{4,6},{5,7},{6,4},{7,5},{8,10},{9,11},{10,... | collective-permute-start | bytes 3538952 | tf_op jit(solution)/shard_map/ppermute | solution.py:257
  15.9 13.0 %copy-start.8 = (bf16[128,1664]{1,0:T(8,128)(2,1)}, bf16[128,1664]{1,0:T(8,128)(2,1)S(1)}, u32[]{:S(2)}) copy-start(bf16[128,1664]{1,0:T(8,128)(2,1)S(1)} %collective-permute-done.refs_1_) | copy-start | bytes 1277956
  15.9 11.0 %collective-permute-start.2 = (bf16[128,1664]{1,0:T(8,128)(2,1)S(1)}, bf16[128,1664]{1,0:T(8,128)(2,1)S(1)}, u32[]{:S(2)}, u32[]{:S(2)}) collective-permute-start(bf16[128,1664]{1,0:T(8,128)(2,1)S(1)} %collective-permute-done.refs_1_), channel_id=1, source_target_pairs={{0,8},{8,16},{16,24},{24,28},{28,20},{20,12},{12,4},{4,0},{1,9},{9... | collective-permute-start | bytes 1277960 | tf_op jit(solution)/shard_map/ppermute | solution.py:293
  17.7 11.2 %copy-start.9 = (bf16[128,1664]{1,0:T(8,128)(2,1)}, bf16[128,1664]{1,0:T(8,128)(2,1)S(1)}, u32[]{:S(2)}) copy-start(bf16[128,1664]{1,0:T(8,128)(2,1)S(1)} %collective-permute-done.1.refs_2_) | copy-start | bytes 1277956
  17.7 10.7 %collective-permute-start.3 = (bf16[128,1664]{1,0:T(8,128)(2,1)S(1)}, bf16[128,1664]{1,0:T(8,128)(2,1)S(1)}, u32[]{:S(2)}, u32[]{:S(2)}) collective-permute-start(bf16[128,1664]{1,0:T(8,128)(2,1)S(1)} %collective-permute-done.1.refs_2_), channel_id=1, source_target_pairs={{8,0},{16,8},{24,16},{28,24},{20,28},{12,20},{4,12},{0,4},{9,1},{1... | collective-permute-start | bytes 1277960 | tf_op jit(solution)/shard_map/ppermute | solution.py:296
  26.9 10.1 %collective-permute-start.6 = (bf16[128,1664]{1,0:T(8,128)(2,1)S(1)}, bf16[128,1664]{1,0:T(8,128)(2,1)S(1)}, u32[]{:S(2)}, u32[]{:S(2)}) collective-permute-start(bf16[128,1664]{1,0:T(8,128)(2,1)S(1)} %collective-permute-done.2.refs_3_), channel_id=1, source_target_pairs={{0,8},{8,16},{16,24},{24,28},{28,20},{20,12},{12,4},{4,0},{1,9},{9... | collective-permute-start | bytes 1277960 | tf_op jit(solution)/shard_map/ppermute | solution.py:293
  28.4 9.5 %copy-start.11 = (bf16[128,1664]{1,0:T(8,128)(2,1)}, bf16[128,1664]{1,0:T(8,128)(2,1)S(1)}, u32[]{:S(2)}) copy-start(bf16[128,1664]{1,0:T(8,128)(2,1)S(1)} %collective-permute-done.3.refs_4_) | copy-start | bytes 1277956
  28.4 9.5 %collective-permute-start.7 = (bf16[128,1664]{1,0:T(8,128)(2,1)S(1)}, bf16[128,1664]{1,0:T(8,128)(2,1)S(1)}, u32[]{:S(2)}, u32[]{:S(2)}) collective-permute-start(bf16[128,1664]{1,0:T(8,128)(2,1)S(1)} %collective-permute-done.3.refs_4_), channel_id=1, source_target_pairs={{8,0},{16,8},{24,16},{28,24},{20,28},{12,20},{4,12},{0,4},{9,1},{1... | collective-permute-start | bytes 1277960 | tf_op jit(solution)/shard_map/ppermute | solution.py:296
  28.9 14.7 %collective-permute-start.4 = (bf16[768,768]{1,0:T(8,128)(2,1)}, bf16[768,768]{1,0:T(8,128)(2,1)}, u32[]{:S(2)}, u32[]{:S(2)}) collective-permute-start(bf16[768,768]{1,0:T(8,128)(2,1)} %get-tuple-element.31.refs_5_), channel_id=1, source_target_pairs={{0,1},{1,0},{2,3},{3,2},{4,5},{5,4},{6,7},{7,6},{8,9},{9,8},{10,11... | collective-permute-start | bytes 3538952 | tf_op jit(solution)/shard_map/ppermute | solution.py:257
  37.9 5.7 %collective-permute-start.8 = (bf16[768,768]{1,0:T(8,128)(2,1)S(1)}, bf16[768,768]{1,0:T(8,128)(2,1)}, u32[]{:S(2)}, u32[]{:S(2)}) collective-permute-start(bf16[768,768]{1,0:T(8,128)(2,1)S(1)} %after.4.refs_7_), channel_id=1, source_target_pairs={{0,1},{1,0},{2,3},{3,2},{4,5},{5,4},{6,7},{7,6},{8,9},{9,8},{10,11... | collective-permute-start | bytes 3538952 | tf_op jit(solution)/shard_map/ppermute | solution.py:257
  39.3 18.4 %collective-permute-start.12 = (bf16[192,1536]{1,0:T(8,128)(2,1)S(1)}, bf16[192,1536]{1,0:T(8,128)(2,1)S(1)}, u32[]{:S(2)}, u32[]{:S(2)}) collective-permute-start(bf16[192,1536]{1,0:T(8,128)(2,1)S(1)} %bitcast.8), channel_id=1, source_target_pairs={{0,2},{1,3},{2,0},{3,1},{4,6},{5,7},{6,4},{7,5},{8,10},{9,11},{10,... | collective-permute-start | bytes 1769480 | tf_op jit(solution)/shard_map/ppermute | solution.py:257
  40.8 11.4 %collective-permute-start.10 = (bf16[64,1664]{1,0:T(8,128)(2,1)S(1)}, bf16[64,1664]{1,0:T(8,128)(2,1)S(1)}, u32[]{:S(2)}, u32[]{:S(2)}) collective-permute-start(bf16[64,1664]{1,0:T(8,128)(2,1)S(1)} %slice.28), channel_id=1, source_target_pairs={{8,0},{16,8},{24,16},{28,24},{20,28},{12,20},{4,12},{0,4},{9,1},{1... | collective-permute-start | bytes 638984 | tf_op jit(solution)/shard_map/ppermute | solution.py:296
  41.4 10.9 %collective-permute-start.9 = (bf16[64,1664]{1,0:T(8,128)(2,1)S(1)}, bf16[64,1664]{1,0:T(8,128)(2,1)S(1)}, u32[]{:S(2)}, u32[]{:S(2)}) collective-permute-start(bf16[64,1664]{1,0:T(8,128)(2,1)S(1)} %slice.27), channel_id=1, source_target_pairs={{0,8},{8,16},{16,24},{24,28},{28,20},{20,12},{12,4},{4,0},{1,9},{9... | collective-permute-start | bytes 638984 | tf_op jit(solution)/shard_map/ppermute | solution.py:293
  43.6 14.7 %collective-permute-start.11 = (bf16[192,1536]{1,0:T(8,128)(2,1)S(1)}, bf16[192,1536]{1,0:T(8,128)(2,1)S(1)}, u32[]{:S(2)}, u32[]{:S(2)}) collective-permute-start(bf16[192,1536]{1,0:T(8,128)(2,1)S(1)} %bitcast.9), channel_id=1, source_target_pairs={{0,1},{1,0},{2,3},{3,2},{4,5},{5,4},{6,7},{7,6},{8,9},{9,8},{10,11... | collective-permute-start | bytes 1769480 | tf_op jit(solution)/shard_map/ppermute | solution.py:257
  43.6 8.6 %copy-start.3 = (f32[1,128]{1,0:T(1,128)S(1)}, f32[1,128]{1,0:T(1,128)}, u32[]{:S(2)}) copy-start(f32[1,128]{1,0:T(1,128)} %fusion.own_ref) | copy-start | bytes 1540
  57.7 2.2 %collective-permute-start.13 = (bf16[192,1536]{1,0:T(8,128)(2,1)S(1)}, bf16[192,1536]{1,0:T(8,128)(2,1)S(1)}, u32[]{:S(2)}, u32[]{:S(2)}) collective-permute-start(bf16[192,1536]{1,0:T(8,128)(2,1)S(1)} %after.7.refs_7_), channel_id=1, source_target_pairs={{0,1},{1,0},{2,3},{3,2},{4,5},{5,4},{6,7},{7,6},{8,9},{9,8},{10,11... | collective-permute-start | bytes 1769480 | tf_op jit(solution)/shard_map/ppermute | solution.py:257
  61.5 7.8 %collective-permute-start.14 = (bf16[128,768]{1,0:T(8,128)(2,1)S(1)}, bf16[128,768]{1,0:T(8,128)(2,1)S(1)}, u32[]{:S(2)}, u32[]{:S(2)}) collective-permute-start(bf16[128,768]{1,0:T(8,128)(2,1)S(1)} %get-tuple-element.40), channel_id=1, source_target_pairs={{0,8},{8,16},{16,24},{24,28},{28,20},{20,12},{12,4},{4,0},{1,9},{9... | collective-permute-start | bytes 589832 | tf_op jit(solution)/shard_map/ppermute | solution.py:293
  63.2 7.8 %collective-permute-start.18 = (bf16[128,768]{1,0:T(8,128)(2,1)S(1)}, bf16[128,768]{1,0:T(8,128)(2,1)S(1)}, u32[]{:S(2)}, u32[]{:S(2)}) collective-permute-start(bf16[128,768]{1,0:T(8,128)(2,1)S(1)} %get-tuple-element.44), channel_id=1, source_target_pairs={{8,0},{16,8},{24,16},{28,24},{20,28},{12,20},{4,12},{0,4},{9,1},{1... | collective-permute-start | bytes 589832 | tf_op jit(solution)/shard_map/ppermute | solution.py:296
  65.2 10.0 %collective-permute-start.21 = (bf16[128,768]{1,0:T(8,128)(2,1)S(1)}, bf16[128,768]{1,0:T(8,128)(2,1)S(1)}, u32[]{:S(2)}, u32[]{:S(2)}) collective-permute-start(bf16[128,768]{1,0:T(8,128)(2,1)S(1)} %get-tuple-element.48), channel_id=1, source_target_pairs={{8,0},{16,8},{24,16},{28,24},{20,28},{12,20},{4,12},{0,4},{9,1},{1... | collective-permute-start | bytes 589832 | tf_op jit(solution)/shard_map/ppermute | solution.py:296
  65.7 10.0 %collective-permute-start.25 = (bf16[128,768]{1,0:T(8,128)(2,1)S(1)}, bf16[128,768]{1,0:T(8,128)(2,1)S(1)}, u32[]{:S(2)}, u32[]{:S(2)}) collective-permute-start(bf16[128,768]{1,0:T(8,128)(2,1)S(1)} %get-tuple-element.52), channel_id=1, source_target_pairs={{0,8},{8,16},{16,24},{24,28},{28,20},{20,12},{12,4},{4,0},{1,9},{9... | collective-permute-start | bytes 589832 | tf_op jit(solution)/shard_map/ppermute | solution.py:293
  69.3 8.4 %collective-permute-start.15 = (bf16[128,768]{1,0:T(8,128)(2,1)S(1)}, bf16[128,768]{1,0:T(8,128)(2,1)S(1)}, u32[]{:S(2)}, u32[]{:S(2)}) collective-permute-start(bf16[128,768]{1,0:T(8,128)(2,1)S(1)} %add_convert_fusion.11), channel_id=1, source_target_pairs={{0,8},{8,16},{16,24},{24,28},{28,20},{20,12},{12,4},{4,0},{1,9},{9... | collective-permute-start | bytes 589832 | tf_op jit(solution)/shard_map/ppermute | solution.py:293
  71.0 8.4 %collective-permute-start.19 = (bf16[128,768]{1,0:T(8,128)(2,1)S(1)}, bf16[128,768]{1,0:T(8,128)(2,1)S(1)}, u32[]{:S(2)}, u32[]{:S(2)}) collective-permute-start(bf16[128,768]{1,0:T(8,128)(2,1)S(1)} %add_convert_fusion.8), channel_id=1, source_target_pairs={{8,0},{16,8},{24,16},{28,24},{20,28},{12,20},{4,12},{0,4},{9,1},{1... | collective-permute-start | bytes 589832 | tf_op jit(solution)/shard_map/ppermute | solution.py:296
  75.2 8.4 %collective-permute-start.22 = (bf16[128,768]{1,0:T(8,128)(2,1)S(1)}, bf16[128,768]{1,0:T(8,128)(2,1)S(1)}, u32[]{:S(2)}, u32[]{:S(2)}) collective-permute-start(bf16[128,768]{1,0:T(8,128)(2,1)S(1)} %add_convert_fusion.5), channel_id=1, source_target_pairs={{8,0},{16,8},{24,16},{28,24},{20,28},{12,20},{4,12},{0,4},{9,1},{1... | collective-permute-start | bytes 589832 | tf_op jit(solution)/shard_map/ppermute | solution.py:296
  75.7 8.4 %collective-permute-start.26 = (bf16[128,768]{1,0:T(8,128)(2,1)S(1)}, bf16[128,768]{1,0:T(8,128)(2,1)S(1)}, u32[]{:S(2)}, u32[]{:S(2)}) collective-permute-start(bf16[128,768]{1,0:T(8,128)(2,1)S(1)} %add_convert_fusion.2), channel_id=1, source_target_pairs={{0,8},{8,16},{16,24},{24,28},{28,20},{20,12},{12,4},{4,0},{1,9},{9... | collective-permute-start | bytes 589832 | tf_op jit(solution)/shard_map/ppermute | solution.py:293
  77.7 8.5 %collective-permute-start.16 = (bf16[128,768]{1,0:T(8,128)(2,1)S(1)}, bf16[128,768]{1,0:T(8,128)(2,1)S(1)}, u32[]{:S(2)}, u32[]{:S(2)}) collective-permute-start(bf16[128,768]{1,0:T(8,128)(2,1)S(1)} %add_convert_fusion.10), channel_id=1, source_target_pairs={{0,8},{8,16},{16,24},{24,28},{28,20},{20,12},{12,4},{4,0},{1,9},{9... | collective-permute-start | bytes 589832 | tf_op jit(solution)/shard_map/ppermute | solution.py:293
  79.5 12.2 %collective-permute-start.20 = (bf16[128,768]{1,0:T(8,128)(2,1)S(1)}, bf16[128,768]{1,0:T(8,128)(2,1)S(1)}, u32[]{:S(2)}, u32[]{:S(2)}) collective-permute-start(bf16[128,768]{1,0:T(8,128)(2,1)S(1)} %add_convert_fusion.7), channel_id=1, source_target_pairs={{8,0},{16,8},{24,16},{28,24},{20,28},{12,20},{4,12},{0,4},{9,1},{1... | collective-permute-start | bytes 589832 | tf_op jit(solution)/shard_map/ppermute | solution.py:296
  83.6 7.5 %collective-permute-start.23 = (bf16[128,768]{1,0:T(8,128)(2,1)S(1)}, bf16[128,768]{1,0:T(8,128)(2,1)S(1)}, u32[]{:S(2)}, u32[]{:S(2)}) collective-permute-start(bf16[128,768]{1,0:T(8,128)(2,1)S(1)} %add_convert_fusion.4), channel_id=1, source_target_pairs={{8,0},{16,8},{24,16},{28,24},{20,28},{12,20},{4,12},{0,4},{9,1},{1... | collective-permute-start | bytes 589832 | tf_op jit(solution)/shard_map/ppermute | solution.py:296
  84.1 10.0 %collective-permute-start.27 = (bf16[128,768]{1,0:T(8,128)(2,1)S(1)}, bf16[128,768]{1,0:T(8,128)(2,1)S(1)}, u32[]{:S(2)}, u32[]{:S(2)}) collective-permute-start(bf16[128,768]{1,0:T(8,128)(2,1)S(1)} %add_convert_fusion.1), channel_id=1, source_target_pairs={{0,8},{8,16},{16,24},{24,28},{28,20},{20,12},{12,4},{4,0},{1,9},{9... | collective-permute-start | bytes 589832 | tf_op jit(solution)/shard_map/ppermute | solution.py:293
  86.3 7.8 %collective-permute-start.17 = (bf16[128,768]{1,0:T(8,128)(2,1)S(1)}, bf16[128,768]{1,0:T(8,128)(2,1)S(1)}, u32[]{:S(2)}, u32[]{:S(2)}) collective-permute-start(bf16[128,768]{1,0:T(8,128)(2,1)S(1)} %add_convert_fusion.9), channel_id=1, source_target_pairs={{0,8},{8,16},{16,24},{24,28},{28,20},{20,12},{12,4},{4,0},{1,9},{9... | collective-permute-start | bytes 589832 | tf_op jit(solution)/shard_map/ppermute | solution.py:293
  91.2 6.1 %collective-permute-start.24 = (bf16[128,768]{1,0:T(8,128)(2,1)S(1)}, bf16[128,768]{1,0:T(8,128)(2,1)S(1)}, u32[]{:S(2)}, u32[]{:S(2)}) collective-permute-start(bf16[128,768]{1,0:T(8,128)(2,1)S(1)} %add_convert_fusion.3), channel_id=1, source_target_pairs={{8,0},{16,8},{24,16},{28,24},{20,28},{12,20},{4,12},{0,4},{9,1},{1... | collective-permute-start | bytes 589832 | tf_op jit(solution)/shard_map/ppermute | solution.py:296
  (9 other events, 22.1 us)

commit v3 on v2

--- a/solution.py
+++ b/solution.py
@@ -9,7 +9,7 @@
 
 VMEM_LIMIT = 28 * 1024 * 1024
 MOST_VMEM = 60 * 1024 * 1024
-MUCH_VMEM = 54 * 1024 * 1024
+MUCH_VMEM = 52 * 1024 * 1024
 EXTRA = 128
 WHOLE = pl.BlockSpec(memory_space=pltpu.VMEM)
 SCALAR = pl.BlockSpec(memory_space=pltpu.SMEM)
@@ -37,20 +37,22 @@
     return order
 
 
-def after_kernel(*refs):
-    pass
-
-
-def after(place, value, *others):
+def after_kernel(count, value_ref, *refs):
+    outs = refs[len(refs) - count :]
+    rows = outs[0].shape[0]
+    for at, out in enumerate(outs):
+        out[...] = value_ref[at * rows : (at + 1) * rows, :]
+
+
+def after(value, count, *others):
     marks = [other[:8, :128] for other in others]
+    part = jax.ShapeDtypeStruct((value.shape[0] // count, value.shape[1]), value.dtype)
     return pl.pallas_call(
-        after_kernel,
-        out_shape=jax.ShapeDtypeStruct(value.shape, value.dtype),
-        in_specs=[place] + [WHOLE] * len(marks),
-        out_specs=place,
-        input_output_aliases={0: 0},
+        functools.partial(after_kernel, count),
+        out_shape=(part,) * count,
+        in_specs=[WHOLE] * (1 + len(marks)),
+        out_specs=(WHOLE,) * count,
         compiler_params=params(),
-        cost_estimate=cost(0, 4096),
         name="after",
     )(value, *marks)
 
@@ -118,108 +120,117 @@
     )(*small, gate, upper)
 
 
-def fetch(me, refs, first, columns, target, sems):
-    depth = target.shape[0] // len(refs)
-    copies = []
-    for apart, ref in enumerate(refs):
+def assemble(me, pieces, first, columns, target):
+    depth = target.shape[0] // len(pieces)
+    for apart, parts in enumerate(pieces):
         at = pl.multiple_of((me ^ apart) * depth, depth)
-        source = ref.at[pl.ds(first, depth), columns]
-        copy = pltpu.make_async_copy(source, target.at[pl.ds(at, depth), :], sems.at[apart])
-        copy.start()
-        copies.append(copy)
-    return copies
-
-
-def hidden_rows(rows, own_ref, gate_mat, upper_mat, ready=()):
-    width = gate_mat.shape[0]
-    scale = jnp.sum(rows[:, width:].astype(jnp.float32) * own_ref[...], axis=1, keepdims=True)
-    gate = jnp.dot(rows[:, :width], gate_mat[...], preferred_element_type=jnp.float32)
-    for copy in ready:
-        copy.wait()
-    upper = jnp.dot(rows[:, :width], upper_mat[...], preferred_element_type=jnp.float32)
-    hidden = jnp.where(scale > 0, jnp.maximum(gate, 0.0) * upper * scale, 0.0)
-    return hidden.astype(jnp.bfloat16)
-
-
-def first_hidden_kernel(inputs, pieces, me_ref, own_ref, *refs):
-    blocks, weights = refs[:inputs], refs[inputs : inputs + pieces]
-    outs, scratch = refs[inputs + pieces : -4], refs[-4:]
-    outs, (gate_mat, upper_mat) = outs[:-2], outs[-2:]
-    rows_ref, gate_sems, upper_sems, row_sems = scratch
-    width, units = gate_mat.shape
-    columns = pl.ds(0, units)
-    row_copies, at = [], 0
+        begin = 0
+        for part in parts:
+            end = begin + part.shape[0]
+            low, high = max(begin, first), min(end, first + depth)
+            if low < high:
+                place = pl.ds(pl.multiple_of(at + (low - first), 16), high - low)
+                target[place, :] = part[low - begin : high - begin, columns]
+            begin = end
+
+
+def take_pieces(layout, refs):
+    pieces, at = [], 0
+    for count in layout:
+        pieces.append(refs[at : at + count])
+        at += count
+    return pieces, refs[at:]
+
+
+def stacked(pieces, first, depth):
+    found = []
+    for parts in pieces:
+        begin = 0
+        for part in parts:
+            end = begin + part.shape[0]
+            low, high = max(begin, first), min(end, first + depth)
+            if low < high:
+                found.append(part[low - begin : high - begin, :])
+            begin = end
+    return jnp.concatenate(found, axis=0)
+
+
+def hidden_kernel(inputs, layout, me_ref, place_ref, *refs):
+    blocks, refs = refs[:inputs], refs[inputs:]
+    pieces, refs = take_pieces(layout, refs)
+    outs, (rows_ref, gate_mat, upper_mat, sems) = refs[:-4], refs[-4:]
+    width = rows_ref.shape[1] - EXTRA
+    depth = width // len(pieces)
+    in_place = depth % 128 == 0
+    copies, at = [], 0
     for place, block in enumerate(blocks):
         target = rows_ref.at[at : at + block.shape[0], :]
-        row_copies.append(pltpu.make_async_copy(block, target, row_sems.at[place]))
+        copies.append(pltpu.make_async_copy(block, target, sems.at[place]))
+        copies[-1].start()
         at += block.shape[0]
-    for copy in row_copies:
-        copy.start()
-    gate_copies = fetch(me_ref[0], weights, 0, columns, gate_mat, gate_sems)
-    upper_copies = fetch(me_ref[0], weights, width // pieces, columns, upper_mat, upper_sems)
-    for copy in row_copies + gate_copies:
-        copy.wait()
-    at = 0
+    if not in_place:
+        columns = slice(0, gate_mat.shape[1])
+        assemble(me_ref[0], pieces, 0, columns, gate_mat)
+        assemble(me_ref[0], pieces, depth, columns, upper_mat)
+    lanes = lax.broadcasted_iota(jnp.int32, (1, EXTRA), 1)
+    own = jnp.zeros((1, EXTRA), jnp.float32)
+    experts = place_ref.shape[0]
+    for expert in range(experts):
+        mine = ((lanes == expert) | (lanes == expert + experts)) & (place_ref[expert] == me_ref[1])
+        own = jnp.where(mine, 1.0, own)
+    at, done, fetched = 0, 0, 0
     for out in outs:
-        rows = rows_ref[at : at + out.shape[0], :]
-        ready = () if at else upper_copies
-        out[...] = hidden_rows(rows, own_ref, gate_mat, upper_mat, ready)
+        here = slice(at, at + out.shape[0])
         at += out.shape[0]
-
-
-def first_hidden_blocks(me, own, groups, pairs):
-    pieces = len(pairs)
-    width, units = pairs[0].shape[0] // 2 * pieces, pairs[0].shape[1]
+        while fetched < at:
+            copies[done].wait()
+            fetched += blocks[done].shape[0]
+            done += 1
+        weights = rows_ref[here, width:].astype(jnp.float32)
+        scale = jnp.sum(weights * own, axis=1, keepdims=True)
+        if in_place:
+            rows = [
+                rows_ref[here, pl.ds(pl.multiple_of((me_ref[0] ^ apart) * depth, depth), depth)]
+                for apart in range(len(pieces))
+            ]
+            rows = jnp.concatenate(rows, axis=1)
+            first, second = stacked(pieces, 0, depth), stacked(pieces, depth, depth)
+        else:
+            rows, first, second = rows_ref[here, :width], gate_mat[...], upper_mat[...]
+        gate = jnp.dot(rows, first, preferred_element_type=jnp.float32)
+        upper = jnp.dot(rows, second, preferred_element_type=jnp.float32)
+        hidden = jnp.where(scale > 0, jnp.maximum(gate, 0.0) * upper * scale, 0.0)
+        out[...] = hidden.astype(jnp.bfloat16)
+
+
+def hidden_blocks(me, placement, groups, pairs):
+    layout = [len(parts) for parts in pairs]
+    flat = [part for parts in pairs for part in parts]
+    width, units = sum(part.shape[0] for part in flat) // 2, flat[0].shape[1]
     heights = [sum(block.shape[0] for block in group) for group in groups]
     blocks = [block for group in groups for block in group]
-    shapes = [(height, units) for height in heights] + [(width, units)] * 2
+    whole = (width, units) if width // len(pairs) % 128 else (16, 128)
     return pl.pallas_call(
-        functools.partial(first_hidden_kernel, len(blocks), pieces),
-        out_shape=tuple(jax.ShapeDtypeStruct(shape, jnp.bfloat16) for shape in shapes),
-        in_specs=[SCALAR, WHOLE] + [ANYWHERE] * (len(blocks) + pieces),
-        out_specs=tuple(WHOLE for _ in shapes),
+        functools.partial(hidden_kernel, len(blocks), layout),
+        out_shape=tuple(jax.ShapeDtypeStruct((h, units), jnp.bfloat16) for h in heights),
+        in_specs=[SCALAR, SCALAR] + [ANYWHERE] * len(blocks) + [WHOLE] * len(flat),
+        out_specs=tuple(WHOLE for _ in groups),
         scratch_shapes=[
             pltpu.VMEM((sum(heights), width + EXTRA), jnp.bfloat16),
-            pltpu.SemaphoreType.DMA((pieces,)),
-            pltpu.SemaphoreType.DMA((pieces,)),
+            pltpu.VMEM(whole, jnp.bfloat16),
+            pltpu.VMEM(whole, jnp.bfloat16),
             pltpu.SemaphoreType.DMA((len(blocks),)),
         ],
         compiler_params=params(MUCH_VMEM),
-        name="first_hidden",
-    )(me, own, *blocks, *pairs)
-
-
-def hidden_kernel(counts, own_ref, gate_mat, upper_mat, *refs):
-    outs, at = refs[sum(counts) :], 0
-    for count, out in zip(counts, outs):
-        group = [block[...] for block in refs[at : at + count]]
-        at += count
-        rows = jnp.concatenate(group, axis=0) if count > 1 else group[0]
-        out[...] = hidden_rows(rows, own_ref, gate_mat, upper_mat)
-
-
-def hidden_blocks(own, groups, gate_mat, upper_mat):
-    width, units = gate_mat.shape
-    heights = [sum(block.shape[0] for block in group) for group in groups]
-    blocks = [block for group in groups for block in group]
-    return pl.pallas_call(
-        functools.partial(hidden_kernel, [len(group) for group in groups]),
-        out_shape=tuple(jax.ShapeDtypeStruct((h, units), jnp.bfloat16) for h in heights),
-        in_specs=[WHOLE] * (3 + len(blocks)),
-        out_specs=tuple(WHOLE for _ in groups),
-        compiler_params=params(),
         name="hidden",
-    )(own, gate_mat, upper_mat, *blocks)
-
-
-def down_kernel(slots, pieces, column, me_ref, *refs):
-    inputs = len(slots)
-    hidden = refs[:inputs]
-    outs = refs[inputs + pieces : -2]
-    down_mat, sems = refs[-2:]
-    columns = pl.ds(column, down_mat.shape[1])
-    for copy in fetch(me_ref[0], refs[inputs : inputs + pieces], 0, columns, down_mat, sems):
-        copy.wait()
+    )(me, placement, *blocks, *flat)
+
+
+def down_kernel(slots, layout, column, me_ref, *refs):
+    hidden, refs = refs[: len(slots)], refs[len(slots) :]
+    pieces, refs = take_pieces(layout, refs)
+    outs, down_mat = refs[:-1], refs[-1]
+    assemble(me_ref[0], pieces, 0, slice(column, column + down_mat.shape[1]), down_mat)
     for group, parts in zip(hidden, slots):
         out = jnp.dot(group[...], down_mat[...], preferred_element_type=jnp.float32)
         at = 0
@@ -230,26 +241,22 @@
 
 
 def down_blocks(me, column, width, hidden, slots, kinds, downs):
-    pieces = len(downs)
-    units = downs[0].shape[0] * pieces
+    layout = [len(parts) for parts in downs]
+    pieces = [part for parts in downs for part in parts]
+    units = sum(part.shape[0] for part in pieces)
     flat = [part for parts in slots for part in parts]
     heights = [sum(c for slot, _, c in flat if slot == at) for at in range(len(kinds))]
-    rows = sum(heights)
     return pl.pallas_call(
-        functools.partial(down_kernel, slots, pieces, column),
+        functools.partial(down_kernel, slots, layout, column),
         out_shape=tuple(
             jax.ShapeDtypeStruct((height, width), kind) for height, kind in zip(heights, kinds)
         ),
-        in_specs=[SCALAR] + [WHOLE] * len(hidden) + [ANYWHERE] * pieces,
+        in_specs=[SCALAR] + [WHOLE] * (len(hidden) + len(pieces)),
         out_specs=tuple(WHOLE for _ in kinds),
-        scratch_shapes=[
-            pltpu.VMEM((units, width), jnp.bfloat16),
-            pltpu.SemaphoreType.DMA((pieces,)),
-        ],
+        scratch_shapes=[pltpu.VMEM((units, width), jnp.bfloat16)],
         compiler_params=params(),
-        cost_estimate=cost(2 * rows * width * units, 2 * width * units + 4 * rows * width),
         name="down",
-    )(me, *hidden, *downs)
+    )(me, *hidden, *pieces)
 
 
 def swap_blk(value, bit):
@@ -266,9 +273,9 @@
     return have
 
 
-def last_round(have, *others):
-    have = {k: after(ANYWHERE, value, *others) if k else value for k, value in have.items()}
-    have.update({k ^ 1: swap_blk(value, 1) for k, value in list(have.items())})
+def last_round(have, count, *others):
+    have = {k: after(v, count, *others) if k else [v] for k, v in have.items()}
+    have.update({k ^ 1: [swap_blk(part, 1) for part in parts] for k, parts in list(have.items())})
     return [have[k] for k in sorted(have)]
 
 
@@ -295,26 +302,23 @@
     def counter(x):
         return lax.ppermute(x, "ep", behind)
 
-    me = lax.axis_index("blk").astype(jnp.int32).reshape(1)
-    experts = router_weight.shape[1]
-    held = (placement == lax.axis_index("ep")).astype(jnp.float32)
-    own = jnp.pad(jnp.concatenate([held, held]), (0, EXTRA - 2 * experts))[None, :]
-
+    me = jnp.stack([lax.axis_index("blk"), lax.axis_index("ep")]).astype(jnp.int32)
+
+    downs = outer_rounds(down_weight[0])
     packed, pair = pack(
         norm_gain, router_weight.T, routes.T, tokens, gate_weight[0], up_weight[0]
     )
     pairs = outer_rounds(pair)
     half = width // 2
-    downs = outer_rounds(down_weight[0])
 
     cut = tok_rows // 2
     from_behind, from_ahead = [packed], [packed]
     for step in range(1, far):
+        from_ahead.append(counter(from_ahead[-1]))
         from_behind.append(clock(from_behind[-1]))
-        from_ahead.append(counter(from_ahead[-1]))
     far_parts = [clock(from_behind[-1][:cut]), counter(from_ahead[-1][cut:])]
 
-    pairs = last_round(pairs, from_behind[far - 1], from_ahead[far - 1])
+    pairs = last_round(pairs, 4, from_behind[far - 1], from_ahead[far - 1])
 
     groups = [[((0, 0), 0, packed)]]
     for step in range(1, far):
@@ -323,14 +327,10 @@
     def only_blocks(chosen):
         return [[block for _, _, block in group] for group in chosen]
 
-    *hidden, gate_mat, upper_mat = first_hidden_blocks(me, own, only_blocks(groups[:3]), pairs)
-    first_done = hidden[-1]
-    for low in range(3, len(groups), 2):
-        blocks = only_blocks(groups[low : low + 2])
-        blocks[-1] = [after(WHOLE, block, first_done) for block in blocks[-1]]
-        hidden += hidden_blocks(own, blocks, gate_mat, upper_mat)
-
-    downs = last_round(downs, hidden[-1])
+    hidden = []
+    for low in range(0, len(groups), 5):
+        hidden += hidden_blocks(me, placement, only_blocks(groups[low : low + 5]), pairs)
+    downs = last_round(downs, 1, hidden[-1])
     results = []
     for side in range(2):
         long_way, short_way = (clock, counter) if side == 0 else (counter, clock)

time: 98.4 us -> 96.3 us (0.979)
  local copies, waits for them, and re-layouts: 5.37 us -> 0.09 us
  waiting for transfers between devices: 46.3 us -> 48.6 us
    unnamed x26, local copies, waits for them, and re-layouts: 4.64 us -> 0.06 us
    ppermute x6 -> x9, waiting for transfers between devices: 1.64 us -> 3 us  [swap_blk(): return lax.ppermute(value, 'blk', pairs)]
    pallas_call x8 -> x5, Pallas kernels: 13.1 us -> 14 us  [the longest x1 9.77 us: hidden_blocks(): pl.pallas_call(functools.partial(hidden_kernel, len(blocks), layout), out...]
    ppermute x6 -> x9, starting transfers between devices: 4.12 us -> 4.68 us  [swap_blk(): return lax.ppermute(value, 'blk', pairs)]
  transfers between devices with their start and end apart: 28 -> 31, of which waited for: 13 -> 16; matrix products, arithmetic and copies ran while one was open for 2% -> 1% of each run, Pallas kernels for 12% -> 12%
where the time goes in v3:
time: 96.3 us; the launch traced here: 96.1 us
  waiting for transfers between devices  48.6 us (50%)
  starting transfers between devices  29 us (30%)
  Pallas kernels  16.8 us (17%)
  other arithmetic  1.34 us (1%)
    ppermute x11, waiting for transfers between devices, clock(): return lax.ppermute(x, 'ep', ahead)  30.8 us
    ppermute x11, starting transfers between devices, clock(): return lax.ppermute(x, 'ep', ahead)  19.1 us
    ppermute x11, waiting for transfers between devices, counter(): return lax.ppermute(x, 'ep', behind)  14.8 us
    pallas_call x1, Pallas kernels, hidden_blocks(): pl.pallas_call(functools.partial(hidden_kernel, len(blocks), layout), out...  9.77 us
    ppermute x11, starting transfers between devices, counter(): return lax.ppermute(x, 'ep', behind)  5.21 us
    ppermute x9, starting transfers between devices, swap_blk(): return lax.ppermute(value, 'blk', pairs)  4.68 us
    pallas_call x2, Pallas kernels, down_blocks(): pl.pallas_call(functools.partial(down_kernel, slots, layout, column), out...  4.09 us
    ppermute x9, waiting for transfers between devices, swap_blk(): return lax.ppermute(value, 'blk', pairs)  3 us
  transfers between devices with their start and end apart: 31, of which 16 were waited for; matrix products, arithmetic and copies ran while one was open for 1% of the time, Pallas kernels for 12%

profile of v3, /device:TPU:0, one launch (start us, length us, event | category | flops | bytes accessed | tf_op | source)
XLA Modules:
  0.0 96.1 jit_solution(1130844308665587438)
XLA Ops:
  0.0 2.9 %pack.1 = (bf16[128,1664]{1,0:T(8,128)(2,1)}, bf16[768,768]{1,0:T(8,128)(2,1)}) custom-call(bf16[1536]{0:T(1024)(128)(2,1)} %refs_0_.1, bf16[8,1536]{1,0:T(8,128)(2,1)} %bitcast.13, s32[4,128]{1,0:T(4,128)} %bitcast.14, bf16[128,1536]{1,0:T(8,128)(2,1)} %refs_3_.1, bf16[384,768]{1,0:T(8,128)(2,1)} %bitcast.11, bf16[384,768]{1,0:T(8,128)(2,1)} %bitcast.12), custom_call_target="tpu_custom_call" | custom-call | flops 3145728 | bytes 3145728 | tf_op jit(solution)/shard_map/pack/pallas_call | solution.py:107
  2.9 3.1 %collective-permute-start = (bf16[128,1664]{1,0:T(8,128)(2,1)}, bf16[128,1664]{1,0:T(8,128)(2,1)S(1)}, u32[]{:S(2)}, u32[]{:S(2)}) collective-permute-start(bf16[128,1664]{1,0:T(8,128)(2,1)} %get-tuple-element.32.refs_0_), channel_id=1, source_target_pairs={{0,8},{8,16},{16,24},{24,28},{28,20},{20,12},{12,4},{4,0},{1,9},{9... | collective-permute-start | bytes 1277960 | tf_op jit(solution)/shard_map/ppermute | solution.py:300
  6.0 2.0 %collective-permute-start.9 = (bf16[768,768]{1,0:T(8,128)(2,1)}, bf16[768,768]{1,0:T(8,128)(2,1)S(1)}, u32[]{:S(2)}, u32[]{:S(2)}) collective-permute-start(bf16[768,768]{1,0:T(8,128)(2,1)} %get-tuple-element.33.refs_9_), channel_id=1, source_target_pairs={{0,2},{1,3},{2,0},{3,1},{4,6},{5,7},{6,4},{7,5},{8,10},{9,11},{10,... | collective-permute-start | bytes 3538952 | tf_op jit(solution)/shard_map/ppermute | solution.py:264
  7.9 8.0 %collective-permute-done.refs_1_ = bf16[128,1664]{1,0:T(8,128)(2,1)S(1)} collective-permute-done((bf16[128,1664]{1,0:T(8,128)(2,1)}, bf16[128,1664]{1,0:T(8,128)(2,1)S(1)}, u32[]{:S(2)}, u32[]{:S(2)}) %collective-permute-start) | collective-permute-done | bytes 426016 | tf_op jit(solution)/shard_map/ppermute | solution.py:300
  15.9 1.8 %collective-permute-start.2 = (bf16[128,1664]{1,0:T(8,128)(2,1)S(1)}, bf16[128,1664]{1,0:T(8,128)(2,1)S(1)}, u32[]{:S(2)}, u32[]{:S(2)}) collective-permute-start(bf16[128,1664]{1,0:T(8,128)(2,1)S(1)} %collective-permute-done.refs_1_), channel_id=1, source_target_pairs={{0,8},{8,16},{16,24},{24,28},{28,20},{20,12},{12,4},{4,0},{1,9},{9... | collective-permute-start | bytes 1277960 | tf_op jit(solution)/shard_map/ppermute | solution.py:300
  17.9 9.0 %collective-permute-done.2.refs_3_ = bf16[128,1664]{1,0:T(8,128)(2,1)S(1)} collective-permute-done((bf16[128,1664]{1,0:T(8,128)(2,1)S(1)}, bf16[128,1664]{1,0:T(8,128)(2,1)S(1)}, u32[]{:S(2)}, u32[]{:S(2)}) %collective-permute-start.2) | collective-permute-done | bytes 426016 | tf_op jit(solution)/shard_map/ppermute | solution.py:300
  26.9 1.5 %collective-permute-start.4 = (bf16[128,1664]{1,0:T(8,128)(2,1)S(1)}, bf16[128,1664]{1,0:T(8,128)(2,1)S(1)}, u32[]{:S(2)}, u32[]{:S(2)}) collective-permute-start(bf16[128,1664]{1,0:T(8,128)(2,1)S(1)} %collective-permute-done.2.refs_3_), channel_id=1, source_target_pairs={{0,8},{8,16},{16,24},{24,28},{28,20},{20,12},{12,4},{4,0},{1,9},{9... | collective-permute-start | bytes 1277960 | tf_op jit(solution)/shard_map/ppermute | solution.py:300
  29.0 1.5 %collective-permute-start.15 = (bf16[192,1536]{1,0:T(8,128)(2,1)S(1)}, bf16[192,1536]{1,0:T(8,128)(2,1)S(1)}, u32[]{:S(2)}, u32[]{:S(2)}) collective-permute-start(bf16[192,1536]{1,0:T(8,128)(2,1)S(1)} %bitcast.7), channel_id=1, source_target_pairs={{0,2},{1,3},{2,0},{3,1},{4,6},{5,7},{6,4},{7,5},{8,10},{9,11},{10,... | collective-permute-start | bytes 1769480 | tf_op jit(solution)/shard_map/ppermute | solution.py:264
  30.5 6.5 %collective-permute-done.4.refs_5_ = bf16[128,1664]{1,0:T(8,128)(2,1)S(1)} collective-permute-done((bf16[128,1664]{1,0:T(8,128)(2,1)S(1)}, bf16[128,1664]{1,0:T(8,128)(2,1)S(1)}, u32[]{:S(2)}, u32[]{:S(2)}) %collective-permute-start.4) | collective-permute-done | bytes 426016 | tf_op jit(solution)/shard_map/ppermute | solution.py:300
  37.0 1.4 %collective-permute-start.6 = (bf16[64,1664]{1,0:T(8,128)(2,1)S(1)}, bf16[64,1664]{1,0:T(8,128)(2,1)S(1)}, u32[]{:S(2)}, u32[]{:S(2)}) collective-permute-start(bf16[64,1664]{1,0:T(8,128)(2,1)S(1)} %slice.20), channel_id=1, source_target_pairs={{0,8},{8,16},{16,24},{24,28},{28,20},{20,12},{12,4},{4,0},{1,9},{9... | collective-permute-start | bytes 638984 | tf_op jit(solution)/shard_map/ppermute | solution.py:300
  38.4 0.7 collective-permute-start.7
  39.9 3.0 %collective-permute-done.6.refs_7_ = bf16[64,1664]{1,0:T(8,128)(2,1)S(1)} collective-permute-done((bf16[64,1664]{1,0:T(8,128)(2,1)S(1)}, bf16[64,1664]{1,0:T(8,128)(2,1)S(1)}, u32[]{:S(2)}, u32[]{:S(2)}) %collective-permute-start.6) | collective-permute-done | bytes 213024 | tf_op jit(solution)/shard_map/ppermute | solution.py:300
  42.9 1.4 %collective-permute-done.7.refs_8_ = bf16[64,1664]{1,0:T(8,128)(2,1)S(1)} collective-permute-done((bf16[64,1664]{1,0:T(8,128)(2,1)S(1)}, bf16[64,1664]{1,0:T(8,128)(2,1)S(1)}, u32[]{:S(2)}, u32[]{:S(2)}) %collective-permute-start.7) | collective-permute-done | bytes 213024 | tf_op jit(solution)/shard_map/ppermute | solution.py:303
  44.9 1.1 %collective-permute-done.13.refs_18_ = bf16[192,768]{1,0:T(8,128)(2,1)} collective-permute-done((bf16[192,768]{1,0:T(8,128)(2,1)S(1)}, bf16[192,768]{1,0:T(8,128)(2,1)}, u32[]{:S(2)}, u32[]{:S(2)}) %collective-permute-start.13) | collective-permute-done | bytes 294944 | tf_op jit(solution)/shard_map/ppermute | solution.py:264
  46.1 9.8 %hidden.1 = (bf16[128,768]{1,0:T(8,128)(2,1)S(1)}, bf16[256,768]{1,0:T(8,128)(2,1)}, bf16[256,768]{1,0:T(8,128)(2,1)}, bf16[256,768]{1,0:T(8,128)(2,1)}, bf16[128,768]{1,0:T(8,128)(2,1)S(1)}) custom-call(s32[2]{0:T(128)S(1)} %pad_add_fusion.me_ref, s32[8]{0:T(128)S(1)} %copy-done.4, bf16[128,1664]{1,0:T(8,128)(2,1)} %get-tuple-element.32.refs_0_, ...), custom_call_target="tpu_custom_call" | custom-call | tf_op jit(solution)/shard_map/hidden/pallas_call | solution.py:213
  56.1 1.9 %collective-permute-done.16.refs_8_ = bf16[192,1536]{1,0:T(8,128)(2,1)S(1)} collective-permute-done((bf16[192,1536]{1,0:T(8,128)(2,1)S(1)}, bf16[192,1536]{1,0:T(8,128)(2,1)S(1)}, u32[]{:S(2)}, u32[]{:S(2)}) %collective-permute-start.16) | collective-permute-done | bytes 589856 | tf_op jit(solution)/shard_map/ppermute | solution.py:264
  58.0 2.0 %down.2 = (f32[128,768]{1,0:T(8,128)S(1)}, f32[128,768]{1,0:T(8,128)S(1)}, f32[128,768]{1,0:T(8,128)S(1)}, f32[128,768]{1,0:T(8,128)S(1)}, f32[128,768]{1,0:T(8,...) custom-call(s32[2]{0:T(128)S(1)} %pad_add_fusion.me_ref, ...), custom_call_target="tpu_custom_call" | custom-call | tf_op jit(solution)/shard_map/down/pallas_call | solution.py:249
  60.1 1.6 %collective-permute-start.17 = (bf16[128,768]{1,0:T(8,128)(2,1)S(1)}, bf16[128,768]{1,0:T(8,128)(2,1)S(1)}, u32[]{:S(2)}, u32[]{:S(2)}) collective-permute-start(bf16[128,768]{1,0:T(8,128)(2,1)S(1)} %get-tuple-element.44), channel_id=1, source_target_pairs={{0,8},{8,16},{16,24},{24,28},{28,20},{20,12},{12,4},{4,0},{1,9},{9... | collective-permute-start | bytes 589832 | tf_op jit(solution)/shard_map/ppermute | solution.py:300
  62.2 2.0 %down.3 = (f32[128,768]{1,0:T(8,128)S(1)}, f32[128,768]{1,0:T(8,128)S(1)}, f32[128,768]{1,0:T(8,128)S(1)}, f32[128,768]{1,0:T(8,128)S(1)}, f32[128,768]{1,0:T(8,...) custom-call(s32[2]{0:T(128)S(1)} %pad_add_fusion.me_ref, ...), custom_call_target="tpu_custom_call" | custom-call | tf_op jit(solution)/shard_map/down/pallas_call | solution.py:249
  64.9 1.3 %collective-permute-start.28 = (bf16[128,768]{1,0:T(8,128)(2,1)S(1)}, bf16[128,768]{1,0:T(8,128)(2,1)S(1)}, u32[]{:S(2)}, u32[]{:S(2)}) collective-permute-start(bf16[128,768]{1,0:T(8,128)(2,1)S(1)} %get-tuple-element.56), channel_id=1, source_target_pairs={{0,8},{8,16},{16,24},{24,28},{28,20},{20,12},{12,4},{4,0},{1,9},{9... | collective-permute-start | bytes 589832 | tf_op jit(solution)/shard_map/ppermute | solution.py:300
  66.3 1.0 collective-permute-done.17
  67.3 1.9 %collective-permute-start.18 = (bf16[128,768]{1,0:T(8,128)(2,1)S(1)}, bf16[128,768]{1,0:T(8,128)(2,1)S(1)}, u32[]{:S(2)}, u32[]{:S(2)}) collective-permute-start(bf16[128,768]{1,0:T(8,128)(2,1)S(1)} %add_convert_fusion.11), channel_id=1, source_target_pairs={{0,8},{8,16},{16,24},{24,28},{28,20},{20,12},{12,4},{4,0},{1,9},{9... | collective-permute-start | bytes 589832 | tf_op jit(solution)/shard_map/ppermute | solution.py:300
  70.0 3.7 %collective-permute-done.24 = bf16[128,768]{1,0:T(8,128)(2,1)S(1)} collective-permute-done((bf16[128,768]{1,0:T(8,128)(2,1)S(1)}, bf16[128,768]{1,0:T(8,128)(2,1)S(1)}, u32[]{:S(2)}, u32[]{:S(2)}) %collective-permute-start.24) | collective-permute-done | bytes 196640 | tf_op jit(solution)/shard_map/ppermute | solution.py:303
  74.3 1.6 %collective-permute-start.29 = (bf16[128,768]{1,0:T(8,128)(2,1)S(1)}, bf16[128,768]{1,0:T(8,128)(2,1)S(1)}, u32[]{:S(2)}, u32[]{:S(2)}) collective-permute-start(bf16[128,768]{1,0:T(8,128)(2,1)S(1)} %add_convert_fusion.2), channel_id=1, source_target_pairs={{0,8},{8,16},{16,24},{24,28},{28,20},{20,12},{12,4},{4,0},{1,9},{9... | collective-permute-start | bytes 589832 | tf_op jit(solution)/shard_map/ppermute | solution.py:300
  76.4 1.6 %collective-permute-start.19 = (bf16[128,768]{1,0:T(8,128)(2,1)S(1)}, bf16[128,768]{1,0:T(8,128)(2,1)S(1)}, u32[]{:S(2)}, u32[]{:S(2)}) collective-permute-start(bf16[128,768]{1,0:T(8,128)(2,1)S(1)} %add_convert_fusion.10), channel_id=1, source_target_pairs={{0,8},{8,16},{16,24},{24,28},{28,20},{20,12},{12,4},{4,0},{1,9},{9... | collective-permute-start | bytes 589832 | tf_op jit(solution)/shard_map/ppermute | solution.py:300
  78.6 3.5 %collective-permute-done.25 = bf16[128,768]{1,0:T(8,128)(2,1)S(1)} collective-permute-done((bf16[128,768]{1,0:T(8,128)(2,1)S(1)}, bf16[128,768]{1,0:T(8,128)(2,1)S(1)}, u32[]{:S(2)}, u32[]{:S(2)}) %collective-permute-start.25) | collective-permute-done | bytes 196640 | tf_op jit(solution)/shard_map/ppermute | solution.py:303
  82.7 1.6 %collective-permute-start.30 = (bf16[128,768]{1,0:T(8,128)(2,1)S(1)}, bf16[128,768]{1,0:T(8,128)(2,1)S(1)}, u32[]{:S(2)}, u32[]{:S(2)}) collective-permute-start(bf16[128,768]{1,0:T(8,128)(2,1)S(1)} %add_convert_fusion.1), channel_id=1, source_target_pairs={{0,8},{8,16},{16,24},{24,28},{28,20},{20,12},{12,4},{4,0},{1,9},{9... | collective-permute-start | bytes 589832 | tf_op jit(solution)/shard_map/ppermute | solution.py:300
  84.9 1.6 %collective-permute-start.20 = (bf16[128,768]{1,0:T(8,128)(2,1)S(1)}, bf16[128,768]{1,0:T(8,128)(2,1)S(1)}, u32[]{:S(2)}, u32[]{:S(2)}) collective-permute-start(bf16[128,768]{1,0:T(8,128)(2,1)S(1)} %add_convert_fusion.9), channel_id=1, source_target_pairs={{0,8},{8,16},{16,24},{24,28},{28,20},{20,12},{12,4},{4,0},{1,9},{9... | collective-permute-start | bytes 589832 | tf_op jit(solution)/shard_map/ppermute | solution.py:300
  86.5 2.9 %collective-permute-done.26 = bf16[128,768]{1,0:T(8,128)(2,1)S(1)} collective-permute-done((bf16[128,768]{1,0:T(8,128)(2,1)S(1)}, bf16[128,768]{1,0:T(8,128)(2,1)S(1)}, u32[]{:S(2)}, u32[]{:S(2)}) %collective-permute-start.26) | collective-permute-done | bytes 196640 | tf_op jit(solution)/shard_map/ppermute | solution.py:303
  90.0 2.4 %collective-permute-done.20 = bf16[128,768]{1,0:T(8,128)(2,1)S(1)} collective-permute-done((bf16[128,768]{1,0:T(8,128)(2,1)S(1)}, bf16[128,768]{1,0:T(8,128)(2,1)S(1)}, u32[]{:S(2)}, u32[]{:S(2)}) %collective-permute-start.20) | collective-permute-done | bytes 196640 | tf_op jit(solution)/shard_map/ppermute | solution.py:300
  92.4 2.9 %collective-permute-done.27 = bf16[128,768]{1,0:T(8,128)(2,1)S(1)} collective-permute-done((bf16[128,768]{1,0:T(8,128)(2,1)S(1)}, bf16[128,768]{1,0:T(8,128)(2,1)S(1)}, u32[]{:S(2)}, u32[]{:S(2)}) %collective-permute-start.27) | collective-permute-done | bytes 196640 | tf_op jit(solution)/shard_map/ppermute | solution.py:303
  95.4 0.8 pad_maximum_fusion
  (81 shorter events, 7.9 us)
Async XLA Ops:
  2.9 43.2 %copy-start.4 = (s32[8]{0:T(128)S(1)}, s32[8]{0:T(128)}, u32[]{:S(2)}) copy-start(s32[8]{0:T(128)} %place_ref.1) | copy-start | bytes 100
  2.9 13.0 %collective-permute-start = (bf16[128,1664]{1,0:T(8,128)(2,1)}, bf16[128,1664]{1,0:T(8,128)(2,1)S(1)}, u32[]{:S(2)}, u32[]{:S(2)}) collective-permute-start(bf16[128,1664]{1,0:T(8,128)(2,1)} %get-tuple-element.32.refs_0_), channel_id=1, source_target_pairs={{0,8},{8,16},{16,24},{24,28},{28,20},{20,12},{12,4},{4,0},{1,9},{9... | collective-permute-start | bytes 1277960 | tf_op jit(solution)/shard_map/ppermute | solution.py:300
  6.0 11.8 %collective-permute-start.1 = (bf16[128,1664]{1,0:T(8,128)(2,1)}, bf16[128,1664]{1,0:T(8,128)(2,1)S(1)}, u32[]{:S(2)}, u32[]{:S(2)}) collective-permute-start(bf16[128,1664]{1,0:T(8,128)(2,1)} %get-tuple-element.32.refs_0_), channel_id=1, source_target_pairs={{8,0},{16,8},{24,16},{28,24},{20,28},{12,20},{4,12},{0,4},{9,1},{1... | collective-permute-start | bytes 1277960 | tf_op jit(solution)/shard_map/ppermute | solution.py:303
  6.0 33.2 %collective-permute-start.9 = (bf16[768,768]{1,0:T(8,128)(2,1)}, bf16[768,768]{1,0:T(8,128)(2,1)S(1)}, u32[]{:S(2)}, u32[]{:S(2)}) collective-permute-start(bf16[768,768]{1,0:T(8,128)(2,1)} %get-tuple-element.33.refs_9_), channel_id=1, source_target_pairs={{0,2},{1,3},{2,0},{3,1},{4,6},{5,7},{6,4},{7,5},{8,10},{9,11},{10,... | collective-permute-start | bytes 3538952 | tf_op jit(solution)/shard_map/ppermute | solution.py:264
  7.9 31.4 %collective-permute-start.8 = (bf16[768,768]{1,0:T(8,128)(2,1)}, bf16[768,768]{1,0:T(8,128)(2,1)S(1)}, u32[]{:S(2)}, u32[]{:S(2)}) collective-permute-start(bf16[768,768]{1,0:T(8,128)(2,1)} %get-tuple-element.33.refs_9_), channel_id=1, source_target_pairs={{0,1},{1,0},{2,3},{3,2},{4,5},{5,4},{6,7},{7,6},{8,9},{9,8},{10,11... | collective-permute-start | bytes 3538952 | tf_op jit(solution)/shard_map/ppermute | solution.py:264
  15.9 11.0 %collective-permute-start.2 = (bf16[128,1664]{1,0:T(8,128)(2,1)S(1)}, bf16[128,1664]{1,0:T(8,128)(2,1)S(1)}, u32[]{:S(2)}, u32[]{:S(2)}) collective-permute-start(bf16[128,1664]{1,0:T(8,128)(2,1)S(1)} %collective-permute-done.refs_1_), channel_id=1, source_target_pairs={{0,8},{8,16},{16,24},{24,28},{28,20},{20,12},{12,4},{4,0},{1,9},{9... | collective-permute-start | bytes 1277960 | tf_op jit(solution)/shard_map/ppermute | solution.py:300
  17.7 10.7 %collective-permute-start.3 = (bf16[128,1664]{1,0:T(8,128)(2,1)S(1)}, bf16[128,1664]{1,0:T(8,128)(2,1)S(1)}, u32[]{:S(2)}, u32[]{:S(2)}) collective-permute-start(bf16[128,1664]{1,0:T(8,128)(2,1)S(1)} %collective-permute-done.1.refs_2_), channel_id=1, source_target_pairs={{8,0},{16,8},{24,16},{28,24},{20,28},{12,20},{4,12},{0,4},{9,1},{1... | collective-permute-start | bytes 1277960 | tf_op jit(solution)/shard_map/ppermute | solution.py:303
  26.9 10.1 %collective-permute-start.4 = (bf16[128,1664]{1,0:T(8,128)(2,1)S(1)}, bf16[128,1664]{1,0:T(8,128)(2,1)S(1)}, u32[]{:S(2)}, u32[]{:S(2)}) collective-permute-start(bf16[128,1664]{1,0:T(8,128)(2,1)S(1)} %collective-permute-done.2.refs_3_), channel_id=1, source_target_pairs={{0,8},{8,16},{16,24},{24,28},{28,20},{20,12},{12,4},{4,0},{1,9},{9... | collective-permute-start | bytes 1277960 | tf_op jit(solution)/shard_map/ppermute | solution.py:300
  28.4 10.0 %collective-permute-start.5 = (bf16[128,1664]{1,0:T(8,128)(2,1)S(1)}, bf16[128,1664]{1,0:T(8,128)(2,1)S(1)}, u32[]{:S(2)}, u32[]{:S(2)}) collective-permute-start(bf16[128,1664]{1,0:T(8,128)(2,1)S(1)} %collective-permute-done.3.refs_4_), channel_id=1, source_target_pairs={{8,0},{16,8},{24,16},{28,24},{20,28},{12,20},{4,12},{0,4},{9,1},{1... | collective-permute-start | bytes 1277960 | tf_op jit(solution)/shard_map/ppermute | solution.py:303
  29.0 26.9 %collective-permute-start.15 = (bf16[192,1536]{1,0:T(8,128)(2,1)S(1)}, bf16[192,1536]{1,0:T(8,128)(2,1)S(1)}, u32[]{:S(2)}, u32[]{:S(2)}) collective-permute-start(bf16[192,1536]{1,0:T(8,128)(2,1)S(1)} %bitcast.7), channel_id=1, source_target_pairs={{0,2},{1,3},{2,0},{3,1},{4,6},{5,7},{6,4},{7,5},{8,10},{9,11},{10,... | collective-permute-start | bytes 1769480 | tf_op jit(solution)/shard_map/ppermute | solution.py:264
  37.0 5.9 %collective-permute-start.6 = (bf16[64,1664]{1,0:T(8,128)(2,1)S(1)}, bf16[64,1664]{1,0:T(8,128)(2,1)S(1)}, u32[]{:S(2)}, u32[]{:S(2)}) collective-permute-start(bf16[64,1664]{1,0:T(8,128)(2,1)S(1)} %slice.20), channel_id=1, source_target_pairs={{0,8},{8,16},{16,24},{24,28},{28,20},{20,12},{12,4},{4,0},{1,9},{9... | collective-permute-start | bytes 638984 | tf_op jit(solution)/shard_map/ppermute | solution.py:300
  38.4 5.9 %collective-permute-start.7 = (bf16[64,1664]{1,0:T(8,128)(2,1)S(1)}, bf16[64,1664]{1,0:T(8,128)(2,1)S(1)}, u32[]{:S(2)}, u32[]{:S(2)}) collective-permute-start(bf16[64,1664]{1,0:T(8,128)(2,1)S(1)} %slice.21), channel_id=1, source_target_pairs={{8,0},{16,8},{24,16},{28,24},{20,28},{12,20},{4,12},{0,4},{9,1},{1... | collective-permute-start | bytes 638984 | tf_op jit(solution)/shard_map/ppermute | solution.py:303
  39.3 5.1 %collective-permute-start.10 = (bf16[192,768]{1,0:T(8,128)(2,1)S(1)}, bf16[192,768]{1,0:T(8,128)(2,1)S(1)}, u32[]{:S(2)}, u32[]{:S(2)}) collective-permute-start(bf16[192,768]{1,0:T(8,128)(2,1)S(1)} %get-tuple-element.34.refs_11_), channel_id=1, source_target_pairs={{0,1},{1,0},{2,3},{3,2},{4,5},{5,4},{6,7},{7,6},{8,9},{9,8},{10,11... | collective-permute-start | bytes 884744 | tf_op jit(solution)/shard_map/ppermute | solution.py:264
  39.4 5.6 %collective-permute-start.11 = (bf16[192,768]{1,0:T(8,128)(2,1)S(1)}, bf16[192,768]{1,0:T(8,128)(2,1)}, u32[]{:S(2)}, u32[]{:S(2)}) collective-permute-start(bf16[192,768]{1,0:T(8,128)(2,1)S(1)} %get-tuple-element.35.refs_12_), channel_id=1, source_target_pairs={{0,1},{1,0},{2,3},{3,2},{4,5},{5,4},{6,7},{7,6},{8,9},{9,8},{10,11... | collective-permute-start | bytes 884744 | tf_op jit(solution)/shard_map/ppermute | solution.py:264
  42.9 2.0 %collective-permute-start.12 = (bf16[192,768]{1,0:T(8,128)(2,1)S(1)}, bf16[192,768]{1,0:T(8,128)(2,1)}, u32[]{:S(2)}, u32[]{:S(2)}) collective-permute-start(bf16[192,768]{1,0:T(8,128)(2,1)S(1)} %get-tuple-element.36.refs_13_), channel_id=1, source_target_pairs={{0,1},{1,0},{2,3},{3,2},{4,5},{5,4},{6,7},{7,6},{8,9},{9,8},{10,11... | collective-permute-start | bytes 884744 | tf_op jit(solution)/shard_map/ppermute | solution.py:264
  44.3 1.7 %collective-permute-start.13 = (bf16[192,768]{1,0:T(8,128)(2,1)S(1)}, bf16[192,768]{1,0:T(8,128)(2,1)}, u32[]{:S(2)}, u32[]{:S(2)}) collective-permute-start(bf16[192,768]{1,0:T(8,128)(2,1)S(1)} %get-tuple-element.37.refs_14_), channel_id=1, source_target_pairs={{0,1},{1,0},{2,3},{3,2},{4,5},{5,4},{6,7},{7,6},{8,9},{9,8},{10,11... | collective-permute-start | bytes 884744 | tf_op jit(solution)/shard_map/ppermute | solution.py:264
  44.4 11.7 %collective-permute-start.14 = (bf16[192,1536]{1,0:T(8,128)(2,1)S(1)}, bf16[192,1536]{1,0:T(8,128)(2,1)S(1)}, u32[]{:S(2)}, u32[]{:S(2)}) collective-permute-start(bf16[192,1536]{1,0:T(8,128)(2,1)S(1)} %bitcast.8), channel_id=1, source_target_pairs={{0,1},{1,0},{2,3},{3,2},{4,5},{5,4},{6,7},{7,6},{8,9},{9,8},{10,11... | collective-permute-start | bytes 1769480 | tf_op jit(solution)/shard_map/ppermute | solution.py:264
  55.9 2.1 %collective-permute-start.16 = (bf16[192,1536]{1,0:T(8,128)(2,1)S(1)}, bf16[192,1536]{1,0:T(8,128)(2,1)S(1)}, u32[]{:S(2)}, u32[]{:S(2)}) collective-permute-start(bf16[192,1536]{1,0:T(8,128)(2,1)S(1)} %after.3.refs_7_), channel_id=1, source_target_pairs={{0,1},{1,0},{2,3},{3,2},{4,5},{5,4},{6,7},{7,6},{8,9},{9,8},{10,11... | collective-permute-start | bytes 1769480 | tf_op jit(solution)/shard_map/ppermute | solution.py:264
  60.1 7.2 %collective-permute-start.17 = (bf16[128,768]{1,0:T(8,128)(2,1)S(1)}, bf16[128,768]{1,0:T(8,128)(2,1)S(1)}, u32[]{:S(2)}, u32[]{:S(2)}) collective-permute-start(bf16[128,768]{1,0:T(8,128)(2,1)S(1)} %get-tuple-element.44), channel_id=1, source_target_pairs={{0,8},{8,16},{16,24},{24,28},{28,20},{20,12},{12,4},{4,0},{1,9},{9... | collective-permute-start | bytes 589832 | tf_op jit(solution)/shard_map/ppermute | solution.py:300
  61.7 7.8 %collective-permute-start.21 = (bf16[128,768]{1,0:T(8,128)(2,1)S(1)}, bf16[128,768]{1,0:T(8,128)(2,1)S(1)}, u32[]{:S(2)}, u32[]{:S(2)}) collective-permute-start(bf16[128,768]{1,0:T(8,128)(2,1)S(1)} %get-tuple-element.48), channel_id=1, source_target_pairs={{8,0},{16,8},{24,16},{28,24},{20,28},{12,20},{4,12},{0,4},{9,1},{1... | collective-permute-start | bytes 589832 | tf_op jit(solution)/shard_map/ppermute | solution.py:303
  64.2 9.5 %collective-permute-start.24 = (bf16[128,768]{1,0:T(8,128)(2,1)S(1)}, bf16[128,768]{1,0:T(8,128)(2,1)S(1)}, u32[]{:S(2)}, u32[]{:S(2)}) collective-permute-start(bf16[128,768]{1,0:T(8,128)(2,1)S(1)} %get-tuple-element.52), channel_id=1, source_target_pairs={{8,0},{16,8},{24,16},{28,24},{20,28},{12,20},{4,12},{0,4},{9,1},{1... | collective-permute-start | bytes 589832 | tf_op jit(solution)/shard_map/ppermute | solution.py:303
  64.9 9.3 %collective-permute-start.28 = (bf16[128,768]{1,0:T(8,128)(2,1)S(1)}, bf16[128,768]{1,0:T(8,128)(2,1)S(1)}, u32[]{:S(2)}, u32[]{:S(2)}) collective-permute-start(bf16[128,768]{1,0:T(8,128)(2,1)S(1)} %get-tuple-element.56), channel_id=1, source_target_pairs={{0,8},{8,16},{16,24},{24,28},{28,20},{20,12},{12,4},{4,0},{1,9},{9... | collective-permute-start | bytes 589832 | tf_op jit(solution)/shard_map/ppermute | solution.py:300
  67.3 9.1 %collective-permute-start.18 = (bf16[128,768]{1,0:T(8,128)(2,1)S(1)}, bf16[128,768]{1,0:T(8,128)(2,1)S(1)}, u32[]{:S(2)}, u32[]{:S(2)}) collective-permute-start(bf16[128,768]{1,0:T(8,128)(2,1)S(1)} %add_convert_fusion.11), channel_id=1, source_target_pairs={{0,8},{8,16},{16,24},{24,28},{28,20},{20,12},{12,4},{4,0},{1,9},{9... | collective-permute-start | bytes 589832 | tf_op jit(solution)/shard_map/ppermute | solution.py:300
  69.5 8.5 %collective-permute-start.22 = (bf16[128,768]{1,0:T(8,128)(2,1)S(1)}, bf16[128,768]{1,0:T(8,128)(2,1)S(1)}, u32[]{:S(2)}, u32[]{:S(2)}) collective-permute-start(bf16[128,768]{1,0:T(8,128)(2,1)S(1)} %add_convert_fusion.8), channel_id=1, source_target_pairs={{8,0},{16,8},{24,16},{28,24},{20,28},{12,20},{4,12},{0,4},{9,1},{1... | collective-permute-start | bytes 589832 | tf_op jit(solution)/shard_map/ppermute | solution.py:303
  73.8 8.4 %collective-permute-start.25 = (bf16[128,768]{1,0:T(8,128)(2,1)S(1)}, bf16[128,768]{1,0:T(8,128)(2,1)S(1)}, u32[]{:S(2)}, u32[]{:S(2)}) collective-permute-start(bf16[128,768]{1,0:T(8,128)(2,1)S(1)} %add_convert_fusion.5), channel_id=1, source_target_pairs={{8,0},{16,8},{24,16},{28,24},{20,28},{12,20},{4,12},{0,4},{9,1},{1... | collective-permute-start | bytes 589832 | tf_op jit(solution)/shard_map/ppermute | solution.py:303
  74.3 8.4 %collective-permute-start.29 = (bf16[128,768]{1,0:T(8,128)(2,1)S(1)}, bf16[128,768]{1,0:T(8,128)(2,1)S(1)}, u32[]{:S(2)}, u32[]{:S(2)}) collective-permute-start(bf16[128,768]{1,0:T(8,128)(2,1)S(1)} %add_convert_fusion.2), channel_id=1, source_target_pairs={{0,8},{8,16},{16,24},{24,28},{28,20},{20,12},{12,4},{4,0},{1,9},{9... | collective-permute-start | bytes 589832 | tf_op jit(solution)/shard_map/ppermute | solution.py:300
  76.4 8.4 %collective-permute-start.19 = (bf16[128,768]{1,0:T(8,128)(2,1)S(1)}, bf16[128,768]{1,0:T(8,128)(2,1)S(1)}, u32[]{:S(2)}, u32[]{:S(2)}) collective-permute-start(bf16[128,768]{1,0:T(8,128)(2,1)S(1)} %add_convert_fusion.10), channel_id=1, source_target_pairs={{0,8},{8,16},{16,24},{24,28},{28,20},{20,12},{12,4},{4,0},{1,9},{9... | collective-permute-start | bytes 589832 | tf_op jit(solution)/shard_map/ppermute | solution.py:300
  78.1 11.9 %collective-permute-start.23 = (bf16[128,768]{1,0:T(8,128)(2,1)S(1)}, bf16[128,768]{1,0:T(8,128)(2,1)S(1)}, u32[]{:S(2)}, u32[]{:S(2)}) collective-permute-start(bf16[128,768]{1,0:T(8,128)(2,1)S(1)} %add_convert_fusion.7), channel_id=1, source_target_pairs={{8,0},{16,8},{24,16},{28,24},{20,28},{12,20},{4,12},{0,4},{9,1},{1... | collective-permute-start | bytes 589832 | tf_op jit(solution)/shard_map/ppermute | solution.py:303
  82.2 7.3 %collective-permute-start.26 = (bf16[128,768]{1,0:T(8,128)(2,1)S(1)}, bf16[128,768]{1,0:T(8,128)(2,1)S(1)}, u32[]{:S(2)}, u32[]{:S(2)}) collective-permute-start(bf16[128,768]{1,0:T(8,128)(2,1)S(1)} %add_convert_fusion.4), channel_id=1, source_target_pairs={{8,0},{16,8},{24,16},{28,24},{20,28},{12,20},{4,12},{0,4},{9,1},{1... | collective-permute-start | bytes 589832 | tf_op jit(solution)/shard_map/ppermute | solution.py:303
  82.7 9.7 %collective-permute-start.30 = (bf16[128,768]{1,0:T(8,128)(2,1)S(1)}, bf16[128,768]{1,0:T(8,128)(2,1)S(1)}, u32[]{:S(2)}, u32[]{:S(2)}) collective-permute-start(bf16[128,768]{1,0:T(8,128)(2,1)S(1)} %add_convert_fusion.1), channel_id=1, source_target_pairs={{0,8},{8,16},{16,24},{24,28},{28,20},{20,12},{12,4},{4,0},{1,9},{9... | collective-permute-start | bytes 589832 | tf_op jit(solution)/shard_map/ppermute | solution.py:300
  84.9 7.5 %collective-permute-start.20 = (bf16[128,768]{1,0:T(8,128)(2,1)S(1)}, bf16[128,768]{1,0:T(8,128)(2,1)S(1)}, u32[]{:S(2)}, u32[]{:S(2)}) collective-permute-start(bf16[128,768]{1,0:T(8,128)(2,1)S(1)} %add_convert_fusion.9), channel_id=1, source_target_pairs={{0,8},{8,16},{16,24},{24,28},{28,20},{20,12},{12,4},{4,0},{1,9},{9... | collective-permute-start | bytes 589832 | tf_op jit(solution)/shard_map/ppermute | solution.py:300
  89.5 5.8 %collective-permute-start.27 = (bf16[128,768]{1,0:T(8,128)(2,1)S(1)}, bf16[128,768]{1,0:T(8,128)(2,1)S(1)}, u32[]{:S(2)}, u32[]{:S(2)}) collective-permute-start(bf16[128,768]{1,0:T(8,128)(2,1)S(1)} %add_convert_fusion.3), channel_id=1, source_target_pairs={{8,0},{16,8},{24,16},{28,24},{20,28},{12,20},{4,12},{0,4},{9,1},{1... | collective-permute-start | bytes 589832 | tf_op jit(solution)/shard_map/ppermute | solution.py:303
  (12 other events, 103.3 us)

commit v4 on v3

--- a/solution.py
+++ b/solution.py
@@ -337,15 +337,16 @@
         long_sign = 1 if side == 0 else -1
         sent_first = [(0, far), (-long_sign, far - 1)]
         table = {}
-        for low in range(0, len(hidden), 5):
-            chosen = groups[low : low + 5]
+        cuts = [len(groups), len(groups) - 2] + list(range(len(groups) - 7, 0, -5)) + [0]
+        for low, high in zip(cuts[1:], cuts):
+            chosen = groups[low:high]
             keys = list(dict.fromkeys(key for group in chosen for key, _, _ in group))
             kinds = [jnp.bfloat16 if key in sent_first else jnp.float32 for key in keys]
             slots = [
                 [(keys.index(key), first, block.shape[0]) for key, first, block in group]
                 for group in chosen
             ]
-            outs = down_blocks(me, side * half, half, hidden[low : low + 5], slots, kinds, downs)
+            outs = down_blocks(me, side * half, half, hidden[low:high], slots, kinds, downs)
             table.update(zip(keys, outs))
         long_run = long_way(table[0, far])
         short_run = short_way(table[-long_sign, far - 1])

time: 96.3 us -> 95.4 us (level)
  waiting for transfers between devices: 48.6 us -> 46.3 us
  Pallas kernels: 16.8 us -> 18.5 us
    ppermute x11, waiting for transfers between devices: 14.8 us -> 13 us  [counter(): return lax.ppermute(x, 'ep', behind)]
    pallas_call x2 -> x4, Pallas kernels: 4.09 us -> 5.69 us  [down_blocks(): pl.pallas_call(functools.partial(down_kernel, slots, layout, column), out...]
  transfers between devices with their start and end apart: 31 -> 31, of which waited for: 16 -> 15; matrix products, arithmetic and copies ran while one was open for 1% -> 1% of each run, Pallas kernels for 12% -> 15%
where the time goes in v4:
time: 95.4 us; the launch traced here: 95.2 us
  waiting for transfers between devices  46.3 us (49%)
  starting transfers between devices  28.8 us (30%)
  Pallas kernels  18.5 us (19%)
  other arithmetic  1.34 us (1%)
    ppermute x11, waiting for transfers between devices, clock(): return lax.ppermute(x, 'ep', ahead)  30.3 us
    ppermute x11, starting transfers between devices, clock(): return lax.ppermute(x, 'ep', ahead)  18.9 us
    ppermute x11, waiting for transfers between devices, counter(): return lax.ppermute(x, 'ep', behind)  13 us
    pallas_call x1, Pallas kernels, hidden_blocks(): pl.pallas_call(functools.partial(hidden_kernel, len(blocks), layout), out...  9.75 us
    pallas_call x4, Pallas kernels, down_blocks(): pl.pallas_call(functools.partial(down_kernel, slots, layout, column), out...  5.69 us
    ppermute x11, starting transfers between devices, counter(): return lax.ppermute(x, 'ep', behind)  5.22 us
    ppermute x9, starting transfers between devices, swap_blk(): return lax.ppermute(value, 'blk', pairs)  4.69 us
    ppermute x9, waiting for transfers between devices, swap_blk(): return lax.ppermute(value, 'blk', pairs)  2.99 us
  transfers between devices with their start and end apart: 31, of which 15 were waited for; matrix products, arithmetic and copies ran while one was open for 1% of the time, Pallas kernels for 15%

profile of v4, /device:TPU:0, one launch (start us, length us, event | category | flops | bytes accessed | tf_op | source)
XLA Modules:
  0.0 95.2 jit_solution(5222300776628591705)
XLA Ops:
  0.0 2.9 %pack.1 = (bf16[128,1664]{1,0:T(8,128)(2,1)}, bf16[768,768]{1,0:T(8,128)(2,1)}) custom-call(bf16[1536]{0:T(1024)(128)(2,1)} %refs_0_.1, bf16[8,1536]{1,0:T(8,128)(2,1)} %bitcast.15, s32[4,128]{1,0:T(4,128)} %bitcast.16, bf16[128,1536]{1,0:T(8,128)(2,1)} %refs_3_.1, bf16[384,768]{1,0:T(8,128)(2,1)} %bitcast.13, bf16[384,768]{1,0:T(8,128)(2,1)} %bitcast.14), custom_call_target="tpu_custom_call" | custom-call | flops 3145728 | bytes 3145728 | tf_op jit(solution)/shard_map/pack/pallas_call | solution.py:107
  2.9 3.1 %collective-permute-start = (bf16[128,1664]{1,0:T(8,128)(2,1)}, bf16[128,1664]{1,0:T(8,128)(2,1)S(1)}, u32[]{:S(2)}, u32[]{:S(2)}) collective-permute-start(bf16[128,1664]{1,0:T(8,128)(2,1)} %get-tuple-element.32.refs_0_), channel_id=1, source_target_pairs={{0,8},{8,16},{16,24},{24,28},{28,20},{20,12},{12,4},{4,0},{1,9},{9... | collective-permute-start | bytes 1277960 | tf_op jit(solution)/shard_map/ppermute | solution.py:300
  6.0 2.0 %collective-permute-start.9 = (bf16[768,768]{1,0:T(8,128)(2,1)}, bf16[768,768]{1,0:T(8,128)(2,1)S(1)}, u32[]{:S(2)}, u32[]{:S(2)}) collective-permute-start(bf16[768,768]{1,0:T(8,128)(2,1)} %get-tuple-element.33.refs_9_), channel_id=1, source_target_pairs={{0,2},{1,3},{2,0},{3,1},{4,6},{5,7},{6,4},{7,5},{8,10},{9,11},{10,... | collective-permute-start | bytes 3538952 | tf_op jit(solution)/shard_map/ppermute | solution.py:264
  8.0 8.0 %collective-permute-done.refs_1_ = bf16[128,1664]{1,0:T(8,128)(2,1)S(1)} collective-permute-done((bf16[128,1664]{1,0:T(8,128)(2,1)}, bf16[128,1664]{1,0:T(8,128)(2,1)S(1)}, u32[]{:S(2)}, u32[]{:S(2)}) %collective-permute-start) | collective-permute-done | bytes 426016 | tf_op jit(solution)/shard_map/ppermute | solution.py:300
  15.9 1.8 %collective-permute-start.2 = (bf16[128,1664]{1,0:T(8,128)(2,1)S(1)}, bf16[128,1664]{1,0:T(8,128)(2,1)S(1)}, u32[]{:S(2)}, u32[]{:S(2)}) collective-permute-start(bf16[128,1664]{1,0:T(8,128)(2,1)S(1)} %collective-permute-done.refs_1_), channel_id=1, source_target_pairs={{0,8},{8,16},{16,24},{24,28},{28,20},{20,12},{12,4},{4,0},{1,9},{9... | collective-permute-start | bytes 1277960 | tf_op jit(solution)/shard_map/ppermute | solution.py:300
  18.0 9.0 %collective-permute-done.2.refs_3_ = bf16[128,1664]{1,0:T(8,128)(2,1)S(1)} collective-permute-done((bf16[128,1664]{1,0:T(8,128)(2,1)S(1)}, bf16[128,1664]{1,0:T(8,128)(2,1)S(1)}, u32[]{:S(2)}, u32[]{:S(2)}) %collective-permute-start.2) | collective-permute-done | bytes 426016 | tf_op jit(solution)/shard_map/ppermute | solution.py:300
  26.9 1.5 %collective-permute-start.4 = (bf16[128,1664]{1,0:T(8,128)(2,1)S(1)}, bf16[128,1664]{1,0:T(8,128)(2,1)S(1)}, u32[]{:S(2)}, u32[]{:S(2)}) collective-permute-start(bf16[128,1664]{1,0:T(8,128)(2,1)S(1)} %collective-permute-done.2.refs_3_), channel_id=1, source_target_pairs={{0,8},{8,16},{16,24},{24,28},{28,20},{20,12},{12,4},{4,0},{1,9},{9... | collective-permute-start | bytes 1277960 | tf_op jit(solution)/shard_map/ppermute | solution.py:300
  29.0 1.5 %collective-permute-start.15 = (bf16[192,1536]{1,0:T(8,128)(2,1)S(1)}, bf16[192,1536]{1,0:T(8,128)(2,1)S(1)}, u32[]{:S(2)}, u32[]{:S(2)}) collective-permute-start(bf16[192,1536]{1,0:T(8,128)(2,1)S(1)} %bitcast.7), channel_id=1, source_target_pairs={{0,2},{1,3},{2,0},{3,1},{4,6},{5,7},{6,4},{7,5},{8,10},{9,11},{10,... | collective-permute-start | bytes 1769480 | tf_op jit(solution)/shard_map/ppermute | solution.py:264
  30.5 6.5 %collective-permute-done.4.refs_5_ = bf16[128,1664]{1,0:T(8,128)(2,1)S(1)} collective-permute-done((bf16[128,1664]{1,0:T(8,128)(2,1)S(1)}, bf16[128,1664]{1,0:T(8,128)(2,1)S(1)}, u32[]{:S(2)}, u32[]{:S(2)}) %collective-permute-start.4) | collective-permute-done | bytes 426016 | tf_op jit(solution)/shard_map/ppermute | solution.py:300
  37.0 1.4 %collective-permute-start.6 = (bf16[64,1664]{1,0:T(8,128)(2,1)S(1)}, bf16[64,1664]{1,0:T(8,128)(2,1)S(1)}, u32[]{:S(2)}, u32[]{:S(2)}) collective-permute-start(bf16[64,1664]{1,0:T(8,128)(2,1)S(1)} %slice.20), channel_id=1, source_target_pairs={{0,8},{8,16},{16,24},{24,28},{28,20},{20,12},{12,4},{4,0},{1,9},{9... | collective-permute-start | bytes 638984 | tf_op jit(solution)/shard_map/ppermute | solution.py:300
  39.9 3.0 %collective-permute-done.6.refs_7_ = bf16[64,1664]{1,0:T(8,128)(2,1)S(1)} collective-permute-done((bf16[64,1664]{1,0:T(8,128)(2,1)S(1)}, bf16[64,1664]{1,0:T(8,128)(2,1)S(1)}, u32[]{:S(2)}, u32[]{:S(2)}) %collective-permute-start.6) | collective-permute-done | bytes 213024 | tf_op jit(solution)/shard_map/ppermute | solution.py:300
  42.9 1.4 %collective-permute-done.7.refs_8_ = bf16[64,1664]{1,0:T(8,128)(2,1)S(1)} collective-permute-done((bf16[64,1664]{1,0:T(8,128)(2,1)S(1)}, bf16[64,1664]{1,0:T(8,128)(2,1)S(1)}, u32[]{:S(2)}, u32[]{:S(2)}) %collective-permute-start.7) | collective-permute-done | bytes 213024 | tf_op jit(solution)/shard_map/ppermute | solution.py:303
  45.0 1.1 %collective-permute-done.13.refs_18_ = bf16[192,768]{1,0:T(8,128)(2,1)} collective-permute-done((bf16[192,768]{1,0:T(8,128)(2,1)S(1)}, bf16[192,768]{1,0:T(8,128)(2,1)}, u32[]{:S(2)}, u32[]{:S(2)}) %collective-permute-start.13) | collective-permute-done | bytes 294944 | tf_op jit(solution)/shard_map/ppermute | solution.py:264
  46.1 9.8 %hidden.1 = (bf16[128,768]{1,0:T(8,128)(2,1)S(1)}, bf16[256,768]{1,0:T(8,128)(2,1)}, bf16[256,768]{1,0:T(8,128)(2,1)}, bf16[256,768]{1,0:T(8,128)(2,1)}, bf16[128,768]{1,0:T(8,128)(2,1)S(1)}) custom-call(s32[2]{0:T(128)S(1)} %pad_add_fusion.me_ref, s32[8]{0:T(128)S(1)} %copy-done.4, bf16[128,1664]{1,0:T(8,128)(2,1)} %get-tuple-element.32.refs_0_, ...), custom_call_target="tpu_custom_call" | custom-call | tf_op jit(solution)/shard_map/hidden/pallas_call | solution.py:213
  56.1 1.9 %collective-permute-done.16.refs_6_.refs_5_ = bf16[192,1536]{1,0:T(8,128)(2,1)S(1)} collective-permute-done((bf16[192,1536]{1,0:T(8,128)(2,1)S(1)}, bf16[192,1536]{1,0:T(8,128)(2,1)S(1)}, u32[]{:S(2)}, u32[]{:S(2)}) %collective-permute-start.16) | collective-permute-done | bytes 589856 | tf_op jit(solution)/shard_map/ppermute | solution.py:264
  58.0 1.3 %down.5 = (bf16[128,768]{1,0:T(8,128)(2,1)S(1)}, f32[128,768]{1,0:T(8,128)S(1)}, bf16[128,768]{1,0:T(8,128)(2,1)S(1)}) custom-call(s32[2]{0:T(128)S(1)} %pad_add_fusion.me_ref, bf16[256,768]{1,0:T(8,128)(2,1)S(1)} %copy-done.1, bf16[128,768]{1,0:T(8,128)(2,1)S(1)} %get-tuple-element.41.refs_1_, bf16[192,1536]{1,0:T(8,128)(2,1)S(1)} %bitcast.9, ...), custom_call_target="tpu_custom_call" | custom-call | tf_op jit(solution)/shard_map/down/pallas_call | solution.py:249
  59.3 1.6 %collective-permute-start.17 = (bf16[128,768]{1,0:T(8,128)(2,1)S(1)}, bf16[128,768]{1,0:T(8,128)(2,1)S(1)}, u32[]{:S(2)}, u32[]{:S(2)}) collective-permute-start(bf16[128,768]{1,0:T(8,128)(2,1)S(1)} %get-tuple-element.44), channel_id=1, source_target_pairs={{0,8},{8,16},{16,24},{24,28},{28,20},{20,12},{12,4},{4,0},{1,9},{9... | collective-permute-start | bytes 589832 | tf_op jit(solution)/shard_map/ppermute | solution.py:300
  61.4 1.3 %down.7 = (f32[128,768]{1,0:T(8,128)S(1)}, bf16[128,768]{1,0:T(8,128)(2,1)S(1)}, bf16[128,768]{1,0:T(8,128)(2,1)S(1)}) custom-call(s32[2]{0:T(128)S(1)} %pad_add_fusion.me_ref, bf16[256,768]{1,0:T(8,128)(2,1)S(1)} %copy-done.1, bf16[128,768]{1,0:T(8,128)(2,1)S(1)} %get-tuple-element.41.refs_1_, bf16[192,1536]{1,0:T(8,128)(2,1)S(1)} %bitcast.10, ...), custom_call_target="tpu_custom_call" | custom-call | tf_op jit(solution)/shard_map/down/pallas_call | solution.py:249
  63.4 1.3 %collective-permute-start.28 = (bf16[128,768]{1,0:T(8,128)(2,1)S(1)}, bf16[128,768]{1,0:T(8,128)(2,1)S(1)}, u32[]{:S(2)}, u32[]{:S(2)}) collective-permute-start(bf16[128,768]{1,0:T(8,128)(2,1)S(1)} %get-tuple-element.56), channel_id=1, source_target_pairs={{0,8},{8,16},{16,24},{24,28},{28,20},{20,12},{12,4},{4,0},{1,9},{9... | collective-permute-start | bytes 589832 | tf_op jit(solution)/shard_map/ppermute | solution.py:300
  64.7 1.6 %down.4 = (f32[128,768]{1,0:T(8,128)S(1)}, f32[128,768]{1,0:T(8,128)S(1)}, f32[128,768]{1,0:T(8,128)S(1)}, f32[128,768]{1,0:T(8,128)S(1)}, f32[128,768]{1,0:T(8,128)S(1)}) custom-call(s32[2]{0:T(128)S(1)} %pad_add_fusion.me_ref, bf16[128,768]{1,0:T(8,128)(2,1)S(1)} %get-tuple-element.38.refs_0_, bf16[256,768]{1,0:T(8,128)(2,1)S(1)} %copy-done.2, ...), custom_call_target="tpu_custom_call" | custom-call | tf_op jit(solution)/shard_map/down/pallas_call | solution.py:249
  66.3 1.6 %down.6 = (f32[128,768]{1,0:T(8,128)S(1)}, f32[128,768]{1,0:T(8,128)S(1)}, f32[128,768]{1,0:T(8,128)S(1)}, f32[128,768]{1,0:T(8,128)S(1)}, f32[128,768]{1,0:T(8,128)S(1)}) custom-call(s32[2]{0:T(128)S(1)} %pad_add_fusion.me_ref, bf16[128,768]{1,0:T(8,128)(2,1)S(1)} %get-tuple-element.38.refs_0_, bf16[256,768]{1,0:T(8,128)(2,1)S(1)} %copy-done.2, ...), custom_call_target="tpu_custom_call" | custom-call | tf_op jit(solution)/shard_map/down/pallas_call | solution.py:249
  67.9 1.6 %collective-permute-start.18 = (bf16[128,768]{1,0:T(8,128)(2,1)S(1)}, bf16[128,768]{1,0:T(8,128)(2,1)S(1)}, u32[]{:S(2)}, u32[]{:S(2)}) collective-permute-start(bf16[128,768]{1,0:T(8,128)(2,1)S(1)} %add_convert_fusion.11), channel_id=1, source_target_pairs={{0,8},{8,16},{16,24},{24,28},{28,20},{20,12},{12,4},{4,0},{1,9},{9... | collective-permute-start | bytes 589832 | tf_op jit(solution)/shard_map/ppermute | solution.py:300
  70.1 2.4 %collective-permute-done.24 = bf16[128,768]{1,0:T(8,128)(2,1)S(1)} collective-permute-done((bf16[128,768]{1,0:T(8,128)(2,1)S(1)}, bf16[128,768]{1,0:T(8,128)(2,1)S(1)}, u32[]{:S(2)}, u32[]{:S(2)}) %collective-permute-start.24) | collective-permute-done | bytes 196640 | tf_op jit(solution)/shard_map/ppermute | solution.py:303
  73.1 1.6 %collective-permute-start.29 = (bf16[128,768]{1,0:T(8,128)(2,1)S(1)}, bf16[128,768]{1,0:T(8,128)(2,1)S(1)}, u32[]{:S(2)}, u32[]{:S(2)}) collective-permute-start(bf16[128,768]{1,0:T(8,128)(2,1)S(1)} %add_convert_fusion.2), channel_id=1, source_target_pairs={{0,8},{8,16},{16,24},{24,28},{28,20},{20,12},{12,4},{4,0},{1,9},{9... | collective-permute-start | bytes 589832 | tf_op jit(solution)/shard_map/ppermute | solution.py:300
  74.7 0.9 collective-permute-done.18
  75.6 1.6 %collective-permute-start.19 = (bf16[128,768]{1,0:T(8,128)(2,1)S(1)}, bf16[128,768]{1,0:T(8,128)(2,1)S(1)}, u32[]{:S(2)}, u32[]{:S(2)}) collective-permute-start(bf16[128,768]{1,0:T(8,128)(2,1)S(1)} %add_convert_fusion.10), channel_id=1, source_target_pairs={{0,8},{8,16},{16,24},{24,28},{28,20},{20,12},{12,4},{4,0},{1,9},{9... | collective-permute-start | bytes 589832 | tf_op jit(solution)/shard_map/ppermute | solution.py:300
  78.0 3.7 %collective-permute-done.25 = bf16[128,768]{1,0:T(8,128)(2,1)S(1)} collective-permute-done((bf16[128,768]{1,0:T(8,128)(2,1)S(1)}, bf16[128,768]{1,0:T(8,128)(2,1)S(1)}, u32[]{:S(2)}, u32[]{:S(2)}) %collective-permute-start.25) | collective-permute-done | bytes 196640 | tf_op jit(solution)/shard_map/ppermute | solution.py:303
  82.3 1.6 %collective-permute-start.30 = (bf16[128,768]{1,0:T(8,128)(2,1)S(1)}, bf16[128,768]{1,0:T(8,128)(2,1)S(1)}, u32[]{:S(2)}, u32[]{:S(2)}) collective-permute-start(bf16[128,768]{1,0:T(8,128)(2,1)S(1)} %add_convert_fusion.1), channel_id=1, source_target_pairs={{0,8},{8,16},{16,24},{24,28},{28,20},{20,12},{12,4},{4,0},{1,9},{9... | collective-permute-start | bytes 589832 | tf_op jit(solution)/shard_map/ppermute | solution.py:300
  84.5 1.6 %collective-permute-start.20 = (bf16[128,768]{1,0:T(8,128)(2,1)S(1)}, bf16[128,768]{1,0:T(8,128)(2,1)S(1)}, u32[]{:S(2)}, u32[]{:S(2)}) collective-permute-start(bf16[128,768]{1,0:T(8,128)(2,1)S(1)} %add_convert_fusion.9), channel_id=1, source_target_pairs={{0,8},{8,16},{16,24},{24,28},{28,20},{20,12},{12,4},{4,0},{1,9},{9... | collective-permute-start | bytes 589832 | tf_op jit(solution)/shard_map/ppermute | solution.py:300
  86.1 2.6 %collective-permute-done.26 = bf16[128,768]{1,0:T(8,128)(2,1)S(1)} collective-permute-done((bf16[128,768]{1,0:T(8,128)(2,1)S(1)}, bf16[128,768]{1,0:T(8,128)(2,1)S(1)}, u32[]{:S(2)}, u32[]{:S(2)}) %collective-permute-start.26) | collective-permute-done | bytes 196640 | tf_op jit(solution)/shard_map/ppermute | solution.py:303
  89.2 2.4 %collective-permute-done.20 = bf16[128,768]{1,0:T(8,128)(2,1)S(1)} collective-permute-done((bf16[128,768]{1,0:T(8,128)(2,1)S(1)}, bf16[128,768]{1,0:T(8,128)(2,1)S(1)}, u32[]{:S(2)}, u32[]{:S(2)}) %collective-permute-start.20) | collective-permute-done | bytes 196640 | tf_op jit(solution)/shard_map/ppermute | solution.py:300
  91.6 2.8 %collective-permute-done.27 = bf16[128,768]{1,0:T(8,128)(2,1)S(1)} collective-permute-done((bf16[128,768]{1,0:T(8,128)(2,1)S(1)}, bf16[128,768]{1,0:T(8,128)(2,1)S(1)}, u32[]{:S(2)}, u32[]{:S(2)}) %collective-permute-start.27) | collective-permute-done | bytes 196640 | tf_op jit(solution)/shard_map/ppermute | solution.py:303
  (83 shorter events, 8.8 us)
Async XLA Ops:
  2.9 43.2 %copy-start.4 = (s32[8]{0:T(128)S(1)}, s32[8]{0:T(128)}, u32[]{:S(2)}) copy-start(s32[8]{0:T(128)} %place_ref.1) | copy-start | bytes 100
  2.9 13.0 %collective-permute-start = (bf16[128,1664]{1,0:T(8,128)(2,1)}, bf16[128,1664]{1,0:T(8,128)(2,1)S(1)}, u32[]{:S(2)}, u32[]{:S(2)}) collective-permute-start(bf16[128,1664]{1,0:T(8,128)(2,1)} %get-tuple-element.32.refs_0_), channel_id=1, source_target_pairs={{0,8},{8,16},{16,24},{24,28},{28,20},{20,12},{12,4},{4,0},{1,9},{9... | collective-permute-start | bytes 1277960 | tf_op jit(solution)/shard_map/ppermute | solution.py:300
  6.0 11.8 %collective-permute-start.1 = (bf16[128,1664]{1,0:T(8,128)(2,1)}, bf16[128,1664]{1,0:T(8,128)(2,1)S(1)}, u32[]{:S(2)}, u32[]{:S(2)}) collective-permute-start(bf16[128,1664]{1,0:T(8,128)(2,1)} %get-tuple-element.32.refs_0_), channel_id=1, source_target_pairs={{8,0},{16,8},{24,16},{28,24},{20,28},{12,20},{4,12},{0,4},{9,1},{1... | collective-permute-start | bytes 1277960 | tf_op jit(solution)/shard_map/ppermute | solution.py:303
  6.0 33.2 %collective-permute-start.9 = (bf16[768,768]{1,0:T(8,128)(2,1)}, bf16[768,768]{1,0:T(8,128)(2,1)S(1)}, u32[]{:S(2)}, u32[]{:S(2)}) collective-permute-start(bf16[768,768]{1,0:T(8,128)(2,1)} %get-tuple-element.33.refs_9_), channel_id=1, source_target_pairs={{0,2},{1,3},{2,0},{3,1},{4,6},{5,7},{6,4},{7,5},{8,10},{9,11},{10,... | collective-permute-start | bytes 3538952 | tf_op jit(solution)/shard_map/ppermute | solution.py:264
  8.0 31.4 %collective-permute-start.8 = (bf16[768,768]{1,0:T(8,128)(2,1)}, bf16[768,768]{1,0:T(8,128)(2,1)S(1)}, u32[]{:S(2)}, u32[]{:S(2)}) collective-permute-start(bf16[768,768]{1,0:T(8,128)(2,1)} %get-tuple-element.33.refs_9_), channel_id=1, source_target_pairs={{0,1},{1,0},{2,3},{3,2},{4,5},{5,4},{6,7},{7,6},{8,9},{9,8},{10,11... | collective-permute-start | bytes 3538952 | tf_op jit(solution)/shard_map/ppermute | solution.py:264
  15.9 11.0 %collective-permute-start.2 = (bf16[128,1664]{1,0:T(8,128)(2,1)S(1)}, bf16[128,1664]{1,0:T(8,128)(2,1)S(1)}, u32[]{:S(2)}, u32[]{:S(2)}) collective-permute-start(bf16[128,1664]{1,0:T(8,128)(2,1)S(1)} %collective-permute-done.refs_1_), channel_id=1, source_target_pairs={{0,8},{8,16},{16,24},{24,28},{28,20},{20,12},{12,4},{4,0},{1,9},{9... | collective-permute-start | bytes 1277960 | tf_op jit(solution)/shard_map/ppermute | solution.py:300
  17.8 10.7 %collective-permute-start.3 = (bf16[128,1664]{1,0:T(8,128)(2,1)S(1)}, bf16[128,1664]{1,0:T(8,128)(2,1)S(1)}, u32[]{:S(2)}, u32[]{:S(2)}) collective-permute-start(bf16[128,1664]{1,0:T(8,128)(2,1)S(1)} %collective-permute-done.1.refs_2_), channel_id=1, source_target_pairs={{8,0},{16,8},{24,16},{28,24},{20,28},{12,20},{4,12},{0,4},{9,1},{1... | collective-permute-start | bytes 1277960 | tf_op jit(solution)/shard_map/ppermute | solution.py:303
  26.9 10.1 %collective-permute-start.4 = (bf16[128,1664]{1,0:T(8,128)(2,1)S(1)}, bf16[128,1664]{1,0:T(8,128)(2,1)S(1)}, u32[]{:S(2)}, u32[]{:S(2)}) collective-permute-start(bf16[128,1664]{1,0:T(8,128)(2,1)S(1)} %collective-permute-done.2.refs_3_), channel_id=1, source_target_pairs={{0,8},{8,16},{16,24},{24,28},{28,20},{20,12},{12,4},{4,0},{1,9},{9... | collective-permute-start | bytes 1277960 | tf_op jit(solution)/shard_map/ppermute | solution.py:300
  28.5 10.0 %collective-permute-start.5 = (bf16[128,1664]{1,0:T(8,128)(2,1)S(1)}, bf16[128,1664]{1,0:T(8,128)(2,1)S(1)}, u32[]{:S(2)}, u32[]{:S(2)}) collective-permute-start(bf16[128,1664]{1,0:T(8,128)(2,1)S(1)} %collective-permute-done.3.refs_4_), channel_id=1, source_target_pairs={{8,0},{16,8},{24,16},{28,24},{20,28},{12,20},{4,12},{0,4},{9,1},{1... | collective-permute-start | bytes 1277960 | tf_op jit(solution)/shard_map/ppermute | solution.py:303
  29.0 26.8 %collective-permute-start.15 = (bf16[192,1536]{1,0:T(8,128)(2,1)S(1)}, bf16[192,1536]{1,0:T(8,128)(2,1)S(1)}, u32[]{:S(2)}, u32[]{:S(2)}) collective-permute-start(bf16[192,1536]{1,0:T(8,128)(2,1)S(1)} %bitcast.7), channel_id=1, source_target_pairs={{0,2},{1,3},{2,0},{3,1},{4,6},{5,7},{6,4},{7,5},{8,10},{9,11},{10,... | collective-permute-start | bytes 1769480 | tf_op jit(solution)/shard_map/ppermute | solution.py:264
  37.0 5.9 %collective-permute-start.6 = (bf16[64,1664]{1,0:T(8,128)(2,1)S(1)}, bf16[64,1664]{1,0:T(8,128)(2,1)S(1)}, u32[]{:S(2)}, u32[]{:S(2)}) collective-permute-start(bf16[64,1664]{1,0:T(8,128)(2,1)S(1)} %slice.20), channel_id=1, source_target_pairs={{0,8},{8,16},{16,24},{24,28},{28,20},{20,12},{12,4},{4,0},{1,9},{9... | collective-permute-start | bytes 638984 | tf_op jit(solution)/shard_map/ppermute | solution.py:300
  38.5 5.9 %collective-permute-start.7 = (bf16[64,1664]{1,0:T(8,128)(2,1)S(1)}, bf16[64,1664]{1,0:T(8,128)(2,1)S(1)}, u32[]{:S(2)}, u32[]{:S(2)}) collective-permute-start(bf16[64,1664]{1,0:T(8,128)(2,1)S(1)} %slice.21), channel_id=1, source_target_pairs={{8,0},{16,8},{24,16},{28,24},{20,28},{12,20},{4,12},{0,4},{9,1},{1... | collective-permute-start | bytes 638984 | tf_op jit(solution)/shard_map/ppermute | solution.py:303
  39.3 5.1 %collective-permute-start.10 = (bf16[192,768]{1,0:T(8,128)(2,1)S(1)}, bf16[192,768]{1,0:T(8,128)(2,1)S(1)}, u32[]{:S(2)}, u32[]{:S(2)}) collective-permute-start(bf16[192,768]{1,0:T(8,128)(2,1)S(1)} %get-tuple-element.34.refs_11_), channel_id=1, source_target_pairs={{0,1},{1,0},{2,3},{3,2},{4,5},{5,4},{6,7},{7,6},{8,9},{9,8},{10,11... | collective-permute-start | bytes 884744 | tf_op jit(solution)/shard_map/ppermute | solution.py:264
  39.4 5.6 %collective-permute-start.11 = (bf16[192,768]{1,0:T(8,128)(2,1)S(1)}, bf16[192,768]{1,0:T(8,128)(2,1)}, u32[]{:S(2)}, u32[]{:S(2)}) collective-permute-start(bf16[192,768]{1,0:T(8,128)(2,1)S(1)} %get-tuple-element.35.refs_12_), channel_id=1, source_target_pairs={{0,1},{1,0},{2,3},{3,2},{4,5},{5,4},{6,7},{7,6},{8,9},{9,8},{10,11... | collective-permute-start | bytes 884744 | tf_op jit(solution)/shard_map/ppermute | solution.py:264
  42.9 2.0 %collective-permute-start.12 = (bf16[192,768]{1,0:T(8,128)(2,1)S(1)}, bf16[192,768]{1,0:T(8,128)(2,1)}, u32[]{:S(2)}, u32[]{:S(2)}) collective-permute-start(bf16[192,768]{1,0:T(8,128)(2,1)S(1)} %get-tuple-element.36.refs_13_), channel_id=1, source_target_pairs={{0,1},{1,0},{2,3},{3,2},{4,5},{5,4},{6,7},{7,6},{8,9},{9,8},{10,11... | collective-permute-start | bytes 884744 | tf_op jit(solution)/shard_map/ppermute | solution.py:264
  44.4 1.7 %collective-permute-start.13 = (bf16[192,768]{1,0:T(8,128)(2,1)S(1)}, bf16[192,768]{1,0:T(8,128)(2,1)}, u32[]{:S(2)}, u32[]{:S(2)}) collective-permute-start(bf16[192,768]{1,0:T(8,128)(2,1)S(1)} %get-tuple-element.37.refs_14_), channel_id=1, source_target_pairs={{0,1},{1,0},{2,3},{3,2},{4,5},{5,4},{6,7},{7,6},{8,9},{9,8},{10,11... | collective-permute-start | bytes 884744 | tf_op jit(solution)/shard_map/ppermute | solution.py:264
  44.5 11.7 %collective-permute-start.14 = (bf16[192,1536]{1,0:T(8,128)(2,1)S(1)}, bf16[192,1536]{1,0:T(8,128)(2,1)S(1)}, u32[]{:S(2)}, u32[]{:S(2)}) collective-permute-start(bf16[192,1536]{1,0:T(8,128)(2,1)S(1)} %bitcast.8), channel_id=1, source_target_pairs={{0,1},{1,0},{2,3},{3,2},{4,5},{5,4},{6,7},{7,6},{8,9},{9,8},{10,11... | collective-permute-start | bytes 1769480 | tf_op jit(solution)/shard_map/ppermute | solution.py:264
  55.9 2.1 %collective-permute-start.16 = (bf16[192,1536]{1,0:T(8,128)(2,1)S(1)}, bf16[192,1536]{1,0:T(8,128)(2,1)S(1)}, u32[]{:S(2)}, u32[]{:S(2)}) collective-permute-start(bf16[192,1536]{1,0:T(8,128)(2,1)S(1)} %after.3.refs_5_.refs_4_), channel_id=1, source_target_pairs={{0,1},{1,0},{2,3},{3,2},{4,5},{5,4},{6,7},{7,6},{8,9},{9,8},{10,11... | collective-permute-start | bytes 1769480 | tf_op jit(solution)/shard_map/ppermute | solution.py:264
  59.3 8.6 %collective-permute-start.17 = (bf16[128,768]{1,0:T(8,128)(2,1)S(1)}, bf16[128,768]{1,0:T(8,128)(2,1)S(1)}, u32[]{:S(2)}, u32[]{:S(2)}) collective-permute-start(bf16[128,768]{1,0:T(8,128)(2,1)S(1)} %get-tuple-element.44), channel_id=1, source_target_pairs={{0,8},{8,16},{16,24},{24,28},{28,20},{20,12},{12,4},{4,0},{1,9},{9... | collective-permute-start | bytes 589832 | tf_op jit(solution)/shard_map/ppermute | solution.py:300
  60.9 8.7 %collective-permute-start.21 = (bf16[128,768]{1,0:T(8,128)(2,1)S(1)}, bf16[128,768]{1,0:T(8,128)(2,1)S(1)}, u32[]{:S(2)}, u32[]{:S(2)}) collective-permute-start(bf16[128,768]{1,0:T(8,128)(2,1)S(1)} %get-tuple-element.48), channel_id=1, source_target_pairs={{8,0},{16,8},{24,16},{28,24},{20,28},{12,20},{4,12},{0,4},{9,1},{1... | collective-permute-start | bytes 589832 | tf_op jit(solution)/shard_map/ppermute | solution.py:303
  62.6 9.9 %collective-permute-start.24 = (bf16[128,768]{1,0:T(8,128)(2,1)S(1)}, bf16[128,768]{1,0:T(8,128)(2,1)S(1)}, u32[]{:S(2)}, u32[]{:S(2)}) collective-permute-start(bf16[128,768]{1,0:T(8,128)(2,1)S(1)} %get-tuple-element.52), channel_id=1, source_target_pairs={{8,0},{16,8},{24,16},{28,24},{20,28},{12,20},{4,12},{0,4},{9,1},{1... | collective-permute-start | bytes 589832 | tf_op jit(solution)/shard_map/ppermute | solution.py:303
  63.4 9.7 %collective-permute-start.28 = (bf16[128,768]{1,0:T(8,128)(2,1)S(1)}, bf16[128,768]{1,0:T(8,128)(2,1)S(1)}, u32[]{:S(2)}, u32[]{:S(2)}) collective-permute-start(bf16[128,768]{1,0:T(8,128)(2,1)S(1)} %get-tuple-element.56), channel_id=1, source_target_pairs={{0,8},{8,16},{16,24},{24,28},{28,20},{20,12},{12,4},{4,0},{1,9},{9... | collective-permute-start | bytes 589832 | tf_op jit(solution)/shard_map/ppermute | solution.py:300
  67.9 7.7 %collective-permute-start.18 = (bf16[128,768]{1,0:T(8,128)(2,1)S(1)}, bf16[128,768]{1,0:T(8,128)(2,1)S(1)}, u32[]{:S(2)}, u32[]{:S(2)}) collective-permute-start(bf16[128,768]{1,0:T(8,128)(2,1)S(1)} %add_convert_fusion.11), channel_id=1, source_target_pairs={{0,8},{8,16},{16,24},{24,28},{28,20},{20,12},{12,4},{4,0},{1,9},{9... | collective-permute-start | bytes 589832 | tf_op jit(solution)/shard_map/ppermute | solution.py:300
  69.6 7.9 %collective-permute-start.22 = (bf16[128,768]{1,0:T(8,128)(2,1)S(1)}, bf16[128,768]{1,0:T(8,128)(2,1)S(1)}, u32[]{:S(2)}, u32[]{:S(2)}) collective-permute-start(bf16[128,768]{1,0:T(8,128)(2,1)S(1)} %add_convert_fusion.8), channel_id=1, source_target_pairs={{8,0},{16,8},{24,16},{28,24},{20,28},{12,20},{4,12},{0,4},{9,1},{1... | collective-permute-start | bytes 589832 | tf_op jit(solution)/shard_map/ppermute | solution.py:303
  72.5 9.2 %collective-permute-start.25 = (bf16[128,768]{1,0:T(8,128)(2,1)S(1)}, bf16[128,768]{1,0:T(8,128)(2,1)S(1)}, u32[]{:S(2)}, u32[]{:S(2)}) collective-permute-start(bf16[128,768]{1,0:T(8,128)(2,1)S(1)} %add_convert_fusion.5), channel_id=1, source_target_pairs={{8,0},{16,8},{24,16},{28,24},{20,28},{12,20},{4,12},{0,4},{9,1},{1... | collective-permute-start | bytes 589832 | tf_op jit(solution)/shard_map/ppermute | solution.py:303
  73.1 9.2 %collective-permute-start.29 = (bf16[128,768]{1,0:T(8,128)(2,1)S(1)}, bf16[128,768]{1,0:T(8,128)(2,1)S(1)}, u32[]{:S(2)}, u32[]{:S(2)}) collective-permute-start(bf16[128,768]{1,0:T(8,128)(2,1)S(1)} %add_convert_fusion.2), channel_id=1, source_target_pairs={{0,8},{8,16},{16,24},{24,28},{28,20},{20,12},{12,4},{4,0},{1,9},{9... | collective-permute-start | bytes 589832 | tf_op jit(solution)/shard_map/ppermute | solution.py:300
  75.6 8.8 %collective-permute-start.19 = (bf16[128,768]{1,0:T(8,128)(2,1)S(1)}, bf16[128,768]{1,0:T(8,128)(2,1)S(1)}, u32[]{:S(2)}, u32[]{:S(2)}) collective-permute-start(bf16[128,768]{1,0:T(8,128)(2,1)S(1)} %add_convert_fusion.10), channel_id=1, source_target_pairs={{0,8},{8,16},{16,24},{24,28},{28,20},{20,12},{12,4},{4,0},{1,9},{9... | collective-permute-start | bytes 589832 | tf_op jit(solution)/shard_map/ppermute | solution.py:300
  77.5 11.6 %collective-permute-start.23 = (bf16[128,768]{1,0:T(8,128)(2,1)S(1)}, bf16[128,768]{1,0:T(8,128)(2,1)S(1)}, u32[]{:S(2)}, u32[]{:S(2)}) collective-permute-start(bf16[128,768]{1,0:T(8,128)(2,1)S(1)} %add_convert_fusion.7), channel_id=1, source_target_pairs={{8,0},{16,8},{24,16},{28,24},{20,28},{12,20},{4,12},{0,4},{9,1},{1... | collective-permute-start | bytes 589832 | tf_op jit(solution)/shard_map/ppermute | solution.py:303
  81.8 6.9 %collective-permute-start.26 = (bf16[128,768]{1,0:T(8,128)(2,1)S(1)}, bf16[128,768]{1,0:T(8,128)(2,1)S(1)}, u32[]{:S(2)}, u32[]{:S(2)}) collective-permute-start(bf16[128,768]{1,0:T(8,128)(2,1)S(1)} %add_convert_fusion.4), channel_id=1, source_target_pairs={{8,0},{16,8},{24,16},{28,24},{20,28},{12,20},{4,12},{0,4},{9,1},{1... | collective-permute-start | bytes 589832 | tf_op jit(solution)/shard_map/ppermute | solution.py:303
  82.3 9.3 %collective-permute-start.30 = (bf16[128,768]{1,0:T(8,128)(2,1)S(1)}, bf16[128,768]{1,0:T(8,128)(2,1)S(1)}, u32[]{:S(2)}, u32[]{:S(2)}) collective-permute-start(bf16[128,768]{1,0:T(8,128)(2,1)S(1)} %add_convert_fusion.1), channel_id=1, source_target_pairs={{0,8},{8,16},{16,24},{24,28},{28,20},{20,12},{12,4},{4,0},{1,9},{9... | collective-permute-start | bytes 589832 | tf_op jit(solution)/shard_map/ppermute | solution.py:300
  84.5 7.1 %collective-permute-start.20 = (bf16[128,768]{1,0:T(8,128)(2,1)S(1)}, bf16[128,768]{1,0:T(8,128)(2,1)S(1)}, u32[]{:S(2)}, u32[]{:S(2)}) collective-permute-start(bf16[128,768]{1,0:T(8,128)(2,1)S(1)} %add_convert_fusion.9), channel_id=1, source_target_pairs={{0,8},{8,16},{16,24},{24,28},{28,20},{20,12},{12,4},{4,0},{1,9},{9... | collective-permute-start | bytes 589832 | tf_op jit(solution)/shard_map/ppermute | solution.py:300
  88.7 5.7 %collective-permute-start.27 = (bf16[128,768]{1,0:T(8,128)(2,1)S(1)}, bf16[128,768]{1,0:T(8,128)(2,1)S(1)}, u32[]{:S(2)}, u32[]{:S(2)}) collective-permute-start(bf16[128,768]{1,0:T(8,128)(2,1)S(1)} %add_convert_fusion.3), channel_id=1, source_target_pairs={{8,0},{16,8},{24,16},{28,24},{20,28},{12,20},{4,12},{0,4},{9,1},{1... | collective-permute-start | bytes 589832 | tf_op jit(solution)/shard_map/ppermute | solution.py:303
  (12 other events, 106.6 us)

commit v5 on v4

--- a/solution.py
+++ b/solution.py
@@ -286,6 +286,27 @@
     return total.astype(jnp.bfloat16)
 
 
+def finish_kernel(*refs):
+    out_ref, width = refs[-1], refs[0].shape[1]
+    for side in range(2):
+        total = refs[3 * side][...].astype(jnp.float32)
+        for ref in refs[3 * side + 1 : 3 * side + 3]:
+            total = total + ref[...].astype(jnp.float32)
+        out_ref[:, side * width : (side + 1) * width] = total.astype(jnp.bfloat16)
+
+
+def finish(terms):
+    rows, width = terms[0].shape
+    return pl.pallas_call(
+        finish_kernel,
+        out_shape=jax.ShapeDtypeStruct((rows, 2 * width), jnp.bfloat16),
+        in_specs=[WHOLE] * len(terms),
+        out_specs=WHOLE,
+        compiler_params=params(),
+        name="finish",
+    )(*terms)
+
+
 def on_device(
     tokens, norm_gain, router_weight, routes, placement, gate_weight, up_weight, down_weight
 ):
@@ -354,8 +375,8 @@
             long_run = long_way(add_round(long_run, table[long_sign, step]))
             if step > 1:
                 short_run = short_way(add_round(short_run, table[-long_sign, step - 1]))
-        results.append(add_round(table[0, 0], long_run, short_run))
-    return jnp.concatenate(results, axis=1)
+        results += [table[0, 0], long_run, short_run]
+    return finish(results)
 
 
 def solution(mesh):

time: 95.4 us -> 94.9 us (level)
  transfers between devices with their start and end apart: 31 -> 31, of which waited for: 15 -> 16; matrix products, arithmetic and copies ran while one was open for 1% -> 1% of each run, Pallas kernels for 15% -> 15%
where the time goes in v5:
time: 94.9 us; the launch traced here: 94.7 us
  waiting for transfers between devices  45.7 us (48%)
  starting transfers between devices  28.8 us (30%)
  Pallas kernels  19.4 us (20%)
    ppermute x11, waiting for transfers between devices, clock(): return lax.ppermute(x, 'ep', ahead)  29.9 us
    ppermute x11, starting transfers between devices, clock(): return lax.ppermute(x, 'ep', ahead)  18.9 us
    ppermute x11, waiting for transfers between devices, counter(): return lax.ppermute(x, 'ep', behind)  12.9 us
    pallas_call x1, Pallas kernels, hidden_blocks(): pl.pallas_call(functools.partial(hidden_kernel, len(blocks), layout), out...  9.75 us
    pallas_call x4, Pallas kernels, down_blocks(): pl.pallas_call(functools.partial(down_kernel, slots, layout, column), out...  5.69 us
    ppermute x11, starting transfers between devices, counter(): return lax.ppermute(x, 'ep', behind)  5.22 us
    ppermute x9, starting transfers between devices, swap_blk(): return lax.ppermute(value, 'blk', pairs)  4.69 us
    ppermute x9, waiting for transfers between devices, swap_blk(): return lax.ppermute(value, 'blk', pairs)  2.99 us
  transfers between devices with their start and end apart: 31, of which 16 were waited for; matrix products, arithmetic and copies ran while one was open for 1% of the time, Pallas kernels for 15%

profile of v5, /device:TPU:0, one launch (start us, length us, event | category | flops | bytes accessed | tf_op | source)
XLA Modules:
  0.0 94.7 jit_solution(1969952445000469852)
XLA Ops:
  0.0 2.9 %pack.1 = (bf16[128,1664]{1,0:T(8,128)(2,1)}, bf16[768,768]{1,0:T(8,128)(2,1)}) custom-call(bf16[1536]{0:T(1024)(128)(2,1)} %refs_0_.1, bf16[8,1536]{1,0:T(8,128)(2,1)} %bitcast.15, s32[4,128]{1,0:T(4,128)} %bitcast.16, bf16[128,1536]{1,0:T(8,128)(2,1)} %refs_3_.1, bf16[384,768]{1,0:T(8,128)(2,1)} %bitcast.13, bf16[384,768]{1,0:T(8,128)(2,1)} %bitcast.14), custom_call_target="tpu_custom_call" | custom-call | flops 3145728 | bytes 3145728 | tf_op jit(solution)/shard_map/pack/pallas_call | solution.py:107
  2.9 3.1 %collective-permute-start = (bf16[128,1664]{1,0:T(8,128)(2,1)}, bf16[128,1664]{1,0:T(8,128)(2,1)S(1)}, u32[]{:S(2)}, u32[]{:S(2)}) collective-permute-start(bf16[128,1664]{1,0:T(8,128)(2,1)} %get-tuple-element.32.refs_0_), channel_id=1, source_target_pairs={{0,8},{8,16},{16,24},{24,28},{28,20},{20,12},{12,4},{4,0},{1,9},{9... | collective-permute-start | bytes 1277960 | tf_op jit(solution)/shard_map/ppermute | solution.py:321
  6.0 2.0 %collective-permute-start.9 = (bf16[768,768]{1,0:T(8,128)(2,1)}, bf16[768,768]{1,0:T(8,128)(2,1)S(1)}, u32[]{:S(2)}, u32[]{:S(2)}) collective-permute-start(bf16[768,768]{1,0:T(8,128)(2,1)} %get-tuple-element.33.refs_9_), channel_id=1, source_target_pairs={{0,2},{1,3},{2,0},{3,1},{4,6},{5,7},{6,4},{7,5},{8,10},{9,11},{10,... | collective-permute-start | bytes 3538952 | tf_op jit(solution)/shard_map/ppermute | solution.py:264
  8.0 8.0 %collective-permute-done.refs_1_ = bf16[128,1664]{1,0:T(8,128)(2,1)S(1)} collective-permute-done((bf16[128,1664]{1,0:T(8,128)(2,1)}, bf16[128,1664]{1,0:T(8,128)(2,1)S(1)}, u32[]{:S(2)}, u32[]{:S(2)}) %collective-permute-start) | collective-permute-done | bytes 426016 | tf_op jit(solution)/shard_map/ppermute | solution.py:321
  15.9 1.8 %collective-permute-start.2 = (bf16[128,1664]{1,0:T(8,128)(2,1)S(1)}, bf16[128,1664]{1,0:T(8,128)(2,1)S(1)}, u32[]{:S(2)}, u32[]{:S(2)}) collective-permute-start(bf16[128,1664]{1,0:T(8,128)(2,1)S(1)} %collective-permute-done.refs_1_), channel_id=1, source_target_pairs={{0,8},{8,16},{16,24},{24,28},{28,20},{20,12},{12,4},{4,0},{1,9},{9... | collective-permute-start | bytes 1277960 | tf_op jit(solution)/shard_map/ppermute | solution.py:321
  18.0 9.0 %collective-permute-done.2.refs_3_ = bf16[128,1664]{1,0:T(8,128)(2,1)S(1)} collective-permute-done((bf16[128,1664]{1,0:T(8,128)(2,1)S(1)}, bf16[128,1664]{1,0:T(8,128)(2,1)S(1)}, u32[]{:S(2)}, u32[]{:S(2)}) %collective-permute-start.2) | collective-permute-done | bytes 426016 | tf_op jit(solution)/shard_map/ppermute | solution.py:321
  26.9 1.5 %collective-permute-start.4 = (bf16[128,1664]{1,0:T(8,128)(2,1)S(1)}, bf16[128,1664]{1,0:T(8,128)(2,1)S(1)}, u32[]{:S(2)}, u32[]{:S(2)}) collective-permute-start(bf16[128,1664]{1,0:T(8,128)(2,1)S(1)} %collective-permute-done.2.refs_3_), channel_id=1, source_target_pairs={{0,8},{8,16},{16,24},{24,28},{28,20},{20,12},{12,4},{4,0},{1,9},{9... | collective-permute-start | bytes 1277960 | tf_op jit(solution)/shard_map/ppermute | solution.py:321
  29.0 1.5 %collective-permute-start.15 = (bf16[192,1536]{1,0:T(8,128)(2,1)S(1)}, bf16[192,1536]{1,0:T(8,128)(2,1)S(1)}, u32[]{:S(2)}, u32[]{:S(2)}) collective-permute-start(bf16[192,1536]{1,0:T(8,128)(2,1)S(1)} %bitcast.7), channel_id=1, source_target_pairs={{0,2},{1,3},{2,0},{3,1},{4,6},{5,7},{6,4},{7,5},{8,10},{9,11},{10,... | collective-permute-start | bytes 1769480 | tf_op jit(solution)/shard_map/ppermute | solution.py:264
  30.5 6.5 %collective-permute-done.4.refs_5_ = bf16[128,1664]{1,0:T(8,128)(2,1)S(1)} collective-permute-done((bf16[128,1664]{1,0:T(8,128)(2,1)S(1)}, bf16[128,1664]{1,0:T(8,128)(2,1)S(1)}, u32[]{:S(2)}, u32[]{:S(2)}) %collective-permute-start.4) | collective-permute-done | bytes 426016 | tf_op jit(solution)/shard_map/ppermute | solution.py:321
  37.0 1.4 %collective-permute-start.6 = (bf16[64,1664]{1,0:T(8,128)(2,1)S(1)}, bf16[64,1664]{1,0:T(8,128)(2,1)S(1)}, u32[]{:S(2)}, u32[]{:S(2)}) collective-permute-start(bf16[64,1664]{1,0:T(8,128)(2,1)S(1)} %slice.20), channel_id=1, source_target_pairs={{0,8},{8,16},{16,24},{24,28},{28,20},{20,12},{12,4},{4,0},{1,9},{9... | collective-permute-start | bytes 638984 | tf_op jit(solution)/shard_map/ppermute | solution.py:321
  39.9 3.0 %collective-permute-done.6.refs_7_ = bf16[64,1664]{1,0:T(8,128)(2,1)S(1)} collective-permute-done((bf16[64,1664]{1,0:T(8,128)(2,1)S(1)}, bf16[64,1664]{1,0:T(8,128)(2,1)S(1)}, u32[]{:S(2)}, u32[]{:S(2)}) %collective-permute-start.6) | collective-permute-done | bytes 213024 | tf_op jit(solution)/shard_map/ppermute | solution.py:321
  42.9 1.4 %collective-permute-done.7.refs_8_ = bf16[64,1664]{1,0:T(8,128)(2,1)S(1)} collective-permute-done((bf16[64,1664]{1,0:T(8,128)(2,1)S(1)}, bf16[64,1664]{1,0:T(8,128)(2,1)S(1)}, u32[]{:S(2)}, u32[]{:S(2)}) %collective-permute-start.7) | collective-permute-done | bytes 213024 | tf_op jit(solution)/shard_map/ppermute | solution.py:324
  45.0 1.1 %collective-permute-done.13.refs_18_ = bf16[192,768]{1,0:T(8,128)(2,1)} collective-permute-done((bf16[192,768]{1,0:T(8,128)(2,1)S(1)}, bf16[192,768]{1,0:T(8,128)(2,1)}, u32[]{:S(2)}, u32[]{:S(2)}) %collective-permute-start.13) | collective-permute-done | bytes 294944 | tf_op jit(solution)/shard_map/ppermute | solution.py:264
  46.1 9.8 %hidden.1 = (bf16[128,768]{1,0:T(8,128)(2,1)S(1)}, bf16[256,768]{1,0:T(8,128)(2,1)}, bf16[256,768]{1,0:T(8,128)(2,1)}, bf16[256,768]{1,0:T(8,128)(2,1)}, bf16[128,768]{1,0:T(8,128)(2,1)S(1)}) custom-call(s32[2]{0:T(128)S(1)} %pad_add_fusion.me_ref, s32[8]{0:T(128)S(1)} %copy-done.4, bf16[128,1664]{1,0:T(8,128)(2,1)} %get-tuple-element.32.refs_0_, ...), custom_call_target="tpu_custom_call" | custom-call | tf_op jit(solution)/shard_map/hidden/pallas_call | solution.py:213
  56.1 1.9 %collective-permute-done.16.refs_6_.refs_5_ = bf16[192,1536]{1,0:T(8,128)(2,1)S(1)} collective-permute-done((bf16[192,1536]{1,0:T(8,128)(2,1)S(1)}, bf16[192,1536]{1,0:T(8,128)(2,1)S(1)}, u32[]{:S(2)}, u32[]{:S(2)}) %collective-permute-start.16) | collective-permute-done | bytes 589856 | tf_op jit(solution)/shard_map/ppermute | solution.py:264
  58.0 1.3 %down.7 = (f32[128,768]{1,0:T(8,128)S(1)}, bf16[128,768]{1,0:T(8,128)(2,1)S(1)}, bf16[128,768]{1,0:T(8,128)(2,1)S(1)}) custom-call(s32[2]{0:T(128)S(1)} %pad_add_fusion.me_ref, bf16[256,768]{1,0:T(8,128)(2,1)S(1)} %copy-done.1, bf16[128,768]{1,0:T(8,128)(2,1)S(1)} %get-tuple-element.41.refs_1_, bf16[192,1536]{1,0:T(8,128)(2,1)S(1)} %bitcast.9, ...), custom_call_target="tpu_custom_call" | custom-call | tf_op jit(solution)/shard_map/down/pallas_call | solution.py:249
  59.3 1.6 %collective-permute-start.28 = (bf16[128,768]{1,0:T(8,128)(2,1)S(1)}, bf16[128,768]{1,0:T(8,128)(2,1)S(1)}, u32[]{:S(2)}, u32[]{:S(2)}) collective-permute-start(bf16[128,768]{1,0:T(8,128)(2,1)S(1)} %get-tuple-element.56), channel_id=1, source_target_pairs={{0,8},{8,16},{16,24},{24,28},{28,20},{20,12},{12,4},{4,0},{1,9},{9... | collective-permute-start | bytes 589832 | tf_op jit(solution)/shard_map/ppermute | solution.py:321
  61.4 1.3 %down.5 = (bf16[128,768]{1,0:T(8,128)(2,1)S(1)}, f32[128,768]{1,0:T(8,128)S(1)}, bf16[128,768]{1,0:T(8,128)(2,1)S(1)}) custom-call(s32[2]{0:T(128)S(1)} %pad_add_fusion.me_ref, bf16[256,768]{1,0:T(8,128)(2,1)S(1)} %copy-done.1, bf16[128,768]{1,0:T(8,128)(2,1)S(1)} %get-tuple-element.41.refs_1_, bf16[192,1536]{1,0:T(8,128)(2,1)S(1)} %bitcast.10, ...), custom_call_target="tpu_custom_call" | custom-call | tf_op jit(solution)/shard_map/down/pallas_call | solution.py:249
  63.4 1.3 %collective-permute-start.17 = (bf16[128,768]{1,0:T(8,128)(2,1)S(1)}, bf16[128,768]{1,0:T(8,128)(2,1)S(1)}, u32[]{:S(2)}, u32[]{:S(2)}) collective-permute-start(bf16[128,768]{1,0:T(8,128)(2,1)S(1)} %get-tuple-element.44), channel_id=1, source_target_pairs={{0,8},{8,16},{16,24},{24,28},{28,20},{20,12},{12,4},{4,0},{1,9},{9... | collective-permute-start | bytes 589832 | tf_op jit(solution)/shard_map/ppermute | solution.py:321
  64.7 1.6 %down.6 = (f32[128,768]{1,0:T(8,128)S(1)}, f32[128,768]{1,0:T(8,128)S(1)}, f32[128,768]{1,0:T(8,128)S(1)}, f32[128,768]{1,0:T(8,128)S(1)}, f32[128,768]{1,0:T(8,128)S(1)}) custom-call(s32[2]{0:T(128)S(1)} %pad_add_fusion.me_ref, bf16[128,768]{1,0:T(8,128)(2,1)S(1)} %get-tuple-element.38.refs_0_, bf16[256,768]{1,0:T(8,128)(2,1)S(1)} %copy-done.2, ...), custom_call_target="tpu_custom_call" | custom-call | tf_op jit(solution)/shard_map/down/pallas_call | solution.py:249
  66.3 1.6 %down.4 = (f32[128,768]{1,0:T(8,128)S(1)}, f32[128,768]{1,0:T(8,128)S(1)}, f32[128,768]{1,0:T(8,128)S(1)}, f32[128,768]{1,0:T(8,128)S(1)}, f32[128,768]{1,0:T(8,128)S(1)}) custom-call(s32[2]{0:T(128)S(1)} %pad_add_fusion.me_ref, bf16[128,768]{1,0:T(8,128)(2,1)S(1)} %get-tuple-element.38.refs_0_, bf16[256,768]{1,0:T(8,128)(2,1)S(1)} %copy-done.2, ...), custom_call_target="tpu_custom_call" | custom-call | tf_op jit(solution)/shard_map/down/pallas_call | solution.py:249
  67.9 1.6 %collective-permute-start.29 = (bf16[128,768]{1,0:T(8,128)(2,1)S(1)}, bf16[128,768]{1,0:T(8,128)(2,1)S(1)}, u32[]{:S(2)}, u32[]{:S(2)}) collective-permute-start(bf16[128,768]{1,0:T(8,128)(2,1)S(1)} %add_convert_fusion.1), channel_id=1, source_target_pairs={{0,8},{8,16},{16,24},{24,28},{28,20},{20,12},{12,4},{4,0},{1,9},{9... | collective-permute-start | bytes 589832 | tf_op jit(solution)/shard_map/ppermute | solution.py:321
  70.1 2.4 %collective-permute-done.21 = bf16[128,768]{1,0:T(8,128)(2,1)S(1)} collective-permute-done((bf16[128,768]{1,0:T(8,128)(2,1)S(1)}, bf16[128,768]{1,0:T(8,128)(2,1)S(1)}, u32[]{:S(2)}, u32[]{:S(2)}) %collective-permute-start.21) | collective-permute-done | bytes 196640 | tf_op jit(solution)/shard_map/ppermute | solution.py:324
  73.1 1.6 %collective-permute-start.18 = (bf16[128,768]{1,0:T(8,128)(2,1)S(1)}, bf16[128,768]{1,0:T(8,128)(2,1)S(1)}, u32[]{:S(2)}, u32[]{:S(2)}) collective-permute-start(bf16[128,768]{1,0:T(8,128)(2,1)S(1)} %add_convert_fusion.9), channel_id=1, source_target_pairs={{0,8},{8,16},{16,24},{24,28},{28,20},{20,12},{12,4},{4,0},{1,9},{9... | collective-permute-start | bytes 589832 | tf_op jit(solution)/shard_map/ppermute | solution.py:321
  75.6 1.6 %collective-permute-start.30 = (bf16[128,768]{1,0:T(8,128)(2,1)S(1)}, bf16[128,768]{1,0:T(8,128)(2,1)S(1)}, u32[]{:S(2)}, u32[]{:S(2)}) collective-permute-start(bf16[128,768]{1,0:T(8,128)(2,1)S(1)} %add_convert_fusion), channel_id=1, source_target_pairs={{0,8},{8,16},{16,24},{24,28},{28,20},{20,12},{12,4},{4,0},{1,9},{9... | collective-permute-start | bytes 589832 | tf_op jit(solution)/shard_map/ppermute | solution.py:321
  78.0 3.7 %collective-permute-done.22 = bf16[128,768]{1,0:T(8,128)(2,1)S(1)} collective-permute-done((bf16[128,768]{1,0:T(8,128)(2,1)S(1)}, bf16[128,768]{1,0:T(8,128)(2,1)S(1)}, u32[]{:S(2)}, u32[]{:S(2)}) %collective-permute-start.22) | collective-permute-done | bytes 196640 | tf_op jit(solution)/shard_map/ppermute | solution.py:324
  82.3 1.6 %collective-permute-start.19 = (bf16[128,768]{1,0:T(8,128)(2,1)S(1)}, bf16[128,768]{1,0:T(8,128)(2,1)S(1)}, u32[]{:S(2)}, u32[]{:S(2)}) collective-permute-start(bf16[128,768]{1,0:T(8,128)(2,1)S(1)} %add_convert_fusion.8), channel_id=1, source_target_pairs={{0,8},{8,16},{16,24},{24,28},{28,20},{20,12},{12,4},{4,0},{1,9},{9... | collective-permute-start | bytes 589832 | tf_op jit(solution)/shard_map/ppermute | solution.py:321
  83.9 2.0 %collective-permute-done.26 = bf16[128,768]{1,0:T(8,128)(2,1)S(1)} collective-permute-done((bf16[128,768]{1,0:T(8,128)(2,1)S(1)}, bf16[128,768]{1,0:T(8,128)(2,1)S(1)}, u32[]{:S(2)}, u32[]{:S(2)}) %collective-permute-start.26) | collective-permute-done | bytes 196640 | tf_op jit(solution)/shard_map/ppermute | solution.py:324
  86.5 1.6 %collective-permute-done.19 = bf16[128,768]{1,0:T(8,128)(2,1)S(1)} collective-permute-done((bf16[128,768]{1,0:T(8,128)(2,1)S(1)}, bf16[128,768]{1,0:T(8,128)(2,1)S(1)}, u32[]{:S(2)}, u32[]{:S(2)}) %collective-permute-start.19) | collective-permute-done | bytes 196640 | tf_op jit(solution)/shard_map/ppermute | solution.py:321
  88.1 1.6 %collective-permute-start.20 = (bf16[128,768]{1,0:T(8,128)(2,1)S(1)}, bf16[128,768]{1,0:T(8,128)(2,1)S(1)}, u32[]{:S(2)}, u32[]{:S(2)}) collective-permute-start(bf16[128,768]{1,0:T(8,128)(2,1)S(1)} %add_convert_fusion.7), channel_id=1, source_target_pairs={{0,8},{8,16},{16,24},{24,28},{28,20},{20,12},{12,4},{4,0},{1,9},{9... | collective-permute-start | bytes 589832 | tf_op jit(solution)/shard_map/ppermute | solution.py:321
  90.1 2.7 %collective-permute-done.27.refs_4_ = bf16[128,768]{1,0:T(8,128)(2,1)S(1)} collective-permute-done((bf16[128,768]{1,0:T(8,128)(2,1)S(1)}, bf16[128,768]{1,0:T(8,128)(2,1)S(1)}, u32[]{:S(2)}, u32[]{:S(2)}) %collective-permute-start.27) | collective-permute-done | bytes 196640 | tf_op jit(solution)/shard_map/ppermute | solution.py:324
  92.9 0.9 collective-permute-done.20.refs_1_
  (81 shorter events, 9.6 us)
Async XLA Ops:
  2.9 43.2 %copy-start.4 = (s32[8]{0:T(128)S(1)}, s32[8]{0:T(128)}, u32[]{:S(2)}) copy-start(s32[8]{0:T(128)} %place_ref.1) | copy-start | bytes 100
  2.9 13.0 %collective-permute-start = (bf16[128,1664]{1,0:T(8,128)(2,1)}, bf16[128,1664]{1,0:T(8,128)(2,1)S(1)}, u32[]{:S(2)}, u32[]{:S(2)}) collective-permute-start(bf16[128,1664]{1,0:T(8,128)(2,1)} %get-tuple-element.32.refs_0_), channel_id=1, source_target_pairs={{0,8},{8,16},{16,24},{24,28},{28,20},{20,12},{12,4},{4,0},{1,9},{9... | collective-permute-start | bytes 1277960 | tf_op jit(solution)/shard_map/ppermute | solution.py:321
  6.0 11.8 %collective-permute-start.1 = (bf16[128,1664]{1,0:T(8,128)(2,1)}, bf16[128,1664]{1,0:T(8,128)(2,1)S(1)}, u32[]{:S(2)}, u32[]{:S(2)}) collective-permute-start(bf16[128,1664]{1,0:T(8,128)(2,1)} %get-tuple-element.32.refs_0_), channel_id=1, source_target_pairs={{8,0},{16,8},{24,16},{28,24},{20,28},{12,20},{4,12},{0,4},{9,1},{1... | collective-permute-start | bytes 1277960 | tf_op jit(solution)/shard_map/ppermute | solution.py:324
  6.0 33.2 %collective-permute-start.9 = (bf16[768,768]{1,0:T(8,128)(2,1)}, bf16[768,768]{1,0:T(8,128)(2,1)S(1)}, u32[]{:S(2)}, u32[]{:S(2)}) collective-permute-start(bf16[768,768]{1,0:T(8,128)(2,1)} %get-tuple-element.33.refs_9_), channel_id=1, source_target_pairs={{0,2},{1,3},{2,0},{3,1},{4,6},{5,7},{6,4},{7,5},{8,10},{9,11},{10,... | collective-permute-start | bytes 3538952 | tf_op jit(solution)/shard_map/ppermute | solution.py:264
  8.0 31.4 %collective-permute-start.8 = (bf16[768,768]{1,0:T(8,128)(2,1)}, bf16[768,768]{1,0:T(8,128)(2,1)S(1)}, u32[]{:S(2)}, u32[]{:S(2)}) collective-permute-start(bf16[768,768]{1,0:T(8,128)(2,1)} %get-tuple-element.33.refs_9_), channel_id=1, source_target_pairs={{0,1},{1,0},{2,3},{3,2},{4,5},{5,4},{6,7},{7,6},{8,9},{9,8},{10,11... | collective-permute-start | bytes 3538952 | tf_op jit(solution)/shard_map/ppermute | solution.py:264
  15.9 11.0 %collective-permute-start.2 = (bf16[128,1664]{1,0:T(8,128)(2,1)S(1)}, bf16[128,1664]{1,0:T(8,128)(2,1)S(1)}, u32[]{:S(2)}, u32[]{:S(2)}) collective-permute-start(bf16[128,1664]{1,0:T(8,128)(2,1)S(1)} %collective-permute-done.refs_1_), channel_id=1, source_target_pairs={{0,8},{8,16},{16,24},{24,28},{28,20},{20,12},{12,4},{4,0},{1,9},{9... | collective-permute-start | bytes 1277960 | tf_op jit(solution)/shard_map/ppermute | solution.py:321
  17.8 10.7 %collective-permute-start.3 = (bf16[128,1664]{1,0:T(8,128)(2,1)S(1)}, bf16[128,1664]{1,0:T(8,128)(2,1)S(1)}, u32[]{:S(2)}, u32[]{:S(2)}) collective-permute-start(bf16[128,1664]{1,0:T(8,128)(2,1)S(1)} %collective-permute-done.1.refs_2_), channel_id=1, source_target_pairs={{8,0},{16,8},{24,16},{28,24},{20,28},{12,20},{4,12},{0,4},{9,1},{1... | collective-permute-start | bytes 1277960 | tf_op jit(solution)/shard_map/ppermute | solution.py:324
  26.9 10.1 %collective-permute-start.4 = (bf16[128,1664]{1,0:T(8,128)(2,1)S(1)}, bf16[128,1664]{1,0:T(8,128)(2,1)S(1)}, u32[]{:S(2)}, u32[]{:S(2)}) collective-permute-start(bf16[128,1664]{1,0:T(8,128)(2,1)S(1)} %collective-permute-done.2.refs_3_), channel_id=1, source_target_pairs={{0,8},{8,16},{16,24},{24,28},{28,20},{20,12},{12,4},{4,0},{1,9},{9... | collective-permute-start | bytes 1277960 | tf_op jit(solution)/shard_map/ppermute | solution.py:321
  28.5 10.0 %collective-permute-start.5 = (bf16[128,1664]{1,0:T(8,128)(2,1)S(1)}, bf16[128,1664]{1,0:T(8,128)(2,1)S(1)}, u32[]{:S(2)}, u32[]{:S(2)}) collective-permute-start(bf16[128,1664]{1,0:T(8,128)(2,1)S(1)} %collective-permute-done.3.refs_4_), channel_id=1, source_target_pairs={{8,0},{16,8},{24,16},{28,24},{20,28},{12,20},{4,12},{0,4},{9,1},{1... | collective-permute-start | bytes 1277960 | tf_op jit(solution)/shard_map/ppermute | solution.py:324
  29.0 26.8 %collective-permute-start.15 = (bf16[192,1536]{1,0:T(8,128)(2,1)S(1)}, bf16[192,1536]{1,0:T(8,128)(2,1)S(1)}, u32[]{:S(2)}, u32[]{:S(2)}) collective-permute-start(bf16[192,1536]{1,0:T(8,128)(2,1)S(1)} %bitcast.7), channel_id=1, source_target_pairs={{0,2},{1,3},{2,0},{3,1},{4,6},{5,7},{6,4},{7,5},{8,10},{9,11},{10,... | collective-permute-start | bytes 1769480 | tf_op jit(solution)/shard_map/ppermute | solution.py:264
  37.0 5.9 %collective-permute-start.6 = (bf16[64,1664]{1,0:T(8,128)(2,1)S(1)}, bf16[64,1664]{1,0:T(8,128)(2,1)S(1)}, u32[]{:S(2)}, u32[]{:S(2)}) collective-permute-start(bf16[64,1664]{1,0:T(8,128)(2,1)S(1)} %slice.20), channel_id=1, source_target_pairs={{0,8},{8,16},{16,24},{24,28},{28,20},{20,12},{12,4},{4,0},{1,9},{9... | collective-permute-start | bytes 638984 | tf_op jit(solution)/shard_map/ppermute | solution.py:321
  38.5 5.9 %collective-permute-start.7 = (bf16[64,1664]{1,0:T(8,128)(2,1)S(1)}, bf16[64,1664]{1,0:T(8,128)(2,1)S(1)}, u32[]{:S(2)}, u32[]{:S(2)}) collective-permute-start(bf16[64,1664]{1,0:T(8,128)(2,1)S(1)} %slice.21), channel_id=1, source_target_pairs={{8,0},{16,8},{24,16},{28,24},{20,28},{12,20},{4,12},{0,4},{9,1},{1... | collective-permute-start | bytes 638984 | tf_op jit(solution)/shard_map/ppermute | solution.py:324
  39.3 5.1 %collective-permute-start.10 = (bf16[192,768]{1,0:T(8,128)(2,1)S(1)}, bf16[192,768]{1,0:T(8,128)(2,1)S(1)}, u32[]{:S(2)}, u32[]{:S(2)}) collective-permute-start(bf16[192,768]{1,0:T(8,128)(2,1)S(1)} %get-tuple-element.34.refs_11_), channel_id=1, source_target_pairs={{0,1},{1,0},{2,3},{3,2},{4,5},{5,4},{6,7},{7,6},{8,9},{9,8},{10,11... | collective-permute-start | bytes 884744 | tf_op jit(solution)/shard_map/ppermute | solution.py:264
  39.4 5.6 %collective-permute-start.11 = (bf16[192,768]{1,0:T(8,128)(2,1)S(1)}, bf16[192,768]{1,0:T(8,128)(2,1)}, u32[]{:S(2)}, u32[]{:S(2)}) collective-permute-start(bf16[192,768]{1,0:T(8,128)(2,1)S(1)} %get-tuple-element.35.refs_12_), channel_id=1, source_target_pairs={{0,1},{1,0},{2,3},{3,2},{4,5},{5,4},{6,7},{7,6},{8,9},{9,8},{10,11... | collective-permute-start | bytes 884744 | tf_op jit(solution)/shard_map/ppermute | solution.py:264
  42.9 2.0 %collective-permute-start.12 = (bf16[192,768]{1,0:T(8,128)(2,1)S(1)}, bf16[192,768]{1,0:T(8,128)(2,1)}, u32[]{:S(2)}, u32[]{:S(2)}) collective-permute-start(bf16[192,768]{1,0:T(8,128)(2,1)S(1)} %get-tuple-element.36.refs_13_), channel_id=1, source_target_pairs={{0,1},{1,0},{2,3},{3,2},{4,5},{5,4},{6,7},{7,6},{8,9},{9,8},{10,11... | collective-permute-start | bytes 884744 | tf_op jit(solution)/shard_map/ppermute | solution.py:264
  44.4 1.7 %collective-permute-start.13 = (bf16[192,768]{1,0:T(8,128)(2,1)S(1)}, bf16[192,768]{1,0:T(8,128)(2,1)}, u32[]{:S(2)}, u32[]{:S(2)}) collective-permute-start(bf16[192,768]{1,0:T(8,128)(2,1)S(1)} %get-tuple-element.37.refs_14_), channel_id=1, source_target_pairs={{0,1},{1,0},{2,3},{3,2},{4,5},{5,4},{6,7},{7,6},{8,9},{9,8},{10,11... | collective-permute-start | bytes 884744 | tf_op jit(solution)/shard_map/ppermute | solution.py:264
  44.5 11.7 %collective-permute-start.14 = (bf16[192,1536]{1,0:T(8,128)(2,1)S(1)}, bf16[192,1536]{1,0:T(8,128)(2,1)S(1)}, u32[]{:S(2)}, u32[]{:S(2)}) collective-permute-start(bf16[192,1536]{1,0:T(8,128)(2,1)S(1)} %bitcast.8), channel_id=1, source_target_pairs={{0,1},{1,0},{2,3},{3,2},{4,5},{5,4},{6,7},{7,6},{8,9},{9,8},{10,11... | collective-permute-start | bytes 1769480 | tf_op jit(solution)/shard_map/ppermute | solution.py:264
  55.9 2.1 %collective-permute-start.16 = (bf16[192,1536]{1,0:T(8,128)(2,1)S(1)}, bf16[192,1536]{1,0:T(8,128)(2,1)S(1)}, u32[]{:S(2)}, u32[]{:S(2)}) collective-permute-start(bf16[192,1536]{1,0:T(8,128)(2,1)S(1)} %after.3.refs_5_.refs_4_), channel_id=1, source_target_pairs={{0,1},{1,0},{2,3},{3,2},{4,5},{5,4},{6,7},{7,6},{8,9},{9,8},{10,11... | collective-permute-start | bytes 1769480 | tf_op jit(solution)/shard_map/ppermute | solution.py:264
  59.3 8.6 %collective-permute-start.28 = (bf16[128,768]{1,0:T(8,128)(2,1)S(1)}, bf16[128,768]{1,0:T(8,128)(2,1)S(1)}, u32[]{:S(2)}, u32[]{:S(2)}) collective-permute-start(bf16[128,768]{1,0:T(8,128)(2,1)S(1)} %get-tuple-element.56), channel_id=1, source_target_pairs={{0,8},{8,16},{16,24},{24,28},{28,20},{20,12},{12,4},{4,0},{1,9},{9... | collective-permute-start | bytes 589832 | tf_op jit(solution)/shard_map/ppermute | solution.py:321
  60.9 8.7 %collective-permute-start.24 = (bf16[128,768]{1,0:T(8,128)(2,1)S(1)}, bf16[128,768]{1,0:T(8,128)(2,1)S(1)}, u32[]{:S(2)}, u32[]{:S(2)}) collective-permute-start(bf16[128,768]{1,0:T(8,128)(2,1)S(1)} %get-tuple-element.52), channel_id=1, source_target_pairs={{8,0},{16,8},{24,16},{28,24},{20,28},{12,20},{4,12},{0,4},{9,1},{1... | collective-permute-start | bytes 589832 | tf_op jit(solution)/shard_map/ppermute | solution.py:324
  62.6 9.9 %collective-permute-start.21 = (bf16[128,768]{1,0:T(8,128)(2,1)S(1)}, bf16[128,768]{1,0:T(8,128)(2,1)S(1)}, u32[]{:S(2)}, u32[]{:S(2)}) collective-permute-start(bf16[128,768]{1,0:T(8,128)(2,1)S(1)} %get-tuple-element.48), channel_id=1, source_target_pairs={{8,0},{16,8},{24,16},{28,24},{20,28},{12,20},{4,12},{0,4},{9,1},{1... | collective-permute-start | bytes 589832 | tf_op jit(solution)/shard_map/ppermute | solution.py:324
  63.4 9.7 %collective-permute-start.17 = (bf16[128,768]{1,0:T(8,128)(2,1)S(1)}, bf16[128,768]{1,0:T(8,128)(2,1)S(1)}, u32[]{:S(2)}, u32[]{:S(2)}) collective-permute-start(bf16[128,768]{1,0:T(8,128)(2,1)S(1)} %get-tuple-element.44), channel_id=1, source_target_pairs={{0,8},{8,16},{16,24},{24,28},{28,20},{20,12},{12,4},{4,0},{1,9},{9... | collective-permute-start | bytes 589832 | tf_op jit(solution)/shard_map/ppermute | solution.py:321
  67.9 7.7 %collective-permute-start.29 = (bf16[128,768]{1,0:T(8,128)(2,1)S(1)}, bf16[128,768]{1,0:T(8,128)(2,1)S(1)}, u32[]{:S(2)}, u32[]{:S(2)}) collective-permute-start(bf16[128,768]{1,0:T(8,128)(2,1)S(1)} %add_convert_fusion.1), channel_id=1, source_target_pairs={{0,8},{8,16},{16,24},{24,28},{28,20},{20,12},{12,4},{4,0},{1,9},{9... | collective-permute-start | bytes 589832 | tf_op jit(solution)/shard_map/ppermute | solution.py:321
  69.6 7.9 %collective-permute-start.25 = (bf16[128,768]{1,0:T(8,128)(2,1)S(1)}, bf16[128,768]{1,0:T(8,128)(2,1)S(1)}, u32[]{:S(2)}, u32[]{:S(2)}) collective-permute-start(bf16[128,768]{1,0:T(8,128)(2,1)S(1)} %add_convert_fusion.4), channel_id=1, source_target_pairs={{8,0},{16,8},{24,16},{28,24},{20,28},{12,20},{4,12},{0,4},{9,1},{1... | collective-permute-start | bytes 589832 | tf_op jit(solution)/shard_map/ppermute | solution.py:324
  72.6 9.2 %collective-permute-start.22 = (bf16[128,768]{1,0:T(8,128)(2,1)S(1)}, bf16[128,768]{1,0:T(8,128)(2,1)S(1)}, u32[]{:S(2)}, u32[]{:S(2)}) collective-permute-start(bf16[128,768]{1,0:T(8,128)(2,1)S(1)} %add_convert_fusion.6), channel_id=1, source_target_pairs={{8,0},{16,8},{24,16},{28,24},{20,28},{12,20},{4,12},{0,4},{9,1},{1... | collective-permute-start | bytes 589832 | tf_op jit(solution)/shard_map/ppermute | solution.py:324
  73.1 9.2 %collective-permute-start.18 = (bf16[128,768]{1,0:T(8,128)(2,1)S(1)}, bf16[128,768]{1,0:T(8,128)(2,1)S(1)}, u32[]{:S(2)}, u32[]{:S(2)}) collective-permute-start(bf16[128,768]{1,0:T(8,128)(2,1)S(1)} %add_convert_fusion.9), channel_id=1, source_target_pairs={{0,8},{8,16},{16,24},{24,28},{28,20},{20,12},{12,4},{4,0},{1,9},{9... | collective-permute-start | bytes 589832 | tf_op jit(solution)/shard_map/ppermute | solution.py:321
  75.6 14.1 %collective-permute-start.30 = (bf16[128,768]{1,0:T(8,128)(2,1)S(1)}, bf16[128,768]{1,0:T(8,128)(2,1)S(1)}, u32[]{:S(2)}, u32[]{:S(2)}) collective-permute-start(bf16[128,768]{1,0:T(8,128)(2,1)S(1)} %add_convert_fusion), channel_id=1, source_target_pairs={{0,8},{8,16},{16,24},{24,28},{28,20},{20,12},{12,4},{4,0},{1,9},{9... | collective-permute-start | bytes 589832 | tf_op jit(solution)/shard_map/ppermute | solution.py:321
  77.5 8.4 %collective-permute-start.26 = (bf16[128,768]{1,0:T(8,128)(2,1)S(1)}, bf16[128,768]{1,0:T(8,128)(2,1)S(1)}, u32[]{:S(2)}, u32[]{:S(2)}) collective-permute-start(bf16[128,768]{1,0:T(8,128)(2,1)S(1)} %add_convert_fusion.3), channel_id=1, source_target_pairs={{8,0},{16,8},{24,16},{28,24},{20,28},{12,20},{4,12},{0,4},{9,1},{1... | collective-permute-start | bytes 589832 | tf_op jit(solution)/shard_map/ppermute | solution.py:324
  81.8 8.4 %collective-permute-start.23 = (bf16[128,768]{1,0:T(8,128)(2,1)S(1)}, bf16[128,768]{1,0:T(8,128)(2,1)S(1)}, u32[]{:S(2)}, u32[]{:S(2)}) collective-permute-start(bf16[128,768]{1,0:T(8,128)(2,1)S(1)} %add_convert_fusion.5), channel_id=1, source_target_pairs={{8,0},{16,8},{24,16},{28,24},{20,28},{12,20},{4,12},{0,4},{9,1},{1... | collective-permute-start | bytes 589832 | tf_op jit(solution)/shard_map/ppermute | solution.py:324
  82.3 5.7 %collective-permute-start.19 = (bf16[128,768]{1,0:T(8,128)(2,1)S(1)}, bf16[128,768]{1,0:T(8,128)(2,1)S(1)}, u32[]{:S(2)}, u32[]{:S(2)}) collective-permute-start(bf16[128,768]{1,0:T(8,128)(2,1)S(1)} %add_convert_fusion.8), channel_id=1, source_target_pairs={{0,8},{8,16},{16,24},{24,28},{28,20},{20,12},{12,4},{4,0},{1,9},{9... | collective-permute-start | bytes 589832 | tf_op jit(solution)/shard_map/ppermute | solution.py:321
  86.0 6.9 %collective-permute-start.27 = (bf16[128,768]{1,0:T(8,128)(2,1)S(1)}, bf16[128,768]{1,0:T(8,128)(2,1)S(1)}, u32[]{:S(2)}, u32[]{:S(2)}) collective-permute-start(bf16[128,768]{1,0:T(8,128)(2,1)S(1)} %add_convert_fusion.2), channel_id=1, source_target_pairs={{8,0},{16,8},{24,16},{28,24},{20,28},{12,20},{4,12},{0,4},{9,1},{1... | collective-permute-start | bytes 589832 | tf_op jit(solution)/shard_map/ppermute | solution.py:324
  88.1 5.7 %collective-permute-start.20 = (bf16[128,768]{1,0:T(8,128)(2,1)S(1)}, bf16[128,768]{1,0:T(8,128)(2,1)S(1)}, u32[]{:S(2)}, u32[]{:S(2)}) collective-permute-start(bf16[128,768]{1,0:T(8,128)(2,1)S(1)} %add_convert_fusion.7), channel_id=1, source_target_pairs={{0,8},{8,16},{16,24},{24,28},{28,20},{20,12},{12,4},{4,0},{1,9},{9... | collective-permute-start | bytes 589832 | tf_op jit(solution)/shard_map/ppermute | solution.py:321
  (12 other events, 106.6 us)
